TPU v7x, 256 devices: a whole 4x4x8 slice. The times are simulated.
256 devices in a mesh: blk: 64 (over y, z, core), line: 4 (over x).
Axes of the slice: x: 4, y: 4, z: 8, core: 2. Of those that a mesh axis runs over, the one named last changes fastest.
Arguments:
- field: float32 [3, 384, 512, 128], P(None, 'line', 'blk'), may hold values from -6 to 6
- stretch: float32 [384, 512, 128], P('line', 'blk'), may hold values from 0.3 to 3
- lengths: int32 [512], P('blk'), may hold values from 3 to 128, as said below
- connect: int32 [512], P('blk'), may hold values from 0 to 511, as said below
- orient: int32 [512], P('blk'), may hold values from 0 to 3
Outputs:
- rates: float32 [3, 384, 512, 128], P(None, 'line', 'blk')
- advanced: float32 [3, 384, 512, 128], P(None, 'line', 'blk')
Inputs may be any that keep to these rules, and one draw needn't show every extreme that they name: `lengths`: at least 3; some slot has exactly 128. `connect`: A permutation of the slots. Slots of device d are d * 8 to d * 8 + 7. With M = 4, offset 1 = 63 and offset k = 32 + k - 2 for k from 2 to M: for each k, exactly 2 slots of every device d take their neighbours from slots of device (d + offset k) mod 64, at the same slot positions on every device.
All inputs are finite; a program needn't handle non-finite values.
Results may differ from a plain program's by a relative error of at most 0.0003.
Values sent between devices are 32-bit elements; how exact they have to be, the bound alone decides.
No kernel may reach another device: no remote copies, remote signals or barrier semaphores. Data moves between devices by JAX's collectives and lax.ppermute only.
A program may use at most 64 MiB of HBM per device.

v0:
```python
import jax
import jax.numpy as jnp
from jax import lax
from jax.sharding import PartitionSpec as P

LINE_POINTS = 384
HALO_LINES = 3


stencil = (2.0, -27.0, 270.0, -490.0, 270.0, -27.0, 2.0)


def implicit_matrix(count):
    rows = jnp.arange(count)[:, None]
    cols = jnp.arange(count)[None, :]
    gap = jnp.abs(rows - cols)
    amat = jnp.where(gap == 0, 1.0, 0.0) + jnp.where(gap == 1, 2.0 / 11.0, 0.0)
    bmat = (
        jnp.where(gap == 0, -24.0 / 11.0 - 3.0 / 22.0, 0.0)
        + jnp.where(gap == 1, 12.0 / 11.0, 0.0)
        + jnp.where(gap == 2, 3.0 / 44.0, 0.0)
    )
    amat = amat.astype(jnp.float32)
    system = amat - 800.0 * bmat
    factor = jnp.linalg.cholesky(system)
    return jax.scipy.linalg.cho_solve((factor, True), amat)


def rotate(unmasked_values, orient):
    cosine = (jnp.where(orient == 0, 1.0, 0.0) - jnp.where(orient == 2, 1.0, 0.0)).astype(
        jnp.float32
    )
    sine = (jnp.where(orient == 1, 1.0, 0.0) - jnp.where(orient == 3, 1.0, 0.0)).astype(jnp.float32)
    cosine = cosine[None, :, None]
    sine = sine[None, :, None]
    first = cosine * unmasked_values[0] - sine * unmasked_values[1]
    second = sine * unmasked_values[0] + cosine * unmasked_values[1]
    return jnp.stack([first, second, unmasked_values[2]])


def shards(field, stretch, lengths, connect, orient):
    slot_count = lengths.shape[0]
    point_count = field.shape[1]
    nline = field.shape[3]
    slot_index = jnp.arange(slot_count)
    live = (jnp.arange(nline)[None, :] < lengths[:, None]).astype(jnp.float32)
    masked_values = field * live
    position_index = lengths[:, None] - HALO_LINES + jnp.arange(HALO_LINES)[None, :]
    boundary_faces = masked_values[:, :, slot_index[:, None], position_index]
    boundary_rows = jnp.transpose(boundary_faces, (2, 0, 3, 1)).reshape(slot_count, -1)
    everything = lax.all_gather(boundary_rows, "blk", axis=0, tiled=True)
    selected_rows = everything[connect]
    unmasked_values = jnp.transpose(
        selected_rows.reshape(slot_count, 3, HALO_LINES, point_count), (1, 3, 0, 2)
    )
    ghosts = rotate(unmasked_values, orient)
    trailing_rows = jnp.zeros((3, point_count, slot_count, HALO_LINES), jnp.float32)
    ext = jnp.concatenate([ghosts, masked_values, trailing_rows], axis=3)
    second = jnp.zeros_like(masked_values)
    for shift_at in range(7):
        second = second + stencil[shift_at] * ext[:, :, :, shift_at : shift_at + nline]
    second = second / 180.0
    rates = stretch * second * live
    pre = masked_values + 0.1 * rates
    kmat = implicit_matrix(LINE_POINTS)
    result = jnp.einsum(
        "pq,cqsl->cpsl",
        kmat,
        lax.all_to_all(pre, "line", split_axis=2, concat_axis=1, tiled=True),
        precision=lax.Precision.HIGHEST,
    )
    advanced = lax.all_to_all(result, "line", split_axis=1, concat_axis=2, tiled=True)
    return (rates, advanced)


def solution(mesh):
    return jax.shard_map(
        shards,
        mesh=mesh,
        in_specs=(
            P(None, "line", "blk", None),
            P("line", "blk", None),
            P("blk"),
            P("blk"),
            P("blk"),
        ),
        out_specs=(P(None, "line", "blk", None), P(None, "line", "blk", None)),
        check_vma=False,
    )
```

profile of v0, /device:TPU:160, one launch (start us, length us, event | category | flops | bytes accessed | tf_op | source)
XLA Modules:
  0.0 186.0 jit_solution(11713152226467265228)
XLA Ops:
  8.6 3.2 %copy.56 = f32[3,96,8,128]{1,0,3,2:T(4,128)} copy(f32[3,96,8,128]{3,2,1,0:T(8,128)} %param.5) | data formatting | bytes 2359296 | tf_op args[0]
  12.0 2.5 %broadcast_multiply_fusion = f32[3,96,8,128]{1,0,3,2:T(4,128)S(1)} fusion(f32[3,96,8,128]{1,0,3,2:T(4,128)} %copy.56, f32[8,128]{1,0:T(8,128)S(1)} %fusion.49), kind=kLoop, calls=%fused_computation.30 | loop fusion | flops 294912 | bytes 2363392 | tf_op jit(solution)/shard_map/mul | solution.py:47
  17.3 11.7 %cholesky.76 = f32[128,128]{1,0:T(8,128)S(1)} custom-call(f32[128,128]{1,0:T(8,128)S(1)} %cholesky.189), custom_call_target="Cholesky" | custom-call | tf_op jit(solution)/shard_map/jit(cholesky)/cholesky | solution.py:25
  29.1 9.8 %custom-call.26 = f32[1,128,128]{1,2,0:T(8,128)S(1)} custom-call(f32[1,128,128]{2,1,0:T(8,128)S(1)} %get-tuple-element.38), custom_call_target="InvertDiagBlocksLowerTriangular" | custom-call | tf_op jit(solution)/shard_map/jit(cholesky)/cholesky | solution.py:25
  40.2 11.7 %cholesky.160 = f32[128,128]{1,0:T(8,128)S(1)} custom-call(f32[128,128]{1,0:T(8,128)S(1)} %cholesky.193), custom_call_target="Cholesky" | custom-call | tf_op jit(solution)/shard_map/jit(cholesky)/cholesky | solution.py:25
  51.9 10.0 %custom-call.27 = f32[1,128,128]{1,2,0:T(8,128)S(1)} custom-call(f32[1,128,128]{2,1,0:T(8,128)S(1)} %get-tuple-element.35), custom_call_target="InvertDiagBlocksLowerTriangular" | custom-call | tf_op jit(solution)/shard_map/jit(cholesky)/cholesky | solution.py:25
  61.9 1.0 convolution_dynamic-update-slice_fusion
  63.2 11.7 %cholesky.179 = f32[128,128]{1,0:T(8,128)S(1)} custom-call(f32[128,128]{1,0:T(8,128)S(1)} %convolution_subtract_fusion.5), custom_call_target="Cholesky" | custom-call | tf_op jit(solution)/shard_map/jit(cholesky)/cholesky | solution.py:25
  78.1 7.4 %while.1 = (s32[]{:T(128)}, f32[384,384]{1,0:T(8,128)S(1)}, s32[3,2]{0,1:T(2,128)S(1)}, f32[3,128,128]{2,1,0:T(8,128)}, s32[]{:T(128)}) while((s32[]{:T(128)}, f32[384,384]{1,0:T(8,128)S(1)}, s32[3,2]{0,1:T(2,128)S(1)}, f32[3,128,128]{2,1,0:T(8,128)}, s32[]{:T(128)}) %tuple.38), condition=%wide.while_cond, body=%wide.while_body.sunk | while | flops 2 | bytes 132205 | solution.py:26
  78.8 1.9 %bitcast_dynamic-update-slice_fusion.2 = f32[3,128,128]{2,1,0:T(8,128)} fusion(f32[3,128,128]{2,1,0:T(8,128)} %get-tuple-element.85, s32[]{:T(128)S(6)} %copy.85, f32[384,384]{1,0:T(8,128)S(1)} %get-tuple-element.88, s32[]{:T(128)} %bitcast.65, s32[]{:T(128)} %bitcast.66), kind=kLoop, calls=%fused_computation.2.clone.1 | loop fusion | bytes 132100 | tf_op jit(solution)/shard_map/jit(_cho_solve)/triangular_solve
  81.2 1.9 %bitcast_dynamic-update-slice_fusion.2 = f32[3,128,128]{2,1,0:T(8,128)} fusion(f32[3,128,128]{2,1,0:T(8,128)} %get-tuple-element.85, s32[]{:T(128)S(6)} %copy.85, f32[384,384]{1,0:T(8,128)S(1)} %get-tuple-element.88, s32[]{:T(128)} %bitcast.65, s32[]{:T(128)} %bitcast.66), kind=kLoop, calls=%fused_computation.2.clone.1 | loop fusion | bytes 132100 | tf_op jit(solution)/shard_map/jit(_cho_solve)/triangular_solve
  83.7 1.9 %bitcast_dynamic-update-slice_fusion.2 = f32[3,128,128]{2,1,0:T(8,128)} fusion(f32[3,128,128]{2,1,0:T(8,128)} %get-tuple-element.85, s32[]{:T(128)S(6)} %copy.85, f32[384,384]{1,0:T(8,128)S(1)} %get-tuple-element.88, s32[]{:T(128)} %bitcast.65, s32[]{:T(128)} %bitcast.66), kind=kLoop, calls=%fused_computation.2.clone.1 | loop fusion | bytes 132100 | tf_op jit(solution)/shard_map/jit(_cho_solve)/triangular_solve
  85.6 30.3 %custom-call.28 = f32[3,128,128]{1,2,0:T(8,128)S(1)} custom-call(f32[3,128,128]{2,1,0:T(8,128)} %get-tuple-element.9), custom_call_target="InvertDiagBlocksLowerTriangular" | custom-call | tf_op jit(solution)/shard_map/jit(_cho_solve)/triangular_solve | solution.py:26
  118.7 2.1 %gather_fusion.1 = f32[8,864]{1,0:T(8,128)S(1)} fusion(f32[512,864]{1,0:T(8,128)} %all-gather.2.cloned.1.call-done, s32[1024]{0:T(1024)S(1)} %pad_clamp_fusion), kind=kCustom, calls=%fused_computation.1 | custom fusion | bytes 55328 | tf_op jit(solution)/shard_map/gather | solution.py:52
  121.7 7.2 %multiply_add_fusion = (f32[3,96,8,128]{1,0,3,2:T(4,128)}, f32[3,96,8,128]{1,0,3,2:T(4,128)}) fusion(f32[3,96,8,128]{1,0,3,2:T(4,128)S(1)} %broadcast_multiply_fusion, f32[8,128]{1,0:T(8,128)S(1)} %fusion.49, f32[96,8,128]{0,2,1:T(8,128)} %copy.61, f32[3,96,8,3]{1,0,3,2:T(4,128)S(1)} %copy.60), kind=kLoop, calls=%fused_computation.18 | loop fusion | flops 5898240 | bytes 3963904 | tf_op jit(solution)/shard_map/add | solution.py:64
  128.9 2.6 %copy.62 = f32[3,96,8,128]{3,1,0,2:T(8,128)} copy(f32[3,96,8,128]{1,0,3,2:T(4,128)} %get-tuple-element.28) | data formatting | bytes 2359296 | tf_op jit(solution)/shard_map/add | solution.py:64
  131.5 4.3 %all-to-all-start = ((f32[3,96,8,128]{3,1,0,2:T(8,128)}), f32[3,96,8,128]{3,1,0,2:T(8,128)S(1)}, u32[]{:S(2)}, u32[]{:S(2)}) async-start(f32[3,96,8,128]{3,1,0,2:T(8,128)} %copy.62), calls=%async_computation | async-start | bytes 2359296 | tf_op jit(solution)/shard_map/all_to_all | solution.py:69
  137.3 15.1 %all-to-all-done = f32[3,96,8,128]{3,1,0,2:T(8,128)S(1)} async-done(((f32[3,96,8,128]{3,1,0,2:T(8,128)}), f32[3,96,8,128]{3,1,0,2:T(8,128)S(1)}, u32[]{:S(2)}, u32[]{:S(2)}) %all-to-all-start) | async-done | bytes 1179680 | tf_op jit(solution)/shard_map/all_to_all | solution.py:69
  152.4 3.9 %convolution_bitcast_fusion = f32[3,384,2,128]{1,3,2,0:T(8,128)S(1)} fusion(f32[3,384,2,128]{3,1,2,0:T(8,128)S(1)} %bitcast.71, f32[128,384]{1,0:T(8,128)S(1)} %fusion.44, f32[128,384]{1,0:T(8,128)S(1)} %fusion.42, f32[128,384]{1,0:T(8,128)S(1)} %fusion.41), kind=kOutput, calls=%fused_computation.22 | convolution fusion | flops 1359249408 | bytes 2949120 | tf_op jit(solution)/shard_map/pq,cqsl->cpsl/dot_general | solution.py:66
  156.3 1.9 %copy.66 = f32[3,384,2,128]{3,2,0,1:T(2,128)} copy(f32[3,384,2,128]{1,3,2,0:T(8,128)S(1)} %convolution_bitcast_fusion) | data formatting | bytes 2359296 | tf_op jit(solution)/shard_map/pq,cqsl->cpsl/transpose | solution.py:66
  158.2 3.5 %all-to-all-start.1 = ((f32[3,384,2,128]{3,2,0,1:T(2,128)}), f32[3,384,2,128]{3,2,0,1:T(2,128)S(1)}, u32[]{:S(2)}, u32[]{:S(2)}) async-start(f32[3,384,2,128]{3,2,0,1:T(2,128)} %copy.66), calls=%async_computation.1 | async-start | bytes 2359296 | tf_op jit(solution)/shard_map/all_to_all | solution.py:72
  161.7 1.5 copy.69
  163.3 14.0 %all-to-all-done.1 = f32[3,384,2,128]{3,2,0,1:T(2,128)S(1)} async-done(((f32[3,384,2,128]{3,2,0,1:T(2,128)}), f32[3,384,2,128]{3,2,0,1:T(2,128)S(1)}, u32[]{:S(2)}, u32[]{:S(2)}) %all-to-all-start.1) | async-done | bytes 1179680 | tf_op jit(solution)/shard_map/all_to_all | solution.py:72
  177.5 1.7 copy.70
  (66 shorter events, 14.5 us)
Async XLA Ops:
  7.2 111.6 %all-gather.2.cloned.1.call-start = ((), (), s32[]{:S(2)}) async-start(), calls=%async_computation.2 | async-start | bytes 1863680 | tf_op jit(solution)/shard_map/all_gather | solution.py:51
  14.4 1.8 copy-start.2
  29.1 86.8 %copy-start.3 = (s32[8]{0:T(128)S(1)}, s32[8]{0:T(128)}, u32[]{:S(2)}) copy-start(s32[8]{0:T(128)} %param.8) | copy-start | bytes 100
  39.2 76.8 %copy-start.4 = (s32[8]{0:T(128)S(1)}, s32[8]{0:T(128)}, u32[]{:S(2)}) copy-start(s32[8]{0:T(128)} %param.9) | copy-start | bytes 100
  39.5 0.7 copy-start.1
  131.5 20.8 %all-to-all-start = ((f32[3,96,8,128]{3,1,0,2:T(8,128)}), f32[3,96,8,128]{3,1,0,2:T(8,128)S(1)}, u32[]{:S(2)}, u32[]{:S(2)}) async-start(f32[3,96,8,128]{3,1,0,2:T(8,128)} %copy.62), calls=%async_computation | async-start | bytes 2359296 | tf_op jit(solution)/shard_map/all_to_all | solution.py:69
  156.3 5.5 %copy-start = (f32[3,96,8,128]{1,0,3,2:T(4,128)S(1)}, f32[3,96,8,128]{1,0,3,2:T(4,128)}, u32[]{:S(2)}) copy-start(f32[3,96,8,128]{1,0,3,2:T(4,128)} %get-tuple-element.29) | copy-start | bytes 3538948
  158.2 19.1 %all-to-all-start.1 = ((f32[3,384,2,128]{3,2,0,1:T(2,128)}), f32[3,384,2,128]{3,2,0,1:T(2,128)S(1)}, u32[]{:S(2)}, u32[]{:S(2)}) async-start(f32[3,384,2,128]{3,2,0,1:T(2,128)} %copy.66), calls=%async_computation.1 | async-start | bytes 2359296 | tf_op jit(solution)/shard_map/all_to_all | solution.py:72
Sparse Core Ops, SparseCore 0:
  16.1 76.0 all-gather.1
where the time goes:
time: 187 us; the launch traced here: 186 us
  other arithmetic  99.4 us (53%)
  waiting for transfers between devices  29.1 us (16%)
  local copies, waits for them, and re-layouts  24.1 us (13%)
  between operations  16.2 us (9%)
  matrix products  9.25 us (5%)
  starting transfers between devices  7.86 us (4%)
    another operation x10, other arithmetic, implicit_matrix(): factor = jnp.linalg.cholesky(system)  56.3 us
    another operation x3, other arithmetic, implicit_matrix(): return jax.scipy.linalg.cho_solve((factor, True), amat)  30.4 us
    all_to_all x1, waiting for transfers between devices, shards(): lax.all_to_all(pre, 'line', split_axis=2, concat_axis=1, tiled=True)  15.1 us
    all_to_all x1, waiting for transfers between devices, shards(): lax.all_to_all(result, 'line', split_axis=1, concat_axis=2, tiled=True)  14 us
    another operation x9, local copies, waits for them, and re-layouts  7.42 us
    add x1, other arithmetic, shards(): pre = masked_values + 0.1 * rates  7.2 us
    unnamed x13, local copies, waits for them, and re-layouts  7.13 us
    all_to_all x1, starting transfers between devices, shards(): lax.all_to_all(pre, 'line', split_axis=2, concat_axis=1, tiled=True)  4.3 us
  transfers between devices with their start and end apart: 3, of which 2 were waited for; matrix products, arithmetic and copies ran while one was open for 55% of the time, Pallas kernels for 0%

commit v1 on v0

v1 whole, which is shorter than its diff:
```python
import functools

import jax
import jax.numpy as jnp
import ml_dtypes
import numpy as np
from jax import lax
from jax.experimental import pallas as pl
from jax.experimental.pallas import tpu as pltpu
from jax.sharding import PartitionSpec as P

HALO_LINES = 3
STENCIL = (2.0, -27.0, 270.0, -490.0, 270.0, -27.0, 2.0)
SLOTS, LANES = 8, 128
GROUP = 4
PER_TILE = LANES // GROUP


def implicit_matrix(count):
    gap = np.abs(np.arange(count)[:, None] - np.arange(count)[None, :])
    amat = np.where(gap == 0, 1.0, 0.0) + np.where(gap == 1, 2.0 / 11.0, 0.0)
    bmat = (
        np.where(gap == 0, -24.0 / 11.0 - 3.0 / 22.0, 0.0)
        + np.where(gap == 1, 12.0 / 11.0, 0.0)
        + np.where(gap == 2, 3.0 / 44.0, 0.0)
    )
    return np.linalg.solve(amat - 800.0 * bmat, amat)


@functools.lru_cache(None)
def tables(count, parts):
    kmat = implicit_matrix(count)
    size = count // parts
    cut = [slice(e * size, (e + 1) * size) for e in range(parts)]
    basis = {}
    for e in range(parts):
        for side, rows in (("after", slice((e + 1) * size, count)), ("before", slice(0, e * size))):
            block = kmat[rows, cut[e]]
            if block.size:
                basis[e, side] = np.linalg.svd(block, full_matrices=False)[2][:2]
    side = lambda e, i: "after" if i > e else "before"
    project = np.zeros((parts, 4, size))
    out = np.zeros((parts, 6, size))
    for e in range(parts):
        assert side(e, e ^ 2) == side(e, e ^ 3)
        project[e, 0:2] = basis[e, side(e, e ^ 1)]
        project[e, 2:4] = basis[e, side(e, e ^ 2)]
        for k in (1, 2, 3):
            src = e ^ k
            out[e, 2 * k - 2 : 2 * k] = (kmat[cut[e], cut[src]] @ basis[src, side(src, e)].T).T
    packed = np.zeros((parts, 4, size // PER_TILE, LANES))
    for h in range(size // PER_TILE):
        packed[:, :, h] = np.repeat(project[:, :, h * PER_TILE : (h + 1) * PER_TILE], GROUP, axis=2)
    own = np.stack([np.kron(kmat[c, c], np.eye(SLOTS)) for c in cut])
    high = own.astype(ml_dtypes.bfloat16)
    low = (own - high.astype(np.float64)).astype(ml_dtypes.bfloat16)
    f32 = np.float32
    return (
        project.reshape(parts, -1).astype(f32),
        packed.astype(f32),
        out.reshape(parts, -1).astype(f32),
        high,
        low,
    )


def iota(axis):
    return lax.broadcasted_iota(jnp.int32, (SLOTS, LANES), axis)


def by_slot(ref, f=lambda v: v):
    rows = iota(0)
    tile = jnp.full((SLOTS, LANES), f(ref[0]))
    for s in range(1, SLOTS):
        tile = jnp.where(rows == s, f(ref[s]), tile)
    return tile


def faces_kernel(lengths, field, faces):
    lane = iota(1)
    source = by_slot(lengths) - HALO_LINES + jnp.minimum(lane % GROUP, HALO_LINES - 1)
    tiles = faces.shape[0] // 3
    for k in range(faces.shape[0]):
        c, h = divmod(k, tiles)
        tile = jnp.zeros((SLOTS, LANES), jnp.float32)
        for j in range(PER_TILE):
            picked = jnp.take_along_axis(
                field[c, h * PER_TILE + j], source, axis=1, mode="promise_in_bounds"
            )
            tile = jnp.where(lane // GROUP == j, picked, tile)
        faces[k] = tile


def interior_kernel(lengths, project, field, stretch, rates, coef, edge):
    part = lax.axis_index("line")
    size = field.shape[1]
    lane = iota(1)
    live = jnp.where(lane < by_slot(lengths), 1.0, 0.0).astype(jnp.float32)
    weight = []
    for k in range(7):
        from_lane = lane + (k - 3)
        inside = (from_lane >= 0) & (from_lane < LANES)
        weight.append(jnp.where(inside, STENCIL[k] / 180.0, 0.0).astype(jnp.float32))

    for h in range(size // PER_TILE):

        def step(j, carry, h=h):
            sums, tile = carry
            p = h * PER_TILE + j
            metric = stretch[p]
            tile = jnp.where(lane // GROUP == j, pltpu.roll(metric, GROUP * j, 1), tile)
            metric = metric * live
            sums = list(sums)
            for c in range(3):
                x = field[c, p] * live
                second = weight[3] * x
                for k in (0, 1, 2, 4, 5, 6):
                    second = second + weight[k] * pltpu.roll(x, (3 - k) % LANES, 1)
                rate = metric * second
                rates[c, p] = rate
                pre = x + 0.1 * rate
                for r in range(4):
                    sums[3 * r + c] = sums[3 * r + c] + project[part, r * size + p] * pre
            return tuple(sums), tile

        zero = jnp.zeros((SLOTS, LANES), jnp.float32)
        start = (zero,) * 12 if h == 0 else sums
        sums, tile = lax.fori_loop(0, PER_TILE, step, (start, zero), unroll=4)
        edge[h] = tile
    for r in range(4):
        for c in range(3):
            coef[r, c] = sums[3 * r + c]


def ghost_kernel(connect, orient, packed, chip, far, pair, swap, edge, coef, delta, near_out, far_out, rows):
    part = lax.axis_index("line")
    blk = lax.axis_index("blk")
    core = blk % 2
    lane = iota(1)
    tiles = chip.shape[0]
    parts = tiles // 3
    for k in range(tiles):
        rows[0, k] = jnp.where(core == 0, swap[k], chip[k])
        rows[1, k] = pair[k]
        rows[2, k] = jnp.where(core == 0, pair[tiles + k], swap[k])
        rows[3, k] = jnp.where(core == 0, far[k], swap[tiles + k])
    count = lax.axis_size("blk")
    raw = [jnp.zeros((SLOTS, LANES), jnp.float32)] * tiles
    slot = iota(0)
    for s in range(SLOTS):
        shift = lax.rem(connect[s] // SLOTS - blk + count, count)
        which = jnp.where(shift == count - 1, 0, shift - (count // 2 - 1))
        src = connect[s] % SLOTS
        row = rows[which, :, pl.ds(src, 1), :]
        for k in range(tiles):
            raw[k] = jnp.where(slot == s, row[k], raw[k])
    cosine = by_slot(orient, lambda k: jnp.where(k == 0, 1.0, jnp.where(k == 2, -1.0, 0.0)))
    sine = by_slot(orient, lambda k: jnp.where(k == 1, 1.0, jnp.where(k == 3, -1.0, 0.0)))
    at = lane % GROUP
    w0 = jnp.where(at < 3, STENCIL[0] / 180.0, 0.0)
    w1 = jnp.where(at < 2, STENCIL[1] / 180.0, 0.0)
    w2 = jnp.where(at < 1, STENCIL[2] / 180.0, 0.0)
    sums = [None] * 12
    for h in range(parts):
        g0 = cosine * raw[h] - sine * raw[parts + h]
        g1 = sine * raw[h] + cosine * raw[parts + h]
        for c, g in enumerate((g0, g1, raw[2 * parts + h])):
            second = w0 * g + w1 * pltpu.roll(g, LANES - 1, 1) + w2 * pltpu.roll(g, LANES - 2, 1)
            rate = edge[h] * second
            delta[c * parts + h] = rate
            for r in range(4):
                term = packed[part, r, pl.ds(h, 1), :] * rate
                i = 3 * r + c
                sums[i] = term if h == 0 else sums[i] + term
    for step in (GROUP, 2 * GROUP, 4 * GROUP, 8 * GROUP, 16 * GROUP):
        sums = [v + pltpu.roll(v, step, 1) for v in sums]
    first = jnp.where(lane < HALO_LINES, 0.1, 0.0)
    for r in range(4):
        for c in range(3):
            total = coef[r, c] + first * sums[3 * r + c]
            if r < 2:
                near_out[r, c] = total
            else:
                far_out[r - 2, c] = total


def local_kernel(lengths, field, interior, delta, high_hbm, low_hbm, rates, local, high, low, x_high, x_low, sems):
    part = lax.axis_index("line")
    copy_high = pltpu.make_async_copy(high_hbm.at[part], high, sems.at[0])
    copy_low = pltpu.make_async_copy(low_hbm.at[part], low, sems.at[1])
    copy_high.start()
    copy_low.start()
    size = field.shape[1]
    lane = iota(1)
    live = jnp.where(lane < by_slot(lengths), 1.0, 0.0).astype(jnp.float32)
    first = lane < HALO_LINES
    tiles = size // PER_TILE
    for c in range(3):
        for h in range(tiles):

            def step(j2, _, c=c, h=h):
                highs, lows = [], []
                for u in range(2):
                    j = 2 * j2 + u
                    p = h * PER_TILE + j
                    ghost = pltpu.roll(delta[c * tiles + h], lax.rem(LANES - GROUP * j, LANES), 1)
                    rate = interior[c, p] + jnp.where(first, ghost, 0.0)
                    rates[c, p] = rate
                    pre = field[c, p] * live + 0.1 * rate
                    top = pre.astype(jnp.bfloat16)
                    highs.append(top)
                    lows.append((pre - top.astype(jnp.float32)).astype(jnp.bfloat16))
                at = pl.multiple_of((h * PER_TILE + 2 * j2) * SLOTS, 2 * SLOTS)
                x_high[pl.ds(at, 2 * SLOTS), pl.ds(c * LANES, LANES)] = jnp.concatenate(highs, axis=0)
                x_low[pl.ds(at, 2 * SLOTS), pl.ds(c * LANES, LANES)] = jnp.concatenate(lows, axis=0)
                return 0

            lax.fori_loop(0, PER_TILE // 2, step, 0, unroll=4)
    copy_high.wait()
    copy_low.wait()
    dot = functools.partial(jnp.dot, preferred_element_type=jnp.float32)
    block = 128
    for b in range(size * SLOTS // block):
        rows = pl.ds(b * block, block)
        total = dot(high[rows, :], x_high[...]) + dot(high[rows, :], x_low[...]) + dot(low[rows, :], x_high[...])
        for c in range(3):
            local[c, pl.ds(b * block // SLOTS, block // SLOTS)] = total[:, c * LANES : (c + 1) * LANES].reshape(
                block // SLOTS, SLOTS, LANES
            )


def last_kernel(out, local, one, two, three, advanced):
    part = lax.axis_index("line")
    size = local.shape[1]
    for c in range(3):
        got = [ref[r, c] for ref in (one, two, three) for r in range(2)]

        def step(p, _, c=c, got=got):
            total = local[c, p]
            for k in range(6):
                total = total + out[part, k * size + p] * got[k]
            advanced[c, p] = total
            return 0

        lax.fori_loop(0, size, step, 0, unroll=8)


SMEM = pl.BlockSpec(memory_space=pltpu.SMEM)
VMEM = pl.BlockSpec(memory_space=pltpu.VMEM)
HBM = pl.BlockSpec(memory_space=pltpu.HBM)


def call(kernel, name, ins, outs, mib, flops, moved, scratch=()):
    shape = lambda s: jax.ShapeDtypeStruct(s, jnp.float32)
    return pl.pallas_call(
        kernel,
        out_shape=[shape(s) for s in outs] if isinstance(outs, list) else shape(outs),
        in_specs=ins,
        out_specs=[VMEM] * len(outs) if isinstance(outs, list) else VMEM,
        scratch_shapes=scratch,
        compiler_params=pltpu.CompilerParams(vmem_limit_bytes=mib << 20),
        cost_estimate=pl.CostEstimate(flops=flops, bytes_accessed=moved, transcendentals=0),
        name=name,
    )


def shards(field, stretch, lengths, connect, orient, *, points, parts, count):
    size = field.shape[1]
    project, packed, out, high, low = (jnp.asarray(t) for t in tables(points, parts))
    tiles = 3 * (size // PER_TILE)
    block = (3, size, SLOTS, LANES)
    packed_tile = (tiles, SLOTS, LANES)
    half = count // 2

    def over_blk(x, pairs):
        return lax.ppermute(x, "blk", pairs)

    core = [(d ^ 1, d) for d in range(count)]
    pair = [((d + half) % count, d) for d in range(count)]
    far = [((d + half + 2) % count if d % 2 == 0 else (d - 2) % count, d) for d in range(count)]

    with jax.named_scope("faces"):
        faces = call(faces_kernel, "faces", [SMEM, VMEM], packed_tile, 8, 10**6, 1200000)(lengths, field)
        chip = over_blk(faces, core)
        both = jnp.concatenate([faces, chip], axis=0)
        from_far = over_blk(both, far)
        from_pair = over_blk(both, pair)
        swapped = over_blk(from_far, core)
    with jax.named_scope("interior"):
        interior, coef, edge = call(
            interior_kernel, "interior", [SMEM, SMEM, VMEM, VMEM],
            [block, (4, 3, SLOTS, LANES), (size // PER_TILE, SLOTS, LANES)], 8, 10**7, 3000000,
        )(lengths, project, field, stretch)
    with jax.named_scope("ghosts"):
        delta, near_sum, far_sum = call(
            ghost_kernel, "ghosts", [SMEM, SMEM] + [VMEM] * 7,
            [packed_tile, (2, 3, SLOTS, LANES), (2, 3, SLOTS, LANES)], 8, 10**6, 500000,
            scratch=[pltpu.VMEM((4,) + packed_tile, jnp.float32)],
        )(connect, orient, packed, chip, from_far, from_pair, swapped, edge, coef)

    def over_line(x, k):
        return lax.ppermute(x, "line", [(e ^ k, e) for e in range(parts)])

    with jax.named_scope("line"):
        got = [over_line(near_sum, 1), over_line(far_sum, 2), over_line(far_sum, 3)]
    with jax.named_scope("local"):
        rows = size * SLOTS
        rates, local = call(
            local_kernel, "local", [SMEM, VMEM, VMEM, VMEM, HBM, HBM], [block, block], 24, 3 * 10**9, 6000000,
            scratch=[
                pltpu.VMEM((rows, rows), jnp.bfloat16),
                pltpu.VMEM((rows, rows), jnp.bfloat16),
                pltpu.VMEM((rows, 3 * LANES), jnp.bfloat16),
                pltpu.VMEM((rows, 3 * LANES), jnp.bfloat16),
                pltpu.SemaphoreType.DMA((2,)),
            ],
        )(lengths, field, interior, delta, high, low)
    with jax.named_scope("last"):
        advanced = call(last_kernel, "last", [SMEM] + [VMEM] * 4, block, 8, 10**7, 2400000)(out, local, *got)
    return rates, advanced


def solution(mesh):
    parts, count = mesh.shape["line"], mesh.shape["blk"]

    def run(field, stretch, lengths, connect, orient):
        body = functools.partial(shards, points=field.shape[1], parts=parts, count=count)
        spec = P(None, "line", "blk", None)
        return jax.shard_map(
            body,
            mesh=mesh,
            in_specs=(spec, P("line", "blk", None), P("blk"), P("blk"), P("blk")),
            out_specs=(spec, spec),
            check_vma=False,
        )(field, stretch, lengths, connect, orient)

    return run
```

time: 187 us -> 43.5 us (0.23)
  the two profiles are of different devices: /device:TPU:160 before, /device:TPU:1 now
where the time goes in v1:
time: 43.5 us; the launch traced here: 43.2 us
  Pallas kernels  18.5 us (43%)
  starting transfers between devices  10.2 us (23%)
  local copies, waits for them, and re-layouts  7.62 us (18%)
  waiting for transfers between devices  6.09 us (14%)
  between operations  0.78 us (2%)
    unnamed x24, local copies, waits for them, and re-layouts  7.62 us
    ppermute x4, starting transfers between devices, over_blk(): return lax.ppermute(x, 'blk', pairs)  6.49 us
    pallas_call x1, Pallas kernels, shards(): call(local_kernel, 'local', [SMEM, VMEM, VMEM, VMEM, HBM, HBM], [block, b...  6.46 us
    ppermute x4, waiting for transfers between devices, over_blk(): return lax.ppermute(x, 'blk', pairs)  6.08 us
    pallas_call x1, Pallas kernels, shards(): call(last_kernel, 'last', [SMEM] + [VMEM] * 4, block, 8, 10 ** 7, 2400000)  5.62 us
    pallas_call x1, Pallas kernels, shards(): call(interior_kernel, 'interior', [SMEM, SMEM, VMEM, VMEM], [block, (4, 3...  4.46 us
    ppermute x3, starting transfers between devices, over_line(): return lax.ppermute(x, 'line', [(e ^ k, e) for e in range(parts)])  3.69 us
    pallas_call x1, Pallas kernels, shards(): call(ghost_kernel, 'ghosts', [SMEM, SMEM] + [VMEM] * 7, [packed_tile, (2,...  1.09 us
  transfers between devices with their start and end apart: 7, of which 2 were waited for; matrix products, arithmetic and copies ran while one was open for 0% of the time, Pallas kernels for 25%

profile of v1, /device:TPU:1, one launch (start us, length us, event | category | flops | bytes accessed | tf_op | source)
XLA Modules:
  0.0 43.2 jit_solution(6012147959419117436)
XLA Ops:
  0.6 0.0 copy-start.7
  0.7 1.3 %copy-done = f32[3,96,8,128]{3,2,1,0:T(8,128)S(1)} copy-done((f32[3,96,8,128]{3,2,1,0:T(8,128)S(1)}, f32[3,96,8,128]{3,2,1,0:T(8,128)}, u32[]{:S(2)}) %copy-start) | copy-done | bytes 1179672
  1.9 0.7 %copy-done.8 = s32[8]{0:T(128)S(1)} copy-done((s32[8]{0:T(128)S(1)}, s32[8]{0:T(128)}, u32[]{:S(2)}) %copy-start.8) | copy-done | bytes 56
  2.6 0.9 %faces.1 = f32[9,8,128]{2,1,0:T(8,128)S(1)} custom-call(s32[8]{0:T(128)S(1)} %copy-done.8, f32[3,96,8,128]{3,2,1,0:T(8,128)S(1)} %copy-done), custom_call_target="tpu_custom_call" | custom-call | flops 1000000 | bytes 1200000 | tf_op jit(solution)/shard_map/faces/faces/pallas_call | solution.py:283
  3.5 3.3 %collective-permute-start = (f32[9,8,128]{2,1,0:T(8,128)S(1)}, f32[9,8,128]{2,1,0:T(8,128)S(1)}, u32[]{:S(2)}, u32[]{:S(2)}) collective-permute-start(f32[9,8,128]{2,1,0:T(8,128)S(1)} %faces.1), channel_id=1, source_target_pairs={{4,0},{0,4},{12,8},{8,12},{20,16},{16,20},{28,24},{24,28},{36,32},... | collective-permute-start | bytes 110600 | tf_op jit(solution)/shard_map/faces/ppermute | solution.py:276
  6.9 0.9 %collective-permute-done.chip = f32[9,8,128]{2,1,0:T(8,128)S(1)} collective-permute-done((f32[9,8,128]{2,1,0:T(8,128)S(1)}, f32[9,8,128]{2,1,0:T(8,128)S(1)}, u32[]{:S(2)}, u32[]{:S(2)}) %collective-permute-start) | collective-permute-done | bytes 36896 | tf_op jit(solution)/shard_map/faces/ppermute | solution.py:276
  7.7 0.0 collective-permute-start.1
  7.7 2.8 %collective-permute-start.2 = (f32[18,8,128]{2,1,0:T(8,128)S(1)}, f32[18,8,128]{2,1,0:T(8,128)S(1)}, u32[]{:S(2)}, u32[]{:S(2)}) collective-permute-start(f32[18,8,128]{2,1,0:T(8,128)S(1)} %pad_maximum_fusion), channel_id=1, source_target_pairs={{128,0},{132,4},{136,8},{140,12},{144,16},{148,20},{152,24},{156,2... | collective-permute-start | bytes 221192 | tf_op jit(solution)/shard_map/faces/ppermute | solution.py:276
  10.5 5.2 %collective-permute-done.1.far = f32[18,8,128]{2,1,0:T(8,128)S(1)} collective-permute-done((f32[18,8,128]{2,1,0:T(8,128)S(1)}, f32[18,8,128]{2,1,0:T(8,128)S(1)}, u32[]{:S(2)}, u32[]{:S(2)}) %collective-permute-start.1) | collective-permute-done | bytes 73760 | tf_op jit(solution)/shard_map/faces/ppermute | solution.py:276
  15.8 0.4 collective-permute-start.3
  16.1 1.0 %copy-done.4 = f32[96,8,128]{2,1,0:T(8,128)S(1)} copy-done((f32[96,8,128]{2,1,0:T(8,128)S(1)}, f32[96,8,128]{2,1,0:T(8,128)}, u32[]{:S(2)}) %copy-start.4) | copy-done | bytes 393240
  17.1 4.5 %interior.1 = (f32[3,96,8,128]{3,2,1,0:T(8,128)S(1)}, f32[4,3,8,128]{3,2,1,0:T(8,128)S(1)}, f32[3,8,128]{2,1,0:T(8,128)S(1)}) custom-call(s32[8]{0:T(128)S(1)} %copy-done.9, f32[4,384]{1,0:T(4,128)S(1)} %copy-done.7, f32[3,96,8,128]{3,2,1,0:T(8,128)S(1)} %copy-done.1, f32[96,8,128]{2,1,0:T(8,128)S(1)} %copy-done.4), custom_call_target="tpu_custom_call" | custom-call | flops 10000000 | bytes 3000000 | tf_op jit(solution)/shard_map/interior/interior/pallas_call | solution.py:290
  21.6 0.0 collective-permute-done.2.pair
  21.6 0.0 collective-permute-done.3.swap
  21.6 1.1 %ghosts.1 = (f32[9,8,128]{2,1,0:T(8,128)S(1)}, f32[2,3,8,128]{3,2,1,0:T(8,128)S(1)}, f32[2,3,8,128]{3,2,1,0:T(8,128)S(1)}) custom-call(s32[8]{0:T(128)S(1)} %copy-done.10, s32[8]{0:T(128)S(1)} %copy-done.11, f32[4,4,3,128]{3,2,1,0:T(4,128)S(1)} %copy-done.5, f32[9,8,128]{2,1,0:T(8,128)S(1)} %collective-permute-done.chip, ...), custom_call_target="tpu_custom_call" | custom-call | flops 1000000 | bytes 500000 | tf_op jit(solution)/shard_map/ghosts/ghosts/pallas_call | solution.py:295
  22.7 2.8 %collective-permute-start.5 = (f32[2,3,8,128]{3,2,1,0:T(8,128)S(1)}, f32[2,3,8,128]{3,2,1,0:T(8,128)S(1)}, u32[]{:S(2)}, u32[]{:S(2)}) collective-permute-start(f32[2,3,8,128]{3,2,1,0:T(8,128)S(1)} %get-tuple-element.17), channel_id=1, source_target_pairs={{2,0},{3,1},{0,2},{1,3},{6,4},{7,5},{4,6},{5,7},{10,8},{11,9},{8,1... | collective-permute-start | bytes 73736 | tf_op jit(solution)/shard_map/line/ppermute | solution.py:302
  25.6 0.9 %collective-permute-start.6 = (f32[2,3,8,128]{3,2,1,0:T(8,128)S(1)}, f32[2,3,8,128]{3,2,1,0:T(8,128)S(1)}, u32[]{:S(2)}, u32[]{:S(2)}) collective-permute-start(f32[2,3,8,128]{3,2,1,0:T(8,128)S(1)} %get-tuple-element.17), channel_id=1, source_target_pairs={{3,0},{2,1},{1,2},{0,3},{7,4},{6,5},{5,6},{4,7},{11,8},{10,9},{9,1... | collective-permute-start | bytes 73736 | tf_op jit(solution)/shard_map/line/ppermute | solution.py:302
  26.4 0.0 collective-permute-start.4
  26.4 2.3 %copy-done.2 = bf16[4,768,768]{2,1,0:T(8,128)(2,1)S(1)} copy-done((bf16[4,768,768]{2,1,0:T(8,128)(2,1)S(1)}, bf16[4,768,768]{2,1,0:T(8,128)(2,1)}, u32[]{:S(2)}) %copy-start.2) | copy-done | bytes 4718616
  28.8 2.3 %copy-done.3 = bf16[4,768,768]{2,1,0:T(8,128)(2,1)S(1)} copy-done((bf16[4,768,768]{2,1,0:T(8,128)(2,1)S(1)}, bf16[4,768,768]{2,1,0:T(8,128)(2,1)}, u32[]{:S(2)}) %copy-start.3) | copy-done | bytes 4718616
  31.1 6.5 %local.1 = (f32[3,96,8,128]{3,2,1,0:T(8,128)}, f32[3,96,8,128]{3,2,1,0:T(8,128)S(1)}) custom-call(s32[8]{0:T(128)S(1)} %copy-done.9, f32[3,96,8,128]{3,2,1,0:T(8,128)S(1)} %copy-done.1, f32[3,96,8,128]{3,2,1,0:T(8,128)S(1)} %get-tuple-element.10.interior, f32[9,8,128]{2,1,0:T(8,128)S(1)} %get-tuple-element.13.delta, bf16[4,768,768]{2,1,0:T(8,128)(2,1)S(1)} %copy-done.2, ...), custom_call_target="tpu_custom_call" | custom-call | flops 3000000000 | bytes 6000000 | tf_op jit(solution)/shard_map/local/local/pallas_call | solution.py:308
  37.6 0.0 collective-permute-done.5.two
  37.6 0.0 collective-permute-done.6.three
  37.6 5.6 %last.1 = f32[3,96,8,128]{3,2,1,0:T(8,128)} custom-call(f32[4,576]{1,0:T(4,128)S(1)} %copy-done.6, f32[3,96,8,128]{3,2,1,0:T(8,128)S(1)} %get-tuple-element.15.local, f32[2,3,8,128]{3,2,1,0:T(8,128)S(1)} %collective-permute-done.4.one, f32[2,3,8,128]{3,2,1,0:T(8,128)S(1)} %collective-permute-done.5.two, f32[2,3,8,128]{3,2,1,0:T(8,128)S(1)} %collective-permute-done.6.three), custom_call_target="tpu_custom_call" | custom-call | flops 10000000 | bytes 2400000 | tf_op jit(solution)/shard_map/last/last/pallas_call | solution.py:319
  (20 shorter events, 0.0 us)
Async XLA Ops:
  0.6 15.5 %copy-start.7 = (f32[4,384]{1,0:T(4,128)S(1)}, f32[4,384]{1,0:T(4,128)}, u32[]{:S(2)}) copy-start(f32[4,384]{1,0:T(4,128)} %constant.10.clone.project) | copy-start | bytes 18436
  0.6 1.3 %copy-start = (f32[3,96,8,128]{3,2,1,0:T(8,128)S(1)}, f32[3,96,8,128]{3,2,1,0:T(8,128)}, u32[]{:S(2)}) copy-start(f32[3,96,8,128]{3,2,1,0:T(8,128)} %field.5) | copy-start | bytes 3538948
  1.9 0.7 %copy-start.8 = (s32[8]{0:T(128)S(1)}, s32[8]{0:T(128)}, u32[]{:S(2)}) copy-start(s32[8]{0:T(128)} %lengths.5) | copy-start | bytes 100
  2.6 13.5 %copy-start.1 = (f32[3,96,8,128]{3,2,1,0:T(8,128)S(1)}, f32[3,96,8,128]{3,2,1,0:T(8,128)}, u32[]{:S(2)}) copy-start(f32[3,96,8,128]{3,2,1,0:T(8,128)} %field.5) | copy-start | bytes 3538948
  2.6 13.5 %copy-start.9 = (s32[8]{0:T(128)S(1)}, s32[8]{0:T(128)}, u32[]{:S(2)}) copy-start(s32[8]{0:T(128)} %lengths.5) | copy-start | bytes 100
  2.6 19.0 %copy-start.5 = (f32[4,4,3,128]{3,2,1,0:T(4,128)S(1)}, f32[4,4,3,128]{3,2,1,0:T(4,128)}, u32[]{:S(2)}) copy-start(f32[4,4,3,128]{3,2,1,0:T(4,128)} %constant.11.clone.packed) | copy-start | bytes 73732
  2.6 19.0 %copy-start.10 = (s32[8]{0:T(128)S(1)}, s32[8]{0:T(128)}, u32[]{:S(2)}) copy-start(s32[8]{0:T(128)} %connect.1) | copy-start | bytes 100
  2.6 19.0 %copy-start.11 = (s32[8]{0:T(128)S(1)}, s32[8]{0:T(128)}, u32[]{:S(2)}) copy-start(s32[8]{0:T(128)} %orient.1) | copy-start | bytes 100
  3.5 4.2 %collective-permute-start = (f32[9,8,128]{2,1,0:T(8,128)S(1)}, f32[9,8,128]{2,1,0:T(8,128)S(1)}, u32[]{:S(2)}, u32[]{:S(2)}) collective-permute-start(f32[9,8,128]{2,1,0:T(8,128)S(1)} %faces.1), channel_id=1, source_target_pairs={{4,0},{0,4},{12,8},{8,12},{20,16},{16,20},{28,24},{24,28},{36,32},... | collective-permute-start | bytes 110600 | tf_op jit(solution)/shard_map/faces/ppermute | solution.py:276
  7.7 8.0 %collective-permute-start.1 = (f32[18,8,128]{2,1,0:T(8,128)S(1)}, f32[18,8,128]{2,1,0:T(8,128)S(1)}, u32[]{:S(2)}, u32[]{:S(2)}) collective-permute-start(f32[18,8,128]{2,1,0:T(8,128)S(1)} %pad_maximum_fusion), channel_id=1, source_target_pairs={{136,0},{252,4},{144,8},{4,12},{152,16},{12,20},{160,24},{20,28},{... | collective-permute-start | bytes 221192 | tf_op jit(solution)/shard_map/faces/ppermute | solution.py:276
  7.7 13.9 %collective-permute-start.2 = (f32[18,8,128]{2,1,0:T(8,128)S(1)}, f32[18,8,128]{2,1,0:T(8,128)S(1)}, u32[]{:S(2)}, u32[]{:S(2)}) collective-permute-start(f32[18,8,128]{2,1,0:T(8,128)S(1)} %pad_maximum_fusion), channel_id=1, source_target_pairs={{128,0},{132,4},{136,8},{140,12},{144,16},{148,20},{152,24},{156,2... | collective-permute-start | bytes 221192 | tf_op jit(solution)/shard_map/faces/ppermute | solution.py:276
  15.8 5.8 %collective-permute-start.3 = (f32[18,8,128]{2,1,0:T(8,128)S(1)}, f32[18,8,128]{2,1,0:T(8,128)S(1)}, u32[]{:S(2)}, u32[]{:S(2)}) collective-permute-start(f32[18,8,128]{2,1,0:T(8,128)S(1)} %collective-permute-done.1.far), channel_id=1, source_target_pairs={{4,0},{0,4},{12,8},{8,12},{20,16},{16,20},{28,24},{24,28},{36,32},... | collective-permute-start | bytes 221192 | tf_op jit(solution)/shard_map/faces/ppermute | solution.py:276
  16.1 1.0 %copy-start.4 = (f32[96,8,128]{2,1,0:T(8,128)S(1)}, f32[96,8,128]{2,1,0:T(8,128)}, u32[]{:S(2)}) copy-start(f32[96,8,128]{2,1,0:T(8,128)} %stretch.1) | copy-start | bytes 1179652
  22.7 14.8 %collective-permute-start.5 = (f32[2,3,8,128]{3,2,1,0:T(8,128)S(1)}, f32[2,3,8,128]{3,2,1,0:T(8,128)S(1)}, u32[]{:S(2)}, u32[]{:S(2)}) collective-permute-start(f32[2,3,8,128]{3,2,1,0:T(8,128)S(1)} %get-tuple-element.17), channel_id=1, source_target_pairs={{2,0},{3,1},{0,2},{1,3},{6,4},{7,5},{4,6},{5,7},{10,8},{11,9},{8,1... | collective-permute-start | bytes 73736 | tf_op jit(solution)/shard_map/line/ppermute | solution.py:302
  25.6 12.0 %collective-permute-start.6 = (f32[2,3,8,128]{3,2,1,0:T(8,128)S(1)}, f32[2,3,8,128]{3,2,1,0:T(8,128)S(1)}, u32[]{:S(2)}, u32[]{:S(2)}) collective-permute-start(f32[2,3,8,128]{3,2,1,0:T(8,128)S(1)} %get-tuple-element.17), channel_id=1, source_target_pairs={{3,0},{2,1},{1,2},{0,3},{7,4},{6,5},{5,6},{4,7},{11,8},{10,9},{9,1... | collective-permute-start | bytes 73736 | tf_op jit(solution)/shard_map/line/ppermute | solution.py:302
  26.4 11.2 %collective-permute-start.4 = (f32[2,3,8,128]{3,2,1,0:T(8,128)S(1)}, f32[2,3,8,128]{3,2,1,0:T(8,128)S(1)}, u32[]{:S(2)}, u32[]{:S(2)}) collective-permute-start(f32[2,3,8,128]{3,2,1,0:T(8,128)S(1)} %get-tuple-element.16), channel_id=1, source_target_pairs={{1,0},{0,1},{3,2},{2,3},{5,4},{4,5},{7,6},{6,7},{9,8},{8,9},{11,10... | collective-permute-start | bytes 73736 | tf_op jit(solution)/shard_map/line/ppermute | solution.py:302
  26.4 2.3 %copy-start.2 = (bf16[4,768,768]{2,1,0:T(8,128)(2,1)S(1)}, bf16[4,768,768]{2,1,0:T(8,128)(2,1)}, u32[]{:S(2)}) copy-start(bf16[4,768,768]{2,1,0:T(8,128)(2,1)} %constant.13.clone.high_hbm) | copy-start | bytes 14155780
  28.8 2.3 %copy-start.3 = (bf16[4,768,768]{2,1,0:T(8,128)(2,1)S(1)}, bf16[4,768,768]{2,1,0:T(8,128)(2,1)}, u32[]{:S(2)}) copy-start(bf16[4,768,768]{2,1,0:T(8,128)(2,1)} %constant.14.clone.low_hbm) | copy-start | bytes 14155780
  31.1 6.5 %copy-start.6 = (f32[4,576]{1,0:T(4,128)S(1)}, f32[4,576]{1,0:T(4,128)}, u32[]{:S(2)}) copy-start(f32[4,576]{1,0:T(4,128)} %constant.12.clone.out) | copy-start | bytes 27652

commit v2 on v1

v2 whole, which is shorter than its diff:
```python
import functools

import jax
import jax.numpy as jnp
import ml_dtypes
import numpy as np
from jax import lax
from jax.experimental import pallas as pl
from jax.experimental.pallas import tpu as pltpu
from jax.sharding import PartitionSpec as P

HALO_LINES = 3
STENCIL = (2.0, -27.0, 270.0, -490.0, 270.0, -27.0, 2.0)
SLOTS, LANES = 8, 128
GROUP = 4
PER_TILE = LANES // GROUP


def implicit_matrix(count):
    gap = np.abs(np.arange(count)[:, None] - np.arange(count)[None, :])
    amat = np.where(gap == 0, 1.0, 0.0) + np.where(gap == 1, 2.0 / 11.0, 0.0)
    bmat = (
        np.where(gap == 0, -24.0 / 11.0 - 3.0 / 22.0, 0.0)
        + np.where(gap == 1, 12.0 / 11.0, 0.0)
        + np.where(gap == 2, 3.0 / 44.0, 0.0)
    )
    inverse = np.linalg.inv(amat - 800.0 * bmat)
    return inverse, inverse @ amat


@functools.lru_cache(None)
def tables(count, parts):
    inverse, kmat = implicit_matrix(count)
    size = count // parts
    cut = [slice(e * size, (e + 1) * size) for e in range(parts)]
    basis = {}
    for e in range(parts):
        for side, rows in (("after", slice((e + 1) * size, count)), ("before", slice(0, e * size))):
            block = kmat[rows, cut[e]]
            if block.size:
                basis[e, side] = np.linalg.svd(block, full_matrices=False)[2][:2]
    side = lambda e, i: "after" if i > e else "before"
    project = np.zeros((parts, 4, size))
    out = np.zeros((parts, 6, size))
    for e in range(parts):
        assert side(e, e ^ 2) == side(e, e ^ 3)
        project[e, 0:2] = basis[e, side(e, e ^ 1)]
        project[e, 2:4] = basis[e, side(e, e ^ 2)]
        for k in (1, 2, 3):
            src = e ^ k
            out[e, 2 * k - 2 : 2 * k] = (kmat[cut[e], cut[src]] @ basis[src, side(src, e)].T).T
    packed = np.zeros((parts, 4, size // PER_TILE, LANES))
    for h in range(size // PER_TILE):
        packed[:, :, h] = np.repeat(project[:, :, h * PER_TILE : (h + 1) * PER_TILE], GROUP, axis=2)
    rows = lambda t: np.repeat(t[..., None], LANES, axis=-1).astype(np.float32)
    forward = np.zeros((parts, 5, size + SLOTS))
    back = np.zeros((parts, 2, size))
    for e, c in enumerate(cut):
        inner, lower, pivot, upper, right = own_block(kmat, inverse, c)
        for p in range(size):
            for k, q in enumerate((p - 1, p, p + 1)):
                if 0 <= q < size:
                    forward[e, k, p + 1] = right[p, q] / pivot[p]
            for k in (1, 2):
                if p >= k:
                    forward[e, 2 + k, p + 1] = -lower[p, p - k] * pivot[p - k] / pivot[p]
                if p + k < size:
                    back[e, k - 1, p] = -upper[p, p + k]
    outer = np.stack([np.kron(t.T, np.eye(SLOTS)) for t in out])
    high, low = split(outer)
    outer = np.concatenate([high, high, low], axis=2)
    line = np.arange(LANES)
    gap = line[:, None] - line[None, :] + 3
    band = np.where((gap >= 0) & (gap <= 6), np.take(np.asarray(STENCIL), np.clip(gap, 0, 6)), 0.0)
    band = np.concatenate([band, band]).astype(ml_dtypes.bfloat16)
    return rows(project), packed.astype(np.float32), rows(forward), rows(back), outer, band


def split(x):
    high = x.astype(ml_dtypes.bfloat16)
    return high, (x - high.astype(np.float64)).astype(ml_dtypes.bfloat16)


def own_block(kmat, inverse, c):
    t = np.linalg.inv(inverse[c, c])
    right = t @ kmat[c, c]
    size = len(t)
    gap = np.abs(np.arange(size)[:, None] - np.arange(size)[None, :])
    assert np.abs(t[gap > 2]).max() < 1e-8 and np.abs(right[gap > 1]).max() < 1e-8
    t = np.where(gap > 2, 0.0, t)
    upper = t.copy()
    lower = np.eye(size)
    for p in range(size):
        for q in range(p + 1, min(p + 3, size)):
            lower[q, p] = upper[q, p] / upper[p, p]
            upper[q] -= lower[q, p] * upper[p]
    pivot = np.diag(upper).copy()
    return t, lower, pivot, upper / pivot[:, None], right


def iota(axis):
    return lax.broadcasted_iota(jnp.int32, (SLOTS, LANES), axis)


def is_live(lengths):
    return jnp.where(iota(1) < lengths[...], 1.0, 0.0).astype(jnp.float32)


def faces_kernel(lengths, field, faces, held, sems):
    lane = iota(1)
    source = lengths[...] - HALO_LINES + jnp.minimum(lane % GROUP, HALO_LINES - 1)
    tiles = faces.shape[0] // 3
    pieces = [(c, pl.ds(h * PER_TILE, PER_TILE)) for c in range(3) for h in range(tiles)]
    copies = [pltpu.make_async_copy(field.at[at], held.at[at], sems.at[k]) for k, at in enumerate(pieces)]
    for copy in copies:
        copy.start()
    for k, copy in enumerate(copies):
        copy.wait()
        c, h = divmod(k, tiles)
        tile = jnp.zeros((SLOTS, LANES), jnp.float32)
        for j in range(PER_TILE):
            picked = jnp.take_along_axis(
                held[c, h * PER_TILE + j], source, axis=1, mode="promise_in_bounds"
            )
            tile = jnp.where(lane // GROUP == j, picked, tile)
        faces[k] = tile


def interior_kernel(begin, more, *refs):
    lengths, project, band, field, stretch, *refs = refs
    before, (rates, coef, edge) = (refs[0] if more else None), refs[-3:]
    part = lax.axis_index("line")
    lane = iota(1)
    live = is_live(lengths)
    scale = live * (1.0 / 180.0)
    sums = [[None] * 3 for _ in range(4)]
    for h in range(edge.shape[0]):
        tile = jnp.zeros((SLOTS, LANES), jnp.float32)
        at = begin + h * PER_TILE
        for j in range(PER_TILE):
            tile = jnp.where(lane // GROUP == j, pltpu.roll(stretch[at + j], GROUP * j, 1), tile)
        edge[h] = tile
        for c in range(3):
            block = field[c, at : at + PER_TILE] * live
            flat = block.reshape(PER_TILE * SLOTS, LANES)
            high = flat.astype(jnp.bfloat16)
            low = (flat - high.astype(jnp.float32)).astype(jnp.bfloat16)
            second = jnp.dot(
                jnp.concatenate([high, low], axis=1), band[...], preferred_element_type=jnp.float32
            ).reshape(PER_TILE, SLOTS, LANES)
            for j in range(PER_TILE):
                rate = (stretch[at + j] * scale) * second[j]
                rates[c, h * PER_TILE + j] = rate
                pre = block[j] + 0.1 * rate
                for r in range(4):
                    term = project[part, r, at + j : at + j + 1, :] * pre
                    sums[r][c] = term if sums[r][c] is None else sums[r][c] + term
    for r in range(4):
        for c in range(3):
            coef[r, c] = sums[r][c] + before[r, c] if more else sums[r][c]


def ghost_kernel(connect, orient, packed, chip, far, pair, swap, edge_a, edge_b, coef, delta, near_out, far_out):
    part = lax.axis_index("line")
    blk = lax.axis_index("blk")
    count = lax.axis_size("blk")
    even = blk % 2 == 0
    lane = iota(1)
    tiles = chip.shape[0]
    parts = tiles // 3
    shift = (connect[...] // SLOTS - blk) & (count - 1)
    src = connect[...] % SLOTS
    is_one, is_two, is_three = shift == count // 2, shift == count // 2 + 1, shift == count // 2 + 2
    raw = []
    for k in range(tiles):
        pick = lambda v: jnp.take_along_axis(v, src, axis=0, mode="promise_in_bounds")
        row = pick(jnp.where(even, swap[k], chip[k]))
        row = jnp.where(is_one, pick(pair[k]), row)
        row = jnp.where(is_two, pick(jnp.where(even, pair[tiles + k], swap[k])), row)
        raw.append(jnp.where(is_three, pick(jnp.where(even, far[k], swap[tiles + k])), row))
    turn = orient[...]
    cosine = jnp.where(turn == 0, 1.0, jnp.where(turn == 2, -1.0, 0.0))
    sine = jnp.where(turn == 1, 1.0, jnp.where(turn == 3, -1.0, 0.0))
    at = lane % GROUP
    w0 = jnp.where(at < 3, STENCIL[0] / 180.0, 0.0)
    w1 = jnp.where(at < 2, STENCIL[1] / 180.0, 0.0)
    w2 = jnp.where(at < 1, STENCIL[2] / 180.0, 0.0)
    sums = [None] * 12
    for h in range(parts):
        g0 = cosine * raw[h] - sine * raw[parts + h]
        g1 = sine * raw[h] + cosine * raw[parts + h]
        for c, g in enumerate((g0, g1, raw[2 * parts + h])):
            second = w0 * g + w1 * pltpu.roll(g, LANES - 1, 1) + w2 * pltpu.roll(g, LANES - 2, 1)
            rate = (edge_a[h] if h < edge_a.shape[0] else edge_b[h - edge_a.shape[0]]) * second
            delta[c * parts + h] = rate
            for r in range(4):
                term = packed[part, r, h : h + 1, :] * rate
                i = 3 * r + c
                sums[i] = term if h == 0 else sums[i] + term
    for step in (GROUP, 2 * GROUP, 4 * GROUP, 8 * GROUP, 16 * GROUP):
        sums = [v + pltpu.roll(v, step, 1) for v in sums]
    first = jnp.where(lane < HALO_LINES, 0.1, 0.0)
    for r in range(4):
        for c in range(3):
            total = coef[r, c] + first * sums[3 * r + c]
            if r < 2:
                near_out[r, c] = total
            else:
                far_out[r - 2, c] = total


def local_kernel(lengths, forward, back, field, rates_a, rates_b, delta, rates, local, full, held, sems):
    part = lax.axis_index("line")
    size = field.shape[1]
    live = is_live(lengths)
    first = iota(1) < HALO_LINES
    tiles = size // PER_TILE
    zero = jnp.zeros((SLOTS, LANES), jnp.float32)
    step = 8

    def advance(p, x, state):
        weight = [forward[part, k, pl.ds(p, 1), :] for k in range(5)]
        new = []
        for c in range(3):
            x2, x1, y1, y2 = state[c]
            y = (weight[0] * x2 + weight[1] * x1 + weight[2] * x[c] + weight[4] * y2) + weight[3] * y1
            held[c, p] = y
            new.append((x1, x[c], y, y1))
        return new

    state = [(zero, zero, zero, zero)] * 3
    copies = []
    for h in range(tiles):
        ghosts = [delta[c * tiles + h] for c in range(3)]
        inner, offset = (rates_a, 0) if h * PER_TILE < rates_a.shape[1] else (rates_b, rates_a.shape[1])

        def body(i, carry, h=h, inner=inner, offset=offset):
            state, ghosts = carry
            for u in range(step):
                p = h * PER_TILE + step * i + u
                x = []
                for c in range(3):
                    ghost = ghosts[c] if u == 0 else pltpu.roll(ghosts[c], LANES - GROUP * u, 1)
                    rate = inner[c, p - offset] + jnp.where(first, ghost, 0.0)
                    full[c, p] = rate
                    x.append(field[c, p] * live + 0.1 * rate)
                state = advance(p, x, state)
            return state, [pltpu.roll(g, LANES - GROUP * step, 1) for g in ghosts]

        state, _ = lax.fori_loop(0, PER_TILE // step, body, (state, ghosts))
        at = (slice(None), pl.ds(h * PER_TILE, PER_TILE))
        copies.append(pltpu.make_async_copy(full.at[at], rates.at[at], sems.at[h]))
        copies[-1].start()
    state = advance(size, [zero] * 3, state)

    def descend(i, carry):
        new = list(carry)
        for u in range(step):
            p = size - 1 - (step * i + u)
            one, two = back[part, 0, pl.ds(p, 1), :], back[part, 1, pl.ds(p, 1), :]
            for c in range(3):
                z1, z2 = new[c]
                z = (held[c, p + 1] + two * z2) + one * z1
                local[c, p] = z
                new[c] = (z, z1)
        return new

    lax.fori_loop(0, size // step, descend, [(zero, zero)] * 3)
    for copy in copies:
        copy.wait()


def last_kernel(outer, local, one, two, three, advanced, full, sems):
    part = lax.axis_index("line")
    size = local.shape[1]
    got = jnp.concatenate(
        [jnp.concatenate([ref[r, c] for c in range(3)], axis=1) for ref in (one, two, three) for r in range(2)], axis=0
    )
    high = got.astype(jnp.bfloat16)
    low = (got - high.astype(jnp.float32)).astype(jnp.bfloat16)
    got = jnp.concatenate([high, low, high], axis=0)
    copies = []
    for h in range(size // PER_TILE):
        rows = slice(h * PER_TILE * SLOTS, (h + 1) * PER_TILE * SLOTS)
        total = jnp.dot(outer[part, rows, :], got, preferred_element_type=jnp.float32)
        at = pl.ds(h * PER_TILE, PER_TILE)
        for c in range(3):
            tile = total[:, c * LANES : (c + 1) * LANES].reshape(PER_TILE, SLOTS, LANES)
            full[c, at] = local[c, at] + tile
            copies.append(pltpu.make_async_copy(full.at[c, at], advanced.at[c, at], sems.at[3 * h + c]))
            copies[-1].start()
    for copy in copies:
        copy.wait()


SMEM = pl.BlockSpec(memory_space=pltpu.SMEM)
VMEM = pl.BlockSpec(memory_space=pltpu.VMEM)
HBM = pl.BlockSpec(memory_space=pltpu.HBM)


def call(kernel, name, ins, outs, mib, flops, moved, scratch=(), out_specs=None):
    shape = lambda s: jax.ShapeDtypeStruct(s, jnp.float32)
    return pl.pallas_call(
        kernel,
        out_shape=[shape(s) for s in outs],
        in_specs=ins,
        out_specs=out_specs or [VMEM] * len(outs),
        scratch_shapes=scratch,
        compiler_params=pltpu.CompilerParams(vmem_limit_bytes=mib << 20),
        cost_estimate=pl.CostEstimate(flops=flops, bytes_accessed=moved, transcendentals=0),
        name=name,
    )


def shards(field, stretch, lengths, connect, orient, *, points, parts, count):
    size = field.shape[1]
    project, packed, forward, back, outer, band = (jnp.asarray(t) for t in tables(points, parts))
    tiles = 3 * (size // PER_TILE)
    block = (3, size, SLOTS, LANES)
    packed_tile = (tiles, SLOTS, LANES)
    sums = (4, 3, SLOTS, LANES)
    half = count // 2
    lengths, connect, orient = (jnp.broadcast_to(v[:, None], (SLOTS, LANES)) for v in (lengths, connect, orient))
    dma = pltpu.SemaphoreType.DMA

    def over_blk(x, pairs):
        return lax.ppermute(x, "blk", pairs)

    core = [(d ^ 1, d) for d in range(count)]
    pair = [((d + half) % count, d) for d in range(count)]
    far = [((d + half + 2) % count if d % 2 == 0 else (d - 2) % count, d) for d in range(count)]

    field = pltpu.with_memory_space_constraint(field, pltpu.HBM)
    with jax.named_scope("faces"):
        faces, held = call(
            faces_kernel, "faces", [VMEM, HBM], [packed_tile, block], 8, 10**6, 1200000, scratch=[dma((tiles,))]
        )(lengths, field)
        chip = over_blk(faces, core)

    def inside(begin, length, metric, *before):
        return call(
            functools.partial(interior_kernel, begin, bool(before)), "interior", [VMEM] * (5 + len(before)),
            [(3, length, SLOTS, LANES), sums, (length // PER_TILE, SLOTS, LANES)], 8, 10**7, 1500000,
        )(lengths, project, band, held, metric, *before)

    with jax.named_scope("interior"):
        rates_a, coef, edge_a = inside(0, PER_TILE, stretch)
        chip, rates_a, coef, edge_a = lax.optimization_barrier((chip, rates_a, coef, edge_a))
    with jax.named_scope("faces"):
        both = jnp.concatenate([faces, chip], axis=0)
        from_far = over_blk(both, far)
        from_pair = over_blk(both, pair)
        from_far, coef = lax.optimization_barrier((from_far, coef))
        swapped = over_blk(from_far, core)
    with jax.named_scope("interior"):
        rates_b, coef, edge_b = inside(PER_TILE, size - PER_TILE, stretch, coef)
    with jax.named_scope("ghosts"):
        delta, near_sum, far_sum = call(
            ghost_kernel, "ghosts", [VMEM] * 10,
            [packed_tile, (2, 3, SLOTS, LANES), (2, 3, SLOTS, LANES)], 8, 10**6, 500000,
        )(connect, orient, packed, chip, from_far, from_pair, swapped, edge_a, edge_b, coef)

    def over_line(x, k):
        return lax.ppermute(x, "line", [(e ^ k, e) for e in range(parts)])

    with jax.named_scope("line"):
        got = [over_line(near_sum, 1), over_line(far_sum, 2), over_line(far_sum, 3)]
    with jax.named_scope("local"):
        rates, local = call(
            local_kernel, "local", [VMEM] * 7, [block, block], 12, 10**8, 6000000,
            out_specs=[HBM, VMEM],
            scratch=[
                pltpu.VMEM(block, jnp.float32),
                pltpu.VMEM((3, size + 1, SLOTS, LANES), jnp.float32),
                dma((size // PER_TILE,)),
            ],
        )(lengths, forward, back, held, rates_a, rates_b, delta)
    with jax.named_scope("last"):
        (advanced,) = call(
            last_kernel, "last", [VMEM] * 5, [block], 8, 10**7, 2400000, out_specs=[HBM],
            scratch=[pltpu.VMEM(block, jnp.float32), dma((tiles,))],
        )(outer, local, *got)
    return rates, advanced


def solution(mesh):
    parts, count = mesh.shape["line"], mesh.shape["blk"]

    def run(field, stretch, lengths, connect, orient):
        body = functools.partial(shards, points=field.shape[1], parts=parts, count=count)
        spec = P(None, "line", "blk", None)
        return jax.shard_map(
            body,
            mesh=mesh,
            in_specs=(spec, P("line", "blk", None), P("blk"), P("blk"), P("blk")),
            out_specs=(spec, spec),
            check_vma=False,
        )(field, stretch, lengths, connect, orient)

    return run
```

time: 43.5 us -> 28.6 us (0.66)
  the two profiles are of different devices: /device:TPU:1 before, /device:TPU:8 now
where the time goes in v2:
time: 28.6 us; the launch traced here: 28.5 us
  starting transfers between devices  12.3 us (43%)
  waiting for transfers between devices  7.64 us (27%)
  Pallas kernels  6.77 us (24%)
  local copies, waits for them, and re-layouts  1.02 us (4%)
  between operations  0.78 us (3%)
    ppermute x4, starting transfers between devices, over_blk(): return lax.ppermute(x, 'blk', pairs)  7.98 us
    ppermute x4, waiting for transfers between devices, over_blk(): return lax.ppermute(x, 'blk', pairs)  5.07 us
    ppermute x3, starting transfers between devices, over_line(): return lax.ppermute(x, 'line', [(e ^ k, e) for e in range(parts)])  4.31 us
    ppermute x3, waiting for transfers between devices, over_line(): return lax.ppermute(x, 'line', [(e ^ k, e) for e in range(parts)])  2.57 us
    pallas_call x1, Pallas kernels, shards(): call(local_kernel, 'local', [VMEM] * 7, [block, block], 12, 10 ** 8, 6000...  2.1 us
    pallas_call x1, Pallas kernels, shards(): call(faces_kernel, 'faces', [VMEM, HBM], [packed_tile, block], 8, 10 ** 6...  1.92 us
    pallas_call x1, Pallas kernels, shards(): call(last_kernel, 'last', [VMEM] * 5, [block], 8, 10 ** 7, 2400000, out_s...  1.3 us
    pallas_call x2, Pallas kernels, inside(): call(functools.partial(interior_kernel, begin, bool(before)), 'interior',...  0.98 us
  transfers between devices with their start and end apart: 7, of which 5 were waited for; matrix products, arithmetic and copies ran while one was open for 0% of the time, Pallas kernels for 11%

profile of v2, /device:TPU:8, one launch (start us, length us, event | category | flops | bytes accessed | tf_op | source)
XLA Modules:
  0.0 28.5 jit_solution(17065966490270694498)
XLA Ops:
  0.6 0.0 copy-start.5
  0.6 0.0 copy-start
  0.7 0.8 %broadcast_in_dim.6.lengths.refs_0_ = s32[8,128]{1,0:T(8,128)S(1)} broadcast(s32[8]{0:T(128)} %param.13), dimensions={0} | broadcast | bytes 4128 | tf_op jit(solution)/shard_map/broadcast_in_dim | solution.py:323
  1.5 1.9 %faces.1 = (f32[9,8,128]{2,1,0:T(8,128)S(1)}, f32[3,96,8,128]{3,2,1,0:T(8,128)S(1)}) custom-call(s32[8,128]{1,0:T(8,128)S(1)} %broadcast_in_dim.6.lengths.refs_0_, f32[3,96,8,128]{3,2,1,0:T(8,128)} %field.1), custom_call_target="tpu_custom_call" | custom-call | flops 1000000 | bytes 1200000 | tf_op jit(solution)/shard_map/faces/faces/pallas_call | solution.py:335
  3.4 0.1 collective-permute-start
  3.6 0.3 %interior.2 = (f32[3,32,8,128]{3,2,1,0:T(8,128)S(1)}, f32[4,3,8,128]{3,2,1,0:T(8,128)S(1)}, f32[1,8,128]{2,1,0:T(8,128)S(1)}) custom-call(s32[8,128]{1,0:T(8,128)S(1)} %broadcast_in_dim.6.lengths.refs_0_, f32[4,4,96,128]{3,2,1,0:T(8,128)S(1)} %copy-done, bf16[256,128]{1,0:T(8,128)(2,1)S(1)} %copy-done.5, ...), custom_call_target="tpu_custom_call" | custom-call | flops 10000000 | bytes 1500000 | tf_op jit(solution)/shard_map/interior/interior/pallas_call | solution.py:341
  3.9 0.8 %collective-permute-done.chip = f32[9,8,128]{2,1,0:T(8,128)S(1)} collective-permute-done((f32[9,8,128]{2,1,0:T(8,128)S(1)}, f32[9,8,128]{2,1,0:T(8,128)S(1)}, u32[]{:S(2)}, u32[]{:S(2)}) %collective-permute-start) | collective-permute-done | bytes 36896 | tf_op jit(solution)/shard_map/faces/ppermute | solution.py:327
  4.7 0.0 copy-start.3
  4.8 0.0 copy-start.4
  4.8 6.9 %collective-permute-start.1 = (f32[18,8,128]{2,1,0:T(8,128)S(1)}, f32[18,8,128]{2,1,0:T(8,128)S(1)}, u32[]{:S(2)}, u32[]{:S(2)}) collective-permute-start(f32[18,8,128]{2,1,0:T(8,128)S(1)} %constant_dynamic-update-slice_fusion), channel_id=1, source_target_pairs={{136,0},{252,4},{144,8},{4,12},{152,16},{12,20},{160,24},{20,28},{... | collective-permute-start | bytes 221192 | tf_op jit(solution)/shard_map/faces/ppermute | solution.py:327
  11.7 0.9 %collective-permute-start.2 = (f32[18,8,128]{2,1,0:T(8,128)S(1)}, f32[18,8,128]{2,1,0:T(8,128)S(1)}, u32[]{:S(2)}, u32[]{:S(2)}) collective-permute-start(f32[18,8,128]{2,1,0:T(8,128)S(1)} %constant_dynamic-update-slice_fusion), channel_id=1, source_target_pairs={{128,0},{132,4},{136,8},{140,12},{144,16},{148,20},{152,24},{156,2... | collective-permute-start | bytes 221192 | tf_op jit(solution)/shard_map/faces/ppermute | solution.py:327
  12.7 1.0 %collective-permute-done.1.far = f32[18,8,128]{2,1,0:T(8,128)S(1)} collective-permute-done((f32[18,8,128]{2,1,0:T(8,128)S(1)}, f32[18,8,128]{2,1,0:T(8,128)S(1)}, u32[]{:S(2)}, u32[]{:S(2)}) %collective-permute-start.1) | collective-permute-done | bytes 73760 | tf_op jit(solution)/shard_map/faces/ppermute | solution.py:327
  13.7 0.6 %interior.3 = (f32[3,64,8,128]{3,2,1,0:T(8,128)S(1)}, f32[4,3,8,128]{3,2,1,0:T(8,128)S(1)}, f32[2,8,128]{2,1,0:T(8,128)S(1)}) custom-call(s32[8,128]{1,0:T(8,128)S(1)} %broadcast_in_dim.6.lengths.refs_0_, f32[4,4,96,128]{3,2,1,0:T(8,128)S(1)} %copy-done, bf16[256,128]{1,0:T(8,128)(2,1)S(1)} %copy-done.5, ...), custom_call_target="tpu_custom_call" | custom-call | flops 10000000 | bytes 1500000 | tf_op jit(solution)/shard_map/interior/interior/pallas_call | solution.py:341
  14.3 3.2 %collective-permute-done.2.pair = f32[18,8,128]{2,1,0:T(8,128)S(1)} collective-permute-done((f32[18,8,128]{2,1,0:T(8,128)S(1)}, f32[18,8,128]{2,1,0:T(8,128)S(1)}, u32[]{:S(2)}, u32[]{:S(2)}) %collective-permute-start.2) | collective-permute-done | bytes 73760 | tf_op jit(solution)/shard_map/faces/ppermute | solution.py:327
  17.6 0.1 broadcast_in_dim.7.connect
  17.6 0.1 broadcast_in_dim.8.orient
  17.7 0.5 %ghosts.1 = (f32[9,8,128]{2,1,0:T(8,128)S(1)}, f32[2,3,8,128]{3,2,1,0:T(8,128)S(1)}, f32[2,3,8,128]{3,2,1,0:T(8,128)S(1)}) custom-call(s32[8,128]{1,0:T(8,128)S(1)} %broadcast_in_dim.7.connect, s32[8,128]{1,0:T(8,128)S(1)} %broadcast_in_dim.8.orient, f32[4,4,3,128]{3,2,1,0:T(4,128)S(1)} %copy-done.6, f32[9,8,128]{2,1,0:T(8,128)S(1)} %collective-permute-done.chip, ...), custom_call_target="tpu_custom_call" | custom-call | flops 1000000 | bytes 500000 | tf_op jit(solution)/shard_map/ghosts/ghosts/pallas_call | solution.py:358
  18.2 1.6 %collective-permute-start.4 = (f32[2,3,8,128]{3,2,1,0:T(8,128)S(1)}, f32[2,3,8,128]{3,2,1,0:T(8,128)S(1)}, u32[]{:S(2)}, u32[]{:S(2)}) collective-permute-start(f32[2,3,8,128]{3,2,1,0:T(8,128)S(1)} %get-tuple-element.38), channel_id=1, source_target_pairs={{1,0},{0,1},{3,2},{2,3},{5,4},{4,5},{7,6},{6,7},{9,8},{8,9},{11,10... | collective-permute-start | bytes 73736 | tf_op jit(solution)/shard_map/line/ppermute | solution.py:364
  19.8 2.1 %collective-permute-start.6 = (f32[2,3,8,128]{3,2,1,0:T(8,128)S(1)}, f32[2,3,8,128]{3,2,1,0:T(8,128)S(1)}, u32[]{:S(2)}, u32[]{:S(2)}) collective-permute-start(f32[2,3,8,128]{3,2,1,0:T(8,128)S(1)} %get-tuple-element.39), channel_id=1, source_target_pairs={{3,0},{2,1},{1,2},{0,3},{7,4},{6,5},{5,6},{4,7},{11,8},{10,9},{9,1... | collective-permute-start | bytes 73736 | tf_op jit(solution)/shard_map/line/ppermute | solution.py:364
  21.9 0.6 %collective-permute-start.5 = (f32[2,3,8,128]{3,2,1,0:T(8,128)S(1)}, f32[2,3,8,128]{3,2,1,0:T(8,128)S(1)}, u32[]{:S(2)}, u32[]{:S(2)}) collective-permute-start(f32[2,3,8,128]{3,2,1,0:T(8,128)S(1)} %get-tuple-element.39), channel_id=1, source_target_pairs={{2,0},{3,1},{0,2},{1,3},{6,4},{7,5},{4,6},{5,7},{10,8},{11,9},{8,1... | collective-permute-start | bytes 73736 | tf_op jit(solution)/shard_map/line/ppermute | solution.py:364
  22.5 2.1 %local.1 = (f32[3,96,8,128]{3,2,1,0:T(8,128)}, f32[3,96,8,128]{3,2,1,0:T(8,128)S(1)}) custom-call(s32[8,128]{1,0:T(8,128)S(1)} %broadcast_in_dim.6.lengths.refs_0_, f32[4,5,104,128]{3,2,1,0:T(8,128)S(1)} %copy-done.3, f32[4,2,96,128]{3,2,1,0:T(8,128)S(1)} %copy-done.4, f32[3,96,8,128]{3,2,1,0:T(8,128)S(1)} %get-tuple-element.21.refs_3_.field, ...), custom_call_target="tpu_custom_call" | custom-call | flops 100000000 | bytes 6000000 | tf_op jit(solution)/shard_map/local/local/pallas_call | solution.py:369
  24.6 0.2 collective-permute-done.6.three
  24.8 2.4 %collective-permute-done.5.two = f32[2,3,8,128]{3,2,1,0:T(8,128)S(1)} collective-permute-done((f32[2,3,8,128]{3,2,1,0:T(8,128)S(1)}, f32[2,3,8,128]{3,2,1,0:T(8,128)S(1)}, u32[]{:S(2)}, u32[]{:S(2)}) %collective-permute-start.5) | collective-permute-done | bytes 24608 | tf_op jit(solution)/shard_map/line/ppermute | solution.py:364
  27.2 1.3 %last.1 = f32[3,96,8,128]{3,2,1,0:T(8,128)} custom-call(bf16[4,768,144]{2,1,0:T(8,128)(2,1)S(1)} %copy-done.2, f32[3,96,8,128]{3,2,1,0:T(8,128)S(1)} %get-tuple-element.37.local, f32[2,3,8,128]{3,2,1,0:T(8,128)S(1)} %collective-permute-done.4.one, f32[2,3,8,128]{3,2,1,0:T(8,128)S(1)} %collective-permute-done.5.two, ...), custom_call_target="tpu_custom_call" | custom-call | flops 10000000 | bytes 2400000 | tf_op jit(solution)/shard_map/last/last/pallas_call | solution.py:379
  (19 shorter events, 0.0 us)
Async XLA Ops:
  0.6 2.9 %copy-start.5 = (bf16[256,128]{1,0:T(8,128)(2,1)S(1)}, bf16[256,128]{1,0:T(8,128)(2,1)}, u32[]{:S(2)}) copy-start(bf16[256,128]{1,0:T(8,128)(2,1)} %constant.17.clone.refs_2_) | copy-start | bytes 196612
  0.6 2.9 %copy-start = (f32[4,4,96,128]{3,2,1,0:T(8,128)S(1)}, f32[4,4,96,128]{3,2,1,0:T(8,128)}, u32[]{:S(2)}) copy-start(f32[4,4,96,128]{3,2,1,0:T(8,128)} %constant.12.clone.refs_1_) | copy-start | bytes 2359300
  0.7 2.9 %copy-start.1 = (f32[96,8,128]{2,1,0:T(8,128)S(1)}, f32[96,8,128]{2,1,0:T(8,128)}, u32[]{:S(2)}) copy-start(f32[96,8,128]{2,1,0:T(8,128)} %refs_4_.3) | copy-start | bytes 1179652
  3.4 1.3 %collective-permute-start = (f32[9,8,128]{2,1,0:T(8,128)S(1)}, f32[9,8,128]{2,1,0:T(8,128)S(1)}, u32[]{:S(2)}, u32[]{:S(2)}) collective-permute-start(f32[9,8,128]{2,1,0:T(8,128)S(1)} %get-tuple-element.22), channel_id=1, source_target_pairs={{4,0},{0,4},{12,8},{8,12},{20,16},{16,20},{28,24},{24,28},{36,32},... | collective-permute-start | bytes 110600 | tf_op jit(solution)/shard_map/faces/ppermute | solution.py:327
  4.7 12.9 %copy-start.7 = (s32[8]{0:T(128)S(1)}, s32[8]{0:T(128)}, u32[]{:S(2)}) copy-start(s32[8]{0:T(128)} %param.14) | copy-start | bytes 100
  4.7 12.9 %copy-start.8 = (s32[8]{0:T(128)S(1)}, s32[8]{0:T(128)}, u32[]{:S(2)}) copy-start(s32[8]{0:T(128)} %param.15) | copy-start | bytes 100
  4.7 13.0 %copy-start.6 = (f32[4,4,3,128]{3,2,1,0:T(4,128)S(1)}, f32[4,4,3,128]{3,2,1,0:T(4,128)}, u32[]{:S(2)}) copy-start(f32[4,4,3,128]{3,2,1,0:T(4,128)} %constant.13.clone.packed) | copy-start | bytes 73732
  4.7 17.8 %copy-start.3 = (f32[4,5,104,128]{3,2,1,0:T(8,128)S(1)}, f32[4,5,104,128]{3,2,1,0:T(8,128)}, u32[]{:S(2)}) copy-start(f32[4,5,104,128]{3,2,1,0:T(8,128)} %constant.14.clone.forward) | copy-start | bytes 3194884
  4.8 17.8 %copy-start.4 = (f32[4,2,96,128]{3,2,1,0:T(8,128)S(1)}, f32[4,2,96,128]{3,2,1,0:T(8,128)}, u32[]{:S(2)}) copy-start(f32[4,2,96,128]{3,2,1,0:T(8,128)} %constant.15.clone.back) | copy-start | bytes 1179652
  4.8 8.9 %collective-permute-start.1 = (f32[18,8,128]{2,1,0:T(8,128)S(1)}, f32[18,8,128]{2,1,0:T(8,128)S(1)}, u32[]{:S(2)}, u32[]{:S(2)}) collective-permute-start(f32[18,8,128]{2,1,0:T(8,128)S(1)} %constant_dynamic-update-slice_fusion), channel_id=1, source_target_pairs={{136,0},{252,4},{144,8},{4,12},{152,16},{12,20},{160,24},{20,28},{... | collective-permute-start | bytes 221192 | tf_op jit(solution)/shard_map/faces/ppermute | solution.py:327
  11.7 5.9 %collective-permute-start.2 = (f32[18,8,128]{2,1,0:T(8,128)S(1)}, f32[18,8,128]{2,1,0:T(8,128)S(1)}, u32[]{:S(2)}, u32[]{:S(2)}) collective-permute-start(f32[18,8,128]{2,1,0:T(8,128)S(1)} %constant_dynamic-update-slice_fusion), channel_id=1, source_target_pairs={{128,0},{132,4},{136,8},{140,12},{144,16},{148,20},{152,24},{156,2... | collective-permute-start | bytes 221192 | tf_op jit(solution)/shard_map/faces/ppermute | solution.py:327
  13.7 3.9 %collective-permute-start.3 = (f32[18,8,128]{2,1,0:T(8,128)S(1)}, f32[18,8,128]{2,1,0:T(8,128)S(1)}, u32[]{:S(2)}, u32[]{:S(2)}) collective-permute-start(f32[18,8,128]{2,1,0:T(8,128)S(1)} %collective-permute-done.1.far), channel_id=1, source_target_pairs={{4,0},{0,4},{12,8},{8,12},{20,16},{16,20},{28,24},{24,28},{36,32},... | collective-permute-start | bytes 221192 | tf_op jit(solution)/shard_map/faces/ppermute | solution.py:327
  18.2 6.4 %collective-permute-start.4 = (f32[2,3,8,128]{3,2,1,0:T(8,128)S(1)}, f32[2,3,8,128]{3,2,1,0:T(8,128)S(1)}, u32[]{:S(2)}, u32[]{:S(2)}) collective-permute-start(f32[2,3,8,128]{3,2,1,0:T(8,128)S(1)} %get-tuple-element.38), channel_id=1, source_target_pairs={{1,0},{0,1},{3,2},{2,3},{5,4},{4,5},{7,6},{6,7},{9,8},{8,9},{11,10... | collective-permute-start | bytes 73736 | tf_op jit(solution)/shard_map/line/ppermute | solution.py:364
  19.8 5.0 %collective-permute-start.6 = (f32[2,3,8,128]{3,2,1,0:T(8,128)S(1)}, f32[2,3,8,128]{3,2,1,0:T(8,128)S(1)}, u32[]{:S(2)}, u32[]{:S(2)}) collective-permute-start(f32[2,3,8,128]{3,2,1,0:T(8,128)S(1)} %get-tuple-element.39), channel_id=1, source_target_pairs={{3,0},{2,1},{1,2},{0,3},{7,4},{6,5},{5,6},{4,7},{11,8},{10,9},{9,1... | collective-permute-start | bytes 73736 | tf_op jit(solution)/shard_map/line/ppermute | solution.py:364
  21.9 5.3 %collective-permute-start.5 = (f32[2,3,8,128]{3,2,1,0:T(8,128)S(1)}, f32[2,3,8,128]{3,2,1,0:T(8,128)S(1)}, u32[]{:S(2)}, u32[]{:S(2)}) collective-permute-start(f32[2,3,8,128]{3,2,1,0:T(8,128)S(1)} %get-tuple-element.39), channel_id=1, source_target_pairs={{2,0},{3,1},{0,2},{1,3},{6,4},{7,5},{4,6},{5,7},{10,8},{11,9},{8,1... | collective-permute-start | bytes 73736 | tf_op jit(solution)/shard_map/line/ppermute | solution.py:364
  22.5 4.7 %copy-start.2 = (bf16[4,768,144]{2,1,0:T(8,128)(2,1)S(1)}, bf16[4,768,144]{2,1,0:T(8,128)(2,1)}, u32[]{:S(2)}) copy-start(bf16[4,768,144]{2,1,0:T(8,128)(2,1)} %constant.16.clone.outer) | copy-start | bytes 2654212

commit v3 on v2

--- a/solution.py
+++ b/solution.py
@@ -102,18 +102,33 @@
     return lax.broadcasted_iota(jnp.int32, (SLOTS, LANES), axis)
 
 
-def is_live(lengths):
-    return jnp.where(iota(1) < lengths[...], 1.0, 0.0).astype(jnp.float32)
-
-
-def faces_kernel(lengths, field, faces, held, sems):
+def is_live(slots):
+    return jnp.where(iota(1) < slots[0], 1.0, 0.0).astype(jnp.float32)
+
+
+def by_slot(ref):
+    shape = (SLOTS, SLOTS)
+    own = lax.broadcasted_iota(jnp.int32, shape, 0) == lax.broadcasted_iota(jnp.int32, shape, 1)
+    spread = jnp.where(own, jnp.broadcast_to(ref[...], shape).astype(jnp.float32), 0.0)
+    return jnp.broadcast_to(jnp.sum(spread, axis=1, keepdims=True), (SLOTS, LANES)).astype(jnp.int32)
+
+
+def faces_kernel(lengths, connect, orient, field, faces, held, slots, near, link, turn, sems):
     lane = iota(1)
-    source = lengths[...] - HALO_LINES + jnp.minimum(lane % GROUP, HALO_LINES - 1)
     tiles = faces.shape[0] // 3
     pieces = [(c, pl.ds(h * PER_TILE, PER_TILE)) for c in range(3) for h in range(tiles)]
+    small = [
+        pltpu.make_async_copy(ref, to, sems.at[len(pieces) + k])
+        for k, (ref, to) in enumerate(((lengths, near), (connect, link), (orient, turn)))
+    ]
     copies = [pltpu.make_async_copy(field.at[at], held.at[at], sems.at[k]) for k, at in enumerate(pieces)]
-    for copy in copies:
+    for copy in small + copies:
         copy.start()
+    for copy in small:
+        copy.wait()
+    for k, ref in enumerate((near, link, turn)):
+        slots[k] = by_slot(ref)
+    source = slots[0] - HALO_LINES + jnp.minimum(lane % GROUP, HALO_LINES - 1)
     for k, copy in enumerate(copies):
         copy.wait()
         c, h = divmod(k, tiles)
@@ -127,11 +142,11 @@
 
 
 def interior_kernel(begin, more, *refs):
-    lengths, project, band, field, stretch, *refs = refs
+    slots, project, band, field, stretch, *refs = refs
     before, (rates, coef, edge) = (refs[0] if more else None), refs[-3:]
     part = lax.axis_index("line")
     lane = iota(1)
-    live = is_live(lengths)
+    live = is_live(slots)
     scale = live * (1.0 / 180.0)
     sums = [[None] * 3 for _ in range(4)]
     for h in range(edge.shape[0]):
@@ -160,7 +175,7 @@
             coef[r, c] = sums[r][c] + before[r, c] if more else sums[r][c]
 
 
-def ghost_kernel(connect, orient, packed, chip, far, pair, swap, edge_a, edge_b, coef, delta, near_out, far_out):
+def ghost_kernel(slots, packed, chip, far, pair, swap, edge_a, edge_b, coef, delta, near_out, far_out):
     part = lax.axis_index("line")
     blk = lax.axis_index("blk")
     count = lax.axis_size("blk")
@@ -168,17 +183,17 @@
     lane = iota(1)
     tiles = chip.shape[0]
     parts = tiles // 3
-    shift = (connect[...] // SLOTS - blk) & (count - 1)
-    src = connect[...] % SLOTS
+    shift = (slots[1] // SLOTS - blk) & (count - 1)
+    src = slots[1] % SLOTS
     is_one, is_two, is_three = shift == count // 2, shift == count // 2 + 1, shift == count // 2 + 2
     raw = []
     for k in range(tiles):
         pick = lambda v: jnp.take_along_axis(v, src, axis=0, mode="promise_in_bounds")
         row = pick(jnp.where(even, swap[k], chip[k]))
-        row = jnp.where(is_one, pick(pair[k]), row)
-        row = jnp.where(is_two, pick(jnp.where(even, pair[tiles + k], swap[k])), row)
+        row = jnp.where(is_one, pick(jnp.where(even, swap[2 * tiles + k], pair[k])), row)
+        row = jnp.where(is_two, pick(jnp.where(even, swap[tiles + k], swap[k])), row)
         raw.append(jnp.where(is_three, pick(jnp.where(even, far[k], swap[tiles + k])), row))
-    turn = orient[...]
+    turn = slots[2]
     cosine = jnp.where(turn == 0, 1.0, jnp.where(turn == 2, -1.0, 0.0))
     sine = jnp.where(turn == 1, 1.0, jnp.where(turn == 3, -1.0, 0.0))
     at = lane % GROUP
@@ -209,10 +224,10 @@
                 far_out[r - 2, c] = total
 
 
-def local_kernel(lengths, forward, back, field, rates_a, rates_b, delta, rates, local, full, held, sems):
+def local_kernel(slots, forward, back, field, rates_a, rates_b, delta, rates, local, full, held, sems):
     part = lax.axis_index("line")
     size = field.shape[1]
-    live = is_live(lengths)
+    live = is_live(slots)
     first = iota(1) < HALO_LINES
     tiles = size // PER_TILE
     zero = jnp.zeros((SLOTS, LANES), jnp.float32)
@@ -298,11 +313,10 @@
 HBM = pl.BlockSpec(memory_space=pltpu.HBM)
 
 
-def call(kernel, name, ins, outs, mib, flops, moved, scratch=(), out_specs=None):
-    shape = lambda s: jax.ShapeDtypeStruct(s, jnp.float32)
+def call(kernel, name, ins, outs, mib, flops, moved, scratch=(), out_specs=None, kinds={}):
     return pl.pallas_call(
         kernel,
-        out_shape=[shape(s) for s in outs],
+        out_shape=[jax.ShapeDtypeStruct(s, kinds.get(k, jnp.float32)) for k, s in enumerate(outs)],
         in_specs=ins,
         out_specs=out_specs or [VMEM] * len(outs),
         scratch_shapes=scratch,
@@ -320,28 +334,31 @@
     packed_tile = (tiles, SLOTS, LANES)
     sums = (4, 3, SLOTS, LANES)
     half = count // 2
-    lengths, connect, orient = (jnp.broadcast_to(v[:, None], (SLOTS, LANES)) for v in (lengths, connect, orient))
     dma = pltpu.SemaphoreType.DMA
 
     def over_blk(x, pairs):
         return lax.ppermute(x, "blk", pairs)
 
     core = [(d ^ 1, d) for d in range(count)]
-    pair = [((d + half) % count, d) for d in range(count)]
+    pair = [(d if d % 2 == 0 else (d + half) % count, d) for d in range(count)]
     far = [((d + half + 2) % count if d % 2 == 0 else (d - 2) % count, d) for d in range(count)]
 
-    field = pltpu.with_memory_space_constraint(field, pltpu.HBM)
+    lengths, connect, orient = (v[None] for v in (lengths, connect, orient))
+    field, lengths, connect, orient = (
+        pltpu.with_memory_space_constraint(v, pltpu.HBM) for v in (field, lengths, connect, orient)
+    )
     with jax.named_scope("faces"):
-        faces, held = call(
-            faces_kernel, "faces", [VMEM, HBM], [packed_tile, block], 8, 10**6, 1200000, scratch=[dma((tiles,))]
-        )(lengths, field)
+        faces, held, slots = call(
+            faces_kernel, "faces", [HBM] * 4, [packed_tile, block, (3, SLOTS, LANES)], 8, 10**6, 1200000,
+            scratch=[pltpu.VMEM((1, SLOTS), jnp.int32)] * 3 + [dma((tiles + 3,))], kinds={2: jnp.int32},
+        )(lengths, connect, orient, field)
         chip = over_blk(faces, core)
 
     def inside(begin, length, metric, *before):
         return call(
             functools.partial(interior_kernel, begin, bool(before)), "interior", [VMEM] * (5 + len(before)),
             [(3, length, SLOTS, LANES), sums, (length // PER_TILE, SLOTS, LANES)], 8, 10**7, 1500000,
-        )(lengths, project, band, held, metric, *before)
+        )(slots, project, band, held, metric, *before)
 
     with jax.named_scope("interior"):
         rates_a, coef, edge_a = inside(0, PER_TILE, stretch)
@@ -351,14 +368,15 @@
         from_far = over_blk(both, far)
         from_pair = over_blk(both, pair)
         from_far, coef = lax.optimization_barrier((from_far, coef))
-        swapped = over_blk(from_far, core)
+        middle = jnp.where(lax.axis_index("blk") % 2 == 0, from_far[tiles:], from_pair[:tiles])
+        swapped = over_blk(jnp.concatenate([from_far[:tiles], middle, from_pair[tiles:]], axis=0), core)
     with jax.named_scope("interior"):
         rates_b, coef, edge_b = inside(PER_TILE, size - PER_TILE, stretch, coef)
     with jax.named_scope("ghosts"):
         delta, near_sum, far_sum = call(
-            ghost_kernel, "ghosts", [VMEM] * 10,
+            ghost_kernel, "ghosts", [VMEM] * 9,
             [packed_tile, (2, 3, SLOTS, LANES), (2, 3, SLOTS, LANES)], 8, 10**6, 500000,
-        )(connect, orient, packed, chip, from_far, from_pair, swapped, edge_a, edge_b, coef)
+        )(slots, packed, chip, from_far, from_pair, swapped, edge_a, edge_b, coef)
 
     def over_line(x, k):
         return lax.ppermute(x, "line", [(e ^ k, e) for e in range(parts)])
@@ -374,7 +392,7 @@
                 pltpu.VMEM((3, size + 1, SLOTS, LANES), jnp.float32),
                 dma((size // PER_TILE,)),
             ],
-        )(lengths, forward, back, held, rates_a, rates_b, delta)
+        )(slots, forward, back, held, rates_a, rates_b, delta)
     with jax.named_scope("last"):
         (advanced,) = call(
             last_kernel, "last", [VMEM] * 5, [block], 8, 10**7, 2400000, out_specs=[HBM],

time: 28.6 us -> 25.7 us (0.90)
  the two profiles are of different devices: /device:TPU:8 before, /device:TPU:1 now
where the time goes in v3:
time: 25.7 us; the launch traced here: 25.5 us
  starting transfers between devices  11.9 us (46%)
  Pallas kernels  6.86 us (27%)
  waiting for transfers between devices  5.94 us (23%)
  between operations  0.79 us (3%)
    ppermute x4, starting transfers between devices, over_blk(): return lax.ppermute(x, 'blk', pairs)  8.13 us
    ppermute x4, waiting for transfers between devices, over_blk(): return lax.ppermute(x, 'blk', pairs)  4.53 us
    ppermute x3, starting transfers between devices, over_line(): return lax.ppermute(x, 'line', [(e ^ k, e) for e in range(parts)])  3.75 us
    pallas_call x1, Pallas kernels, shards(): call(local_kernel, 'local', [VMEM] * 7, [block, block], 12, 10 ** 8, 6000...  2.1 us
    pallas_call x1, Pallas kernels, shards(): call(faces_kernel, 'faces', [HBM] * 4, [packed_tile, block, (3, SLOTS, LA...  2.09 us
    ppermute x3, waiting for transfers between devices, over_line(): return lax.ppermute(x, 'line', [(e ^ k, e) for e in range(parts)])  1.41 us
    pallas_call x1, Pallas kernels, shards(): call(last_kernel, 'last', [VMEM] * 5, [block], 8, 10 ** 7, 2400000, out_s...  1.3 us
    pallas_call x2, Pallas kernels, inside(): call(functools.partial(interior_kernel, begin, bool(before)), 'interior',...  0.9 us
  transfers between devices with their start and end apart: 7, of which 4 were waited for; matrix products, arithmetic and copies ran while one was open for 0% of the time, Pallas kernels for 12%

profile of v3, /device:TPU:1, one launch (start us, length us, event | category | flops | bytes accessed | tf_op | source)
XLA Modules:
  0.0 25.5 jit_solution(9504137617075781904)
XLA Ops:
  0.6 0.0 copy-start.5
  0.6 0.0 copy-start
  0.7 2.1 %faces.1 = (f32[9,8,128]{2,1,0:T(8,128)S(1)}, f32[3,96,8,128]{3,2,1,0:T(8,128)S(1)}, s32[3,8,128]{2,1,0:T(8,128)S(1)}) custom-call(s32[1,8]{1,0:T(1,128)} %bitcast.3, s32[1,8]{1,0:T(1,128)} %bitcast.4, s32[1,8]{1,0:T(1,128)} %bitcast.5, f32[3,96,8,128]{3,2,1,0:T(8,128)} %field.1), custom_call_target="tpu_custom_call" | custom-call | flops 1000000 | bytes 1200000 | tf_op jit(solution)/shard_map/faces/faces/pallas_call | solution.py:351
  2.8 3.3 %collective-permute-start = (f32[9,8,128]{2,1,0:T(8,128)S(1)}, f32[9,8,128]{2,1,0:T(8,128)S(1)}, u32[]{:S(2)}, u32[]{:S(2)}) collective-permute-start(f32[9,8,128]{2,1,0:T(8,128)S(1)} %get-tuple-element.24), channel_id=1, source_target_pairs={{4,0},{0,4},{12,8},{8,12},{20,16},{16,20},{28,24},{24,28},{36,32},... | collective-permute-start | bytes 110600 | tf_op jit(solution)/shard_map/faces/ppermute | solution.py:340
  6.1 0.3 %interior.2 = (f32[3,32,8,128]{3,2,1,0:T(8,128)S(1)}, f32[4,3,8,128]{3,2,1,0:T(8,128)S(1)}, f32[1,8,128]{2,1,0:T(8,128)S(1)}) custom-call(s32[3,8,128]{2,1,0:T(8,128)S(1)} %get-tuple-element.22.refs_0_.slots, f32[4,4,96,128]{3,2,1,0:T(8,128)S(1)} %copy-done, bf16[256,128]{1,0:T(8,128)(2,1)S(1)} %copy-done.5, ...), custom_call_target="tpu_custom_call" | custom-call | flops 10000000 | bytes 1500000 | tf_op jit(solution)/shard_map/interior/interior/pallas_call | solution.py:358
  6.5 0.5 %collective-permute-done.chip = f32[9,8,128]{2,1,0:T(8,128)S(1)} collective-permute-done((f32[9,8,128]{2,1,0:T(8,128)S(1)}, f32[9,8,128]{2,1,0:T(8,128)S(1)}, u32[]{:S(2)}, u32[]{:S(2)}) %collective-permute-start) | collective-permute-done | bytes 36896 | tf_op jit(solution)/shard_map/faces/ppermute | solution.py:340
  7.0 0.0 collective-permute-start.1
  7.0 4.7 %collective-permute-start.2 = (f32[18,8,128]{2,1,0:T(8,128)S(1)}, f32[18,8,128]{2,1,0:T(8,128)S(1)}, u32[]{:S(2)}, u32[]{:S(2)}) collective-permute-start(f32[18,8,128]{2,1,0:T(8,128)S(1)} %constant_dynamic-update-slice_fusion), channel_id=1, source_target_pairs={{0,0},{132,4},{8,8},{140,12},{16,16},{148,20},{24,24},{156,28},{32... | collective-permute-start | bytes 221192 | tf_op jit(solution)/shard_map/faces/ppermute | solution.py:340
  11.7 3.3 %collective-permute-done.1.far = f32[18,8,128]{2,1,0:T(8,128)S(1)} collective-permute-done((f32[18,8,128]{2,1,0:T(8,128)S(1)}, f32[18,8,128]{2,1,0:T(8,128)S(1)}, u32[]{:S(2)}, u32[]{:S(2)}) %collective-permute-start.1) | collective-permute-done | bytes 73760 | tf_op jit(solution)/shard_map/faces/ppermute | solution.py:340
  15.0 0.0 copy-start.6
  15.0 0.0 copy-start.3
  15.1 0.0 copy-start.4
  15.1 0.1 collective-permute-start.3
  15.2 0.6 %interior.3 = (f32[3,64,8,128]{3,2,1,0:T(8,128)S(1)}, f32[4,3,8,128]{3,2,1,0:T(8,128)S(1)}, f32[2,8,128]{2,1,0:T(8,128)S(1)}) custom-call(s32[3,8,128]{2,1,0:T(8,128)S(1)} %get-tuple-element.22.refs_0_.slots, f32[4,4,96,128]{3,2,1,0:T(8,128)S(1)} %copy-done, bf16[256,128]{1,0:T(8,128)(2,1)S(1)} %copy-done.5, ...), custom_call_target="tpu_custom_call" | custom-call | flops 10000000 | bytes 1500000 | tf_op jit(solution)/shard_map/interior/interior/pallas_call | solution.py:358
  15.7 0.7 %collective-permute-done.3.swap = f32[27,8,128]{2,1,0:T(8,128)S(1)} collective-permute-done((f32[27,8,128]{2,1,0:T(8,128)S(1)}, f32[27,8,128]{2,1,0:T(8,128)S(1)}, u32[]{:S(2)}, u32[]{:S(2)}) %collective-permute-start.3) | collective-permute-done | bytes 110624 | tf_op jit(solution)/shard_map/faces/ppermute | solution.py:340
  16.5 0.5 %ghosts.1 = (f32[9,8,128]{2,1,0:T(8,128)S(1)}, f32[2,3,8,128]{3,2,1,0:T(8,128)S(1)}, f32[2,3,8,128]{3,2,1,0:T(8,128)S(1)}) custom-call(s32[3,8,128]{2,1,0:T(8,128)S(1)} %get-tuple-element.22.refs_0_.slots, f32[4,4,3,128]{3,2,1,0:T(4,128)S(1)} %copy-done.6, f32[9,8,128]{2,1,0:T(8,128)S(1)} %collective-permute-done.chip, ...), custom_call_target="tpu_custom_call" | custom-call | flops 1000000 | bytes 500000 | tf_op jit(solution)/shard_map/ghosts/ghosts/pallas_call | solution.py:376
  16.9 1.3 %collective-permute-start.4 = (f32[2,3,8,128]{3,2,1,0:T(8,128)S(1)}, f32[2,3,8,128]{3,2,1,0:T(8,128)S(1)}, u32[]{:S(2)}, u32[]{:S(2)}) collective-permute-start(f32[2,3,8,128]{3,2,1,0:T(8,128)S(1)} %get-tuple-element.40), channel_id=1, source_target_pairs={{1,0},{0,1},{3,2},{2,3},{5,4},{4,5},{7,6},{6,7},{9,8},{8,9},{11,10... | collective-permute-start | bytes 73736 | tf_op jit(solution)/shard_map/line/ppermute | solution.py:382
  18.2 1.8 %collective-permute-start.6 = (f32[2,3,8,128]{3,2,1,0:T(8,128)S(1)}, f32[2,3,8,128]{3,2,1,0:T(8,128)S(1)}, u32[]{:S(2)}, u32[]{:S(2)}) collective-permute-start(f32[2,3,8,128]{3,2,1,0:T(8,128)S(1)} %get-tuple-element.41), channel_id=1, source_target_pairs={{3,0},{2,1},{1,2},{0,3},{7,4},{6,5},{5,6},{4,7},{11,8},{10,9},{9,1... | collective-permute-start | bytes 73736 | tf_op jit(solution)/shard_map/line/ppermute | solution.py:382
  20.1 0.6 %collective-permute-start.5 = (f32[2,3,8,128]{3,2,1,0:T(8,128)S(1)}, f32[2,3,8,128]{3,2,1,0:T(8,128)S(1)}, u32[]{:S(2)}, u32[]{:S(2)}) collective-permute-start(f32[2,3,8,128]{3,2,1,0:T(8,128)S(1)} %get-tuple-element.41), channel_id=1, source_target_pairs={{2,0},{3,1},{0,2},{1,3},{6,4},{7,5},{4,6},{5,7},{10,8},{11,9},{8,1... | collective-permute-start | bytes 73736 | tf_op jit(solution)/shard_map/line/ppermute | solution.py:382
  20.7 2.1 %local.1 = (f32[3,96,8,128]{3,2,1,0:T(8,128)}, f32[3,96,8,128]{3,2,1,0:T(8,128)S(1)}) custom-call(s32[3,8,128]{2,1,0:T(8,128)S(1)} %get-tuple-element.22.refs_0_.slots, f32[4,5,104,128]{3,2,1,0:T(8,128)S(1)} %copy-done.3, f32[4,2,96,128]{3,2,1,0:T(8,128)S(1)} %copy-done.4, f32[3,96,8,128]{3,2,1,0:T(8,128)S(1)} %get-tuple-element.23.refs_3_.field, ...), custom_call_target="tpu_custom_call" | custom-call | flops 100000000 | bytes 6000000 | tf_op jit(solution)/shard_map/local/local/pallas_call | solution.py:387
  22.8 0.0 collective-permute-done.4.one
  22.8 0.0 collective-permute-done.6.three
  22.8 1.4 %collective-permute-done.5.two = f32[2,3,8,128]{3,2,1,0:T(8,128)S(1)} collective-permute-done((f32[2,3,8,128]{3,2,1,0:T(8,128)S(1)}, f32[2,3,8,128]{3,2,1,0:T(8,128)S(1)}, u32[]{:S(2)}, u32[]{:S(2)}) %collective-permute-start.5) | collective-permute-done | bytes 24608 | tf_op jit(solution)/shard_map/line/ppermute | solution.py:382
  24.2 1.3 %last.1 = f32[3,96,8,128]{3,2,1,0:T(8,128)} custom-call(bf16[4,768,144]{2,1,0:T(8,128)(2,1)S(1)} %copy-done.2, f32[3,96,8,128]{3,2,1,0:T(8,128)S(1)} %get-tuple-element.39.local, f32[2,3,8,128]{3,2,1,0:T(8,128)S(1)} %collective-permute-done.4.one, f32[2,3,8,128]{3,2,1,0:T(8,128)S(1)} %collective-permute-done.5.two, ...), custom_call_target="tpu_custom_call" | custom-call | flops 10000000 | bytes 2400000 | tf_op jit(solution)/shard_map/last/last/pallas_call | solution.py:397
  (14 shorter events, 0.0 us)
Async XLA Ops:
  0.6 5.5 %copy-start.5 = (bf16[256,128]{1,0:T(8,128)(2,1)S(1)}, bf16[256,128]{1,0:T(8,128)(2,1)}, u32[]{:S(2)}) copy-start(bf16[256,128]{1,0:T(8,128)(2,1)} %constant.37.clone.refs_2_) | copy-start | bytes 196612
  0.6 5.5 %copy-start = (f32[4,4,96,128]{3,2,1,0:T(8,128)S(1)}, f32[4,4,96,128]{3,2,1,0:T(8,128)}, u32[]{:S(2)}) copy-start(f32[4,4,96,128]{3,2,1,0:T(8,128)} %constant.32.clone.refs_1_) | copy-start | bytes 2359300
  0.7 5.4 %copy-start.1 = (f32[96,8,128]{2,1,0:T(8,128)S(1)}, f32[96,8,128]{2,1,0:T(8,128)}, u32[]{:S(2)}) copy-start(f32[96,8,128]{2,1,0:T(8,128)} %refs_4_.3) | copy-start | bytes 1179652
  2.8 4.2 %collective-permute-start = (f32[9,8,128]{2,1,0:T(8,128)S(1)}, f32[9,8,128]{2,1,0:T(8,128)S(1)}, u32[]{:S(2)}, u32[]{:S(2)}) collective-permute-start(f32[9,8,128]{2,1,0:T(8,128)S(1)} %get-tuple-element.24), channel_id=1, source_target_pairs={{4,0},{0,4},{12,8},{8,12},{20,16},{16,20},{28,24},{24,28},{36,32},... | collective-permute-start | bytes 110600 | tf_op jit(solution)/shard_map/faces/ppermute | solution.py:340
  7.0 8.0 %collective-permute-start.1 = (f32[18,8,128]{2,1,0:T(8,128)S(1)}, f32[18,8,128]{2,1,0:T(8,128)S(1)}, u32[]{:S(2)}, u32[]{:S(2)}) collective-permute-start(f32[18,8,128]{2,1,0:T(8,128)S(1)} %constant_dynamic-update-slice_fusion), channel_id=1, source_target_pairs={{136,0},{252,4},{144,8},{4,12},{152,16},{12,20},{160,24},{20,28},{... | collective-permute-start | bytes 221192 | tf_op jit(solution)/shard_map/faces/ppermute | solution.py:340
  7.0 8.0 %collective-permute-start.2 = (f32[18,8,128]{2,1,0:T(8,128)S(1)}, f32[18,8,128]{2,1,0:T(8,128)S(1)}, u32[]{:S(2)}, u32[]{:S(2)}) collective-permute-start(f32[18,8,128]{2,1,0:T(8,128)S(1)} %constant_dynamic-update-slice_fusion), channel_id=1, source_target_pairs={{0,0},{132,4},{8,8},{140,12},{16,16},{148,20},{24,24},{156,28},{32... | collective-permute-start | bytes 221192 | tf_op jit(solution)/shard_map/faces/ppermute | solution.py:340
  15.0 1.4 %copy-start.6 = (f32[4,4,3,128]{3,2,1,0:T(4,128)S(1)}, f32[4,4,3,128]{3,2,1,0:T(4,128)}, u32[]{:S(2)}) copy-start(f32[4,4,3,128]{3,2,1,0:T(4,128)} %constant.33.clone.packed) | copy-start | bytes 73732
  15.0 5.7 %copy-start.3 = (f32[4,5,104,128]{3,2,1,0:T(8,128)S(1)}, f32[4,5,104,128]{3,2,1,0:T(8,128)}, u32[]{:S(2)}) copy-start(f32[4,5,104,128]{3,2,1,0:T(8,128)} %constant.34.clone.forward) | copy-start | bytes 3194884
  15.1 5.6 %copy-start.4 = (f32[4,2,96,128]{3,2,1,0:T(8,128)S(1)}, f32[4,2,96,128]{3,2,1,0:T(8,128)}, u32[]{:S(2)}) copy-start(f32[4,2,96,128]{3,2,1,0:T(8,128)} %constant.35.clone.back) | copy-start | bytes 1179652
  15.1 1.4 %collective-permute-start.3 = (f32[27,8,128]{2,1,0:T(8,128)S(1)}, f32[27,8,128]{2,1,0:T(8,128)S(1)}, u32[]{:S(2)}, u32[]{:S(2)}) collective-permute-start(f32[27,8,128]{2,1,0:T(8,128)S(1)} %pad_maximum_fusion), channel_id=1, source_target_pairs={{4,0},{0,4},{12,8},{8,12},{20,16},{16,20},{28,24},{24,28},{36,32},... | collective-permute-start | bytes 331784 | tf_op jit(solution)/shard_map/faces/ppermute | solution.py:340
  16.9 5.9 %collective-permute-start.4 = (f32[2,3,8,128]{3,2,1,0:T(8,128)S(1)}, f32[2,3,8,128]{3,2,1,0:T(8,128)S(1)}, u32[]{:S(2)}, u32[]{:S(2)}) collective-permute-start(f32[2,3,8,128]{3,2,1,0:T(8,128)S(1)} %get-tuple-element.40), channel_id=1, source_target_pairs={{1,0},{0,1},{3,2},{2,3},{5,4},{4,5},{7,6},{6,7},{9,8},{8,9},{11,10... | collective-permute-start | bytes 73736 | tf_op jit(solution)/shard_map/line/ppermute | solution.py:382
  18.2 4.6 %collective-permute-start.6 = (f32[2,3,8,128]{3,2,1,0:T(8,128)S(1)}, f32[2,3,8,128]{3,2,1,0:T(8,128)S(1)}, u32[]{:S(2)}, u32[]{:S(2)}) collective-permute-start(f32[2,3,8,128]{3,2,1,0:T(8,128)S(1)} %get-tuple-element.41), channel_id=1, source_target_pairs={{3,0},{2,1},{1,2},{0,3},{7,4},{6,5},{5,6},{4,7},{11,8},{10,9},{9,1... | collective-permute-start | bytes 73736 | tf_op jit(solution)/shard_map/line/ppermute | solution.py:382
  20.1 4.2 %collective-permute-start.5 = (f32[2,3,8,128]{3,2,1,0:T(8,128)S(1)}, f32[2,3,8,128]{3,2,1,0:T(8,128)S(1)}, u32[]{:S(2)}, u32[]{:S(2)}) collective-permute-start(f32[2,3,8,128]{3,2,1,0:T(8,128)S(1)} %get-tuple-element.41), channel_id=1, source_target_pairs={{2,0},{3,1},{0,2},{1,3},{6,4},{7,5},{4,6},{5,7},{10,8},{11,9},{8,1... | collective-permute-start | bytes 73736 | tf_op jit(solution)/shard_map/line/ppermute | solution.py:382
  20.7 3.5 %copy-start.2 = (bf16[4,768,144]{2,1,0:T(8,128)(2,1)S(1)}, bf16[4,768,144]{2,1,0:T(8,128)(2,1)}, u32[]{:S(2)}) copy-start(bf16[4,768,144]{2,1,0:T(8,128)(2,1)} %constant.36.clone.outer) | copy-start | bytes 2654212

commit v4 on v3

--- a/solution.py
+++ b/solution.py
@@ -175,7 +175,7 @@
             coef[r, c] = sums[r][c] + before[r, c] if more else sums[r][c]
 
 
-def ghost_kernel(slots, packed, chip, far, pair, swap, edge_a, edge_b, coef, delta, near_out, far_out):
+def ghost_kernel(slots, packed, chip, far, pair, swap, edge_a, edge_b, coef, delta, near_out, far_out, far_too):
     part = lax.axis_index("line")
     blk = lax.axis_index("blk")
     count = lax.axis_size("blk")
@@ -222,6 +222,7 @@
                 near_out[r, c] = total
             else:
                 far_out[r - 2, c] = total
+                far_too[r - 2, c] = total
 
 
 def local_kernel(slots, forward, back, field, rates_a, rates_b, delta, rates, local, full, held, sems):
@@ -285,7 +286,7 @@
         copy.wait()
 
 
-def last_kernel(outer, local, one, two, three, advanced, full, sems):
+def last_kernel(outer, local, two, three, one, advanced, full, sems):
     part = lax.axis_index("line")
     size = local.shape[1]
     got = jnp.concatenate(
@@ -373,16 +374,16 @@
     with jax.named_scope("interior"):
         rates_b, coef, edge_b = inside(PER_TILE, size - PER_TILE, stretch, coef)
     with jax.named_scope("ghosts"):
-        delta, near_sum, far_sum = call(
+        delta, near_sum, far_sum, far_again = call(
             ghost_kernel, "ghosts", [VMEM] * 9,
-            [packed_tile, (2, 3, SLOTS, LANES), (2, 3, SLOTS, LANES)], 8, 10**6, 500000,
+            [packed_tile] + [(2, 3, SLOTS, LANES)] * 3, 8, 10**6, 500000,
         )(slots, packed, chip, from_far, from_pair, swapped, edge_a, edge_b, coef)
 
     def over_line(x, k):
         return lax.ppermute(x, "line", [(e ^ k, e) for e in range(parts)])
 
     with jax.named_scope("line"):
-        got = [over_line(near_sum, 1), over_line(far_sum, 2), over_line(far_sum, 3)]
+        got = [over_line(near_sum, 1), over_line(far_sum, 2), over_line(far_again, 3)]
     with jax.named_scope("local"):
         rates, local = call(
             local_kernel, "local", [VMEM] * 7, [block, block], 12, 10**8, 6000000,
@@ -397,7 +398,7 @@
         (advanced,) = call(
             last_kernel, "last", [VMEM] * 5, [block], 8, 10**7, 2400000, out_specs=[HBM],
             scratch=[pltpu.VMEM(block, jnp.float32), dma((tiles,))],
-        )(outer, local, *got)
+        )(outer, local, got[1], got[2], got[0])
     return rates, advanced
 
 

time: 25.7 us -> 25.1 us (0.977)
  waiting for transfers between devices: 5.94 us -> 5.41 us
    ppermute x3, waiting for transfers between devices: 1.41 us -> 0.88 us  [over_line(): return lax.ppermute(x, 'line', [(e ^ k, e) for e in range(parts)])]
where the time goes in v4:
time: 25.1 us; the launch traced here: 25 us
  starting transfers between devices  11.8 us (47%)
  Pallas kernels  6.86 us (27%)
  waiting for transfers between devices  5.41 us (22%)
  between operations  0.8 us (3%)
    ppermute x4, starting transfers between devices, over_blk(): return lax.ppermute(x, 'blk', pairs)  8.13 us
    ppermute x4, waiting for transfers between devices, over_blk(): return lax.ppermute(x, 'blk', pairs)  4.53 us
    ppermute x3, starting transfers between devices, over_line(): return lax.ppermute(x, 'line', [(e ^ k, e) for e in range(parts)])  3.69 us
    pallas_call x1, Pallas kernels, shards(): call(local_kernel, 'local', [VMEM] * 7, [block, block], 12, 10 ** 8, 6000...  2.11 us
    pallas_call x1, Pallas kernels, shards(): call(faces_kernel, 'faces', [HBM] * 4, [packed_tile, block, (3, SLOTS, LA...  2.09 us
    pallas_call x1, Pallas kernels, shards(): call(last_kernel, 'last', [VMEM] * 5, [block], 8, 10 ** 7, 2400000, out_s...  1.3 us
    pallas_call x2, Pallas kernels, inside(): call(functools.partial(interior_kernel, begin, bool(before)), 'interior',...  0.9 us
    ppermute x3, waiting for transfers between devices, over_line(): return lax.ppermute(x, 'line', [(e ^ k, e) for e in range(parts)])  0.88 us
  transfers between devices with their start and end apart: 7, of which 4 were waited for; matrix products, arithmetic and copies ran while one was open for 0% of the time, Pallas kernels for 12%

profile of v4, /device:TPU:1, one launch (start us, length us, event | category | flops | bytes accessed | tf_op | source)
XLA Modules:
  0.0 25.0 jit_solution(13539871548991817388)
XLA Ops:
  0.6 0.0 copy-start.5
  0.6 0.0 copy-start
  0.7 2.1 %faces.1 = (f32[9,8,128]{2,1,0:T(8,128)S(1)}, f32[3,96,8,128]{3,2,1,0:T(8,128)S(1)}, s32[3,8,128]{2,1,0:T(8,128)S(1)}) custom-call(s32[1,8]{1,0:T(1,128)} %bitcast.3, s32[1,8]{1,0:T(1,128)} %bitcast.4, s32[1,8]{1,0:T(1,128)} %bitcast.5, f32[3,96,8,128]{3,2,1,0:T(8,128)} %field.1), custom_call_target="tpu_custom_call" | custom-call | flops 1000000 | bytes 1200000 | tf_op jit(solution)/shard_map/faces/faces/pallas_call | solution.py:352
  2.8 3.3 %collective-permute-start = (f32[9,8,128]{2,1,0:T(8,128)S(1)}, f32[9,8,128]{2,1,0:T(8,128)S(1)}, u32[]{:S(2)}, u32[]{:S(2)}) collective-permute-start(f32[9,8,128]{2,1,0:T(8,128)S(1)} %get-tuple-element.25), channel_id=1, source_target_pairs={{4,0},{0,4},{12,8},{8,12},{20,16},{16,20},{28,24},{24,28},{36,32},... | collective-permute-start | bytes 110600 | tf_op jit(solution)/shard_map/faces/ppermute | solution.py:341
  6.1 0.3 %interior.2 = (f32[3,32,8,128]{3,2,1,0:T(8,128)S(1)}, f32[4,3,8,128]{3,2,1,0:T(8,128)S(1)}, f32[1,8,128]{2,1,0:T(8,128)S(1)}) custom-call(s32[3,8,128]{2,1,0:T(8,128)S(1)} %get-tuple-element.23.refs_0_.slots, f32[4,4,96,128]{3,2,1,0:T(8,128)S(1)} %copy-done, bf16[256,128]{1,0:T(8,128)(2,1)S(1)} %copy-done.5, ...), custom_call_target="tpu_custom_call" | custom-call | flops 10000000 | bytes 1500000 | tf_op jit(solution)/shard_map/interior/interior/pallas_call | solution.py:359
  6.5 0.5 %collective-permute-done.chip = f32[9,8,128]{2,1,0:T(8,128)S(1)} collective-permute-done((f32[9,8,128]{2,1,0:T(8,128)S(1)}, f32[9,8,128]{2,1,0:T(8,128)S(1)}, u32[]{:S(2)}, u32[]{:S(2)}) %collective-permute-start) | collective-permute-done | bytes 36896 | tf_op jit(solution)/shard_map/faces/ppermute | solution.py:341
  7.0 0.0 collective-permute-start.1
  7.0 4.7 %collective-permute-start.2 = (f32[18,8,128]{2,1,0:T(8,128)S(1)}, f32[18,8,128]{2,1,0:T(8,128)S(1)}, u32[]{:S(2)}, u32[]{:S(2)}) collective-permute-start(f32[18,8,128]{2,1,0:T(8,128)S(1)} %constant_dynamic-update-slice_fusion), channel_id=1, source_target_pairs={{0,0},{132,4},{8,8},{140,12},{16,16},{148,20},{24,24},{156,28},{32... | collective-permute-start | bytes 221192 | tf_op jit(solution)/shard_map/faces/ppermute | solution.py:341
  11.7 3.3 %collective-permute-done.1.far = f32[18,8,128]{2,1,0:T(8,128)S(1)} collective-permute-done((f32[18,8,128]{2,1,0:T(8,128)S(1)}, f32[18,8,128]{2,1,0:T(8,128)S(1)}, u32[]{:S(2)}, u32[]{:S(2)}) %collective-permute-start.1) | collective-permute-done | bytes 73760 | tf_op jit(solution)/shard_map/faces/ppermute | solution.py:341
  15.0 0.0 collective-permute-done.2.pair
  15.0 0.0 copy-start.6
  15.0 0.0 copy-start.3
  15.1 0.0 copy-start.4
  15.1 0.1 collective-permute-start.3
  15.2 0.6 %interior.3 = (f32[3,64,8,128]{3,2,1,0:T(8,128)S(1)}, f32[4,3,8,128]{3,2,1,0:T(8,128)S(1)}, f32[2,8,128]{2,1,0:T(8,128)S(1)}) custom-call(s32[3,8,128]{2,1,0:T(8,128)S(1)} %get-tuple-element.23.refs_0_.slots, f32[4,4,96,128]{3,2,1,0:T(8,128)S(1)} %copy-done, bf16[256,128]{1,0:T(8,128)(2,1)S(1)} %copy-done.5, ...), custom_call_target="tpu_custom_call" | custom-call | flops 10000000 | bytes 1500000 | tf_op jit(solution)/shard_map/interior/interior/pallas_call | solution.py:359
  15.7 0.7 %collective-permute-done.3.swap = f32[27,8,128]{2,1,0:T(8,128)S(1)} collective-permute-done((f32[27,8,128]{2,1,0:T(8,128)S(1)}, f32[27,8,128]{2,1,0:T(8,128)S(1)}, u32[]{:S(2)}, u32[]{:S(2)}) %collective-permute-start.3) | collective-permute-done | bytes 110624 | tf_op jit(solution)/shard_map/faces/ppermute | solution.py:341
  16.5 0.5 %ghosts.1 = (f32[9,8,128]{2,1,0:T(8,128)S(1)}, f32[2,3,8,128]{3,2,1,0:T(8,128)S(1)}, f32[2,3,8,128]{3,2,1,0:T(8,128)S(1)}, f32[2,3,8,128]{3,2,1,0:T(8,128)S(1)}) custom-call(s32[3,8,128]{2,1,0:T(8,128)S(1)} %get-tuple-element.23.refs_0_.slots, f32[4,4,3,128]{3,2,1,0:T(4,128)S(1)} %copy-done.6, f32[9,8,128]{2,1,0:T(8,128)S(1)} %collective-permute-done.chip, ...), custom_call_target="tpu_custom_call" | custom-call | flops 1000000 | bytes 500000 | tf_op jit(solution)/shard_map/ghosts/ghosts/pallas_call | solution.py:377
  16.9 2.8 %collective-permute-start.4 = (f32[2,3,8,128]{3,2,1,0:T(8,128)S(1)}, f32[2,3,8,128]{3,2,1,0:T(8,128)S(1)}, u32[]{:S(2)}, u32[]{:S(2)}) collective-permute-start(f32[2,3,8,128]{3,2,1,0:T(8,128)S(1)} %get-tuple-element.41), channel_id=1, source_target_pairs={{2,0},{3,1},{0,2},{1,3},{6,4},{7,5},{4,6},{5,7},{10,8},{11,9},{8,1... | collective-permute-start | bytes 73736 | tf_op jit(solution)/shard_map/line/ppermute | solution.py:383
  19.8 0.9 %collective-permute-start.5 = (f32[2,3,8,128]{3,2,1,0:T(8,128)S(1)}, f32[2,3,8,128]{3,2,1,0:T(8,128)S(1)}, u32[]{:S(2)}, u32[]{:S(2)}) collective-permute-start(f32[2,3,8,128]{3,2,1,0:T(8,128)S(1)} %get-tuple-element.42), channel_id=1, source_target_pairs={{3,0},{2,1},{1,2},{0,3},{7,4},{6,5},{5,6},{4,7},{11,8},{10,9},{9,1... | collective-permute-start | bytes 73736 | tf_op jit(solution)/shard_map/line/ppermute | solution.py:383
  20.6 0.0 copy-start.2
  20.7 2.1 %local.1 = (f32[3,96,8,128]{3,2,1,0:T(8,128)}, f32[3,96,8,128]{3,2,1,0:T(8,128)S(1)}) custom-call(s32[3,8,128]{2,1,0:T(8,128)S(1)} %get-tuple-element.23.refs_0_.slots, f32[4,5,104,128]{3,2,1,0:T(8,128)S(1)} %copy-done.3, f32[4,2,96,128]{3,2,1,0:T(8,128)S(1)} %copy-done.4, f32[3,96,8,128]{3,2,1,0:T(8,128)S(1)} %get-tuple-element.24.refs_3_.field, ...), custom_call_target="tpu_custom_call" | custom-call | flops 100000000 | bytes 6000000 | tf_op jit(solution)/shard_map/local/local/pallas_call | solution.py:388
  22.8 0.0 collective-permute-done.4.two
  22.8 0.9 %collective-permute-done.5.three = f32[2,3,8,128]{3,2,1,0:T(8,128)S(1)} collective-permute-done((f32[2,3,8,128]{3,2,1,0:T(8,128)S(1)}, f32[2,3,8,128]{3,2,1,0:T(8,128)S(1)}, u32[]{:S(2)}, u32[]{:S(2)}) %collective-permute-start.5) | collective-permute-done | bytes 24608 | tf_op jit(solution)/shard_map/line/ppermute | solution.py:383
  23.7 1.3 %last.1 = f32[3,96,8,128]{3,2,1,0:T(8,128)} custom-call(bf16[4,768,144]{2,1,0:T(8,128)(2,1)S(1)} %copy-done.2, f32[3,96,8,128]{3,2,1,0:T(8,128)S(1)} %get-tuple-element.40.local, f32[2,3,8,128]{3,2,1,0:T(8,128)S(1)} %collective-permute-done.4.two, f32[2,3,8,128]{3,2,1,0:T(8,128)S(1)} %collective-permute-done.5.three, ...), custom_call_target="tpu_custom_call" | custom-call | flops 10000000 | bytes 2400000 | tf_op jit(solution)/shard_map/last/last/pallas_call | solution.py:398
  (14 shorter events, 0.1 us)
Async XLA Ops:
  0.6 5.5 %copy-start.5 = (bf16[256,128]{1,0:T(8,128)(2,1)S(1)}, bf16[256,128]{1,0:T(8,128)(2,1)}, u32[]{:S(2)}) copy-start(bf16[256,128]{1,0:T(8,128)(2,1)} %constant.37.clone.refs_2_) | copy-start | bytes 196612
  0.6 5.5 %copy-start = (f32[4,4,96,128]{3,2,1,0:T(8,128)S(1)}, f32[4,4,96,128]{3,2,1,0:T(8,128)}, u32[]{:S(2)}) copy-start(f32[4,4,96,128]{3,2,1,0:T(8,128)} %constant.32.clone.refs_1_) | copy-start | bytes 2359300
  0.7 5.4 %copy-start.1 = (f32[96,8,128]{2,1,0:T(8,128)S(1)}, f32[96,8,128]{2,1,0:T(8,128)}, u32[]{:S(2)}) copy-start(f32[96,8,128]{2,1,0:T(8,128)} %refs_4_.3) | copy-start | bytes 1179652
  2.8 4.2 %collective-permute-start = (f32[9,8,128]{2,1,0:T(8,128)S(1)}, f32[9,8,128]{2,1,0:T(8,128)S(1)}, u32[]{:S(2)}, u32[]{:S(2)}) collective-permute-start(f32[9,8,128]{2,1,0:T(8,128)S(1)} %get-tuple-element.25), channel_id=1, source_target_pairs={{4,0},{0,4},{12,8},{8,12},{20,16},{16,20},{28,24},{24,28},{36,32},... | collective-permute-start | bytes 110600 | tf_op jit(solution)/shard_map/faces/ppermute | solution.py:341
  7.0 8.0 %collective-permute-start.1 = (f32[18,8,128]{2,1,0:T(8,128)S(1)}, f32[18,8,128]{2,1,0:T(8,128)S(1)}, u32[]{:S(2)}, u32[]{:S(2)}) collective-permute-start(f32[18,8,128]{2,1,0:T(8,128)S(1)} %constant_dynamic-update-slice_fusion), channel_id=1, source_target_pairs={{136,0},{252,4},{144,8},{4,12},{152,16},{12,20},{160,24},{20,28},{... | collective-permute-start | bytes 221192 | tf_op jit(solution)/shard_map/faces/ppermute | solution.py:341
  7.0 8.0 %collective-permute-start.2 = (f32[18,8,128]{2,1,0:T(8,128)S(1)}, f32[18,8,128]{2,1,0:T(8,128)S(1)}, u32[]{:S(2)}, u32[]{:S(2)}) collective-permute-start(f32[18,8,128]{2,1,0:T(8,128)S(1)} %constant_dynamic-update-slice_fusion), channel_id=1, source_target_pairs={{0,0},{132,4},{8,8},{140,12},{16,16},{148,20},{24,24},{156,28},{32... | collective-permute-start | bytes 221192 | tf_op jit(solution)/shard_map/faces/ppermute | solution.py:341
  15.0 1.4 %copy-start.6 = (f32[4,4,3,128]{3,2,1,0:T(4,128)S(1)}, f32[4,4,3,128]{3,2,1,0:T(4,128)}, u32[]{:S(2)}) copy-start(f32[4,4,3,128]{3,2,1,0:T(4,128)} %constant.33.clone.packed) | copy-start | bytes 73732
  15.0 5.6 %copy-start.3 = (f32[4,5,104,128]{3,2,1,0:T(8,128)S(1)}, f32[4,5,104,128]{3,2,1,0:T(8,128)}, u32[]{:S(2)}) copy-start(f32[4,5,104,128]{3,2,1,0:T(8,128)} %constant.34.clone.forward) | copy-start | bytes 3194884
  15.1 5.6 %copy-start.4 = (f32[4,2,96,128]{3,2,1,0:T(8,128)S(1)}, f32[4,2,96,128]{3,2,1,0:T(8,128)}, u32[]{:S(2)}) copy-start(f32[4,2,96,128]{3,2,1,0:T(8,128)} %constant.35.clone.back) | copy-start | bytes 1179652
  15.1 1.4 %collective-permute-start.3 = (f32[27,8,128]{2,1,0:T(8,128)S(1)}, f32[27,8,128]{2,1,0:T(8,128)S(1)}, u32[]{:S(2)}, u32[]{:S(2)}) collective-permute-start(f32[27,8,128]{2,1,0:T(8,128)S(1)} %pad_maximum_fusion), channel_id=1, source_target_pairs={{4,0},{0,4},{12,8},{8,12},{20,16},{16,20},{28,24},{24,28},{36,32},... | collective-permute-start | bytes 331784 | tf_op jit(solution)/shard_map/faces/ppermute | solution.py:341
  16.9 5.8 %collective-permute-start.4 = (f32[2,3,8,128]{3,2,1,0:T(8,128)S(1)}, f32[2,3,8,128]{3,2,1,0:T(8,128)S(1)}, u32[]{:S(2)}, u32[]{:S(2)}) collective-permute-start(f32[2,3,8,128]{3,2,1,0:T(8,128)S(1)} %get-tuple-element.41), channel_id=1, source_target_pairs={{2,0},{3,1},{0,2},{1,3},{6,4},{7,5},{4,6},{5,7},{10,8},{11,9},{8,1... | collective-permute-start | bytes 73736 | tf_op jit(solution)/shard_map/line/ppermute | solution.py:383
  19.8 3.9 %collective-permute-start.5 = (f32[2,3,8,128]{3,2,1,0:T(8,128)S(1)}, f32[2,3,8,128]{3,2,1,0:T(8,128)S(1)}, u32[]{:S(2)}, u32[]{:S(2)}) collective-permute-start(f32[2,3,8,128]{3,2,1,0:T(8,128)S(1)} %get-tuple-element.42), channel_id=1, source_target_pairs={{3,0},{2,1},{1,2},{0,3},{7,4},{6,5},{5,6},{4,7},{11,8},{10,9},{9,1... | collective-permute-start | bytes 73736 | tf_op jit(solution)/shard_map/line/ppermute | solution.py:383
  20.6 3.0 %collective-permute-start.6 = (f32[2,3,8,128]{3,2,1,0:T(8,128)S(1)}, f32[2,3,8,128]{3,2,1,0:T(8,128)S(1)}, u32[]{:S(2)}, u32[]{:S(2)}) collective-permute-start(f32[2,3,8,128]{3,2,1,0:T(8,128)S(1)} %get-tuple-element.43), channel_id=1, source_target_pairs={{1,0},{0,1},{3,2},{2,3},{5,4},{4,5},{7,6},{6,7},{9,8},{8,9},{11,10... | collective-permute-start | bytes 73736 | tf_op jit(solution)/shard_map/line/ppermute | solution.py:383
  20.6 3.0 %copy-start.2 = (bf16[4,768,144]{2,1,0:T(8,128)(2,1)S(1)}, bf16[4,768,144]{2,1,0:T(8,128)(2,1)}, u32[]{:S(2)}) copy-start(bf16[4,768,144]{2,1,0:T(8,128)(2,1)} %constant.36.clone.outer) | copy-start | bytes 2654212

commit v5 on v4

--- a/solution.py
+++ b/solution.py
@@ -103,7 +103,7 @@
 
 
 def is_live(slots):
-    return jnp.where(iota(1) < slots[0], 1.0, 0.0).astype(jnp.float32)
+    return jnp.where(iota(1) < slots[...], 1.0, 0.0).astype(jnp.float32)
 
 
 def by_slot(ref):
@@ -113,32 +113,36 @@
     return jnp.broadcast_to(jnp.sum(spread, axis=1, keepdims=True), (SLOTS, LANES)).astype(jnp.int32)
 
 
-def faces_kernel(lengths, connect, orient, field, faces, held, slots, near, link, turn, sems):
+def faces_kernel(lengths, field, faces, held, slots, near, sems):
     lane = iota(1)
     tiles = faces.shape[0] // 3
-    pieces = [(c, pl.ds(h * PER_TILE, PER_TILE)) for c in range(3) for h in range(tiles)]
-    small = [
-        pltpu.make_async_copy(ref, to, sems.at[len(pieces) + k])
-        for k, (ref, to) in enumerate(((lengths, near), (connect, link), (orient, turn)))
-    ]
-    copies = [pltpu.make_async_copy(field.at[at], held.at[at], sems.at[k]) for k, at in enumerate(pieces)]
-    for copy in small + copies:
+    small = pltpu.make_async_copy(lengths, near, sems.at[3])
+    copies = [pltpu.make_async_copy(field.at[c], held.at[c], sems.at[c]) for c in range(3)]
+    small.start()
+    for copy in copies:
         copy.start()
-    for copy in small:
+    small.wait()
+    slots[...] = by_slot(near)
+    source = slots[...] - HALO_LINES + jnp.minimum(lane % GROUP, HALO_LINES - 1)
+    for c, copy in enumerate(copies):
         copy.wait()
-    for k, ref in enumerate((near, link, turn)):
-        slots[k] = by_slot(ref)
-    source = slots[0] - HALO_LINES + jnp.minimum(lane % GROUP, HALO_LINES - 1)
-    for k, copy in enumerate(copies):
+        for h in range(tiles):
+            tile = jnp.zeros((SLOTS, LANES), jnp.float32)
+            for j in range(PER_TILE):
+                picked = jnp.take_along_axis(
+                    held[c, h * PER_TILE + j], source, axis=1, mode="promise_in_bounds"
+                )
+                tile = jnp.where(lane // GROUP == j, picked, tile)
+            faces[c * tiles + h] = tile
+
+
+def joins_kernel(connect, orient, joins, link, turn, sems):
+    copies = [pltpu.make_async_copy(ref, to, sems.at[k]) for k, (ref, to) in enumerate(((connect, link), (orient, turn)))]
+    for copy in copies:
+        copy.start()
+    for k, (copy, to) in enumerate(zip(copies, (link, turn))):
         copy.wait()
-        c, h = divmod(k, tiles)
-        tile = jnp.zeros((SLOTS, LANES), jnp.float32)
-        for j in range(PER_TILE):
-            picked = jnp.take_along_axis(
-                held[c, h * PER_TILE + j], source, axis=1, mode="promise_in_bounds"
-            )
-            tile = jnp.where(lane // GROUP == j, picked, tile)
-        faces[k] = tile
+        joins[k] = by_slot(to)
 
 
 def interior_kernel(begin, more, *refs):
@@ -175,7 +179,7 @@
             coef[r, c] = sums[r][c] + before[r, c] if more else sums[r][c]
 
 
-def ghost_kernel(slots, packed, chip, far, pair, swap, edge_a, edge_b, coef, delta, near_out, far_out, far_too):
+def ghost_kernel(joins, packed, chip, far, pair, swap, edge_a, edge_b, coef, delta, near_out, far_out, far_too):
     part = lax.axis_index("line")
     blk = lax.axis_index("blk")
     count = lax.axis_size("blk")
@@ -183,8 +187,8 @@
     lane = iota(1)
     tiles = chip.shape[0]
     parts = tiles // 3
-    shift = (slots[1] // SLOTS - blk) & (count - 1)
-    src = slots[1] % SLOTS
+    shift = (joins[0] // SLOTS - blk) & (count - 1)
+    src = joins[0] % SLOTS
     is_one, is_two, is_three = shift == count // 2, shift == count // 2 + 1, shift == count // 2 + 2
     raw = []
     for k in range(tiles):
@@ -193,7 +197,7 @@
         row = jnp.where(is_one, pick(jnp.where(even, swap[2 * tiles + k], pair[k])), row)
         row = jnp.where(is_two, pick(jnp.where(even, swap[tiles + k], swap[k])), row)
         raw.append(jnp.where(is_three, pick(jnp.where(even, far[k], swap[tiles + k])), row))
-    turn = slots[2]
+    turn = joins[1]
     cosine = jnp.where(turn == 0, 1.0, jnp.where(turn == 2, -1.0, 0.0))
     sine = jnp.where(turn == 1, 1.0, jnp.where(turn == 3, -1.0, 0.0))
     at = lane % GROUP
@@ -303,8 +307,8 @@
         for c in range(3):
             tile = total[:, c * LANES : (c + 1) * LANES].reshape(PER_TILE, SLOTS, LANES)
             full[c, at] = local[c, at] + tile
-            copies.append(pltpu.make_async_copy(full.at[c, at], advanced.at[c, at], sems.at[3 * h + c]))
-            copies[-1].start()
+        copies.append(pltpu.make_async_copy(full.at[:, at], advanced.at[:, at], sems.at[h]))
+        copies[-1].start()
     for copy in copies:
         copy.wait()
 
@@ -350,9 +354,9 @@
     )
     with jax.named_scope("faces"):
         faces, held, slots = call(
-            faces_kernel, "faces", [HBM] * 4, [packed_tile, block, (3, SLOTS, LANES)], 8, 10**6, 1200000,
-            scratch=[pltpu.VMEM((1, SLOTS), jnp.int32)] * 3 + [dma((tiles + 3,))], kinds={2: jnp.int32},
-        )(lengths, connect, orient, field)
+            faces_kernel, "faces", [HBM] * 2, [packed_tile, block, (SLOTS, LANES)], 8, 10**6, 1200000,
+            scratch=[pltpu.VMEM((1, SLOTS), jnp.int32), dma((4,))], kinds={2: jnp.int32},
+        )(lengths, field)
         chip = over_blk(faces, core)
 
     def inside(begin, length, metric, *before):
@@ -368,7 +372,11 @@
         both = jnp.concatenate([faces, chip], axis=0)
         from_far = over_blk(both, far)
         from_pair = over_blk(both, pair)
-        from_far, coef = lax.optimization_barrier((from_far, coef))
+        (joins,) = call(
+            joins_kernel, "joins", [HBM] * 2, [(2, SLOTS, LANES)], 4, 10**5, 10**5,
+            scratch=[pltpu.VMEM((1, SLOTS), jnp.int32)] * 2 + [dma((2,))], kinds={0: jnp.int32},
+        )(*lax.optimization_barrier((connect, orient, chip))[:2])
+        from_far, coef, joins = lax.optimization_barrier((from_far, coef, joins))
         middle = jnp.where(lax.axis_index("blk") % 2 == 0, from_far[tiles:], from_pair[:tiles])
         swapped = over_blk(jnp.concatenate([from_far[:tiles], middle, from_pair[tiles:]], axis=0), core)
     with jax.named_scope("interior"):
@@ -377,7 +385,7 @@
         delta, near_sum, far_sum, far_again = call(
             ghost_kernel, "ghosts", [VMEM] * 9,
             [packed_tile] + [(2, 3, SLOTS, LANES)] * 3, 8, 10**6, 500000,
-        )(slots, packed, chip, from_far, from_pair, swapped, edge_a, edge_b, coef)
+        )(joins, packed, chip, from_far, from_pair, swapped, edge_a, edge_b, coef)
 
     def over_line(x, k):
         return lax.ppermute(x, "line", [(e ^ k, e) for e in range(parts)])
@@ -397,7 +405,7 @@
     with jax.named_scope("last"):
         (advanced,) = call(
             last_kernel, "last", [VMEM] * 5, [block], 8, 10**7, 2400000, out_specs=[HBM],
-            scratch=[pltpu.VMEM(block, jnp.float32), dma((tiles,))],
+            scratch=[pltpu.VMEM(block, jnp.float32), dma((size // PER_TILE,))],
         )(outer, local, got[1], got[2], got[0])
     return rates, advanced
 

time: 25.1 us -> 24.6 us (0.980)
  waiting for transfers between devices: 5.41 us -> 4.57 us
  Pallas kernels: 6.86 us -> 7.23 us
    ppermute x4, waiting for transfers between devices: 4.53 us -> 3.68 us  [over_blk(): return lax.ppermute(x, 'blk', pairs)]
    pallas_call x1 -> x2, Pallas kernels: 2.09 us -> 2.5 us  [the longest x1 1.66 us: shards(): call(faces_kernel, 'faces', [HBM] * 2, [packed_tile, block, (SLOTS, LANES...]
  transfers between devices with their start and end apart: 7 -> 7, of which waited for: 4 -> 4; matrix products, arithmetic and copies ran while one was open for 0% -> 0% of each run, Pallas kernels for 12% -> 16%
where the time goes in v5:
time: 24.6 us; the launch traced here: 24.5 us
  starting transfers between devices  11.8 us (48%)
  Pallas kernels  7.23 us (29%)
  waiting for transfers between devices  4.57 us (19%)
  between operations  0.8 us (3%)
    ppermute x4, starting transfers between devices, over_blk(): return lax.ppermute(x, 'blk', pairs)  8.13 us
    ppermute x3, starting transfers between devices, over_line(): return lax.ppermute(x, 'line', [(e ^ k, e) for e in range(parts)])  3.69 us
    ppermute x4, waiting for transfers between devices, over_blk(): return lax.ppermute(x, 'blk', pairs)  3.68 us
    pallas_call x1, Pallas kernels, shards(): call(local_kernel, 'local', [VMEM] * 7, [block, block], 12, 10 ** 8, 6000...  2.1 us
    pallas_call x1, Pallas kernels, shards(): call(faces_kernel, 'faces', [HBM] * 2, [packed_tile, block, (SLOTS, LANES...  1.66 us
    pallas_call x1, Pallas kernels, shards(): call(last_kernel, 'last', [VMEM] * 5, [block], 8, 10 ** 7, 2400000, out_s...  1.26 us
    pallas_call x2, Pallas kernels, inside(): call(functools.partial(interior_kernel, begin, bool(before)), 'interior',...  0.91 us
    ppermute x3, waiting for transfers between devices, over_line(): return lax.ppermute(x, 'line', [(e ^ k, e) for e in range(parts)])  0.89 us
  transfers between devices with their start and end apart: 7, of which 4 were waited for; matrix products, arithmetic and copies ran while one was open for 0% of the time, Pallas kernels for 16%

profile of v5, /device:TPU:1, one launch (start us, length us, event | category | flops | bytes accessed | tf_op | source)
XLA Modules:
  0.0 24.5 jit_solution(6839964037523939737)
XLA Ops:
  0.6 0.0 copy-start.5
  0.6 0.0 copy-start
  0.7 1.7 %faces.1 = (f32[9,8,128]{2,1,0:T(8,128)S(1)}, f32[3,96,8,128]{3,2,1,0:T(8,128)S(1)}, s32[8,128]{1,0:T(8,128)S(1)}) custom-call(s32[1,8]{1,0:T(1,128)} %bitcast.3, f32[3,96,8,128]{3,2,1,0:T(8,128)} %field.1), custom_call_target="tpu_custom_call" | custom-call | flops 1000000 | bytes 1200000 | tf_op jit(solution)/shard_map/faces/faces/pallas_call | solution.py:356
  2.3 3.3 %collective-permute-start = (f32[9,8,128]{2,1,0:T(8,128)S(1)}, f32[9,8,128]{2,1,0:T(8,128)S(1)}, u32[]{:S(2)}, u32[]{:S(2)}) collective-permute-start(f32[9,8,128]{2,1,0:T(8,128)S(1)} %get-tuple-element.28), channel_id=1, source_target_pairs={{4,0},{0,4},{12,8},{8,12},{20,16},{16,20},{28,24},{24,28},{36,32},... | collective-permute-start | bytes 110600 | tf_op jit(solution)/shard_map/faces/ppermute | solution.py:345
  5.7 0.3 %interior.2 = (f32[3,32,8,128]{3,2,1,0:T(8,128)S(1)}, f32[4,3,8,128]{3,2,1,0:T(8,128)S(1)}, f32[1,8,128]{2,1,0:T(8,128)S(1)}) custom-call(s32[8,128]{1,0:T(8,128)S(1)} %get-tuple-element.26.refs_0_.slots, f32[4,4,96,128]{3,2,1,0:T(8,128)S(1)} %copy-done, bf16[256,128]{1,0:T(8,128)(2,1)S(1)} %copy-done.5, ...), custom_call_target="tpu_custom_call" | custom-call | flops 10000000 | bytes 1500000 | tf_op jit(solution)/shard_map/interior/interior/pallas_call | solution.py:363
  6.0 0.5 %collective-permute-done.chip = f32[9,8,128]{2,1,0:T(8,128)S(1)} collective-permute-done((f32[9,8,128]{2,1,0:T(8,128)S(1)}, f32[9,8,128]{2,1,0:T(8,128)S(1)}, u32[]{:S(2)}, u32[]{:S(2)}) %collective-permute-start) | collective-permute-done | bytes 36896 | tf_op jit(solution)/shard_map/faces/ppermute | solution.py:345
  6.5 0.0 collective-permute-start.1
  6.5 4.7 %collective-permute-start.2 = (f32[18,8,128]{2,1,0:T(8,128)S(1)}, f32[18,8,128]{2,1,0:T(8,128)S(1)}, u32[]{:S(2)}, u32[]{:S(2)}) collective-permute-start(f32[18,8,128]{2,1,0:T(8,128)S(1)} %constant_dynamic-update-slice_fusion), channel_id=1, source_target_pairs={{0,0},{132,4},{8,8},{140,12},{16,16},{148,20},{24,24},{156,28},{32... | collective-permute-start | bytes 221192 | tf_op jit(solution)/shard_map/faces/ppermute | solution.py:345
  11.3 0.8 %joins.1 = s32[2,8,128]{2,1,0:T(8,128)S(1)} custom-call(s32[1,8]{1,0:T(1,128)} %bitcast.4, s32[1,8]{1,0:T(1,128)} %bitcast.5), custom_call_target="tpu_custom_call" | custom-call | flops 100000 | bytes 100000 | tf_op jit(solution)/shard_map/faces/joins/pallas_call | solution.py:375
  12.1 2.5 %collective-permute-done.1.far = f32[18,8,128]{2,1,0:T(8,128)S(1)} collective-permute-done((f32[18,8,128]{2,1,0:T(8,128)S(1)}, f32[18,8,128]{2,1,0:T(8,128)S(1)}, u32[]{:S(2)}, u32[]{:S(2)}) %collective-permute-start.1) | collective-permute-done | bytes 73760 | tf_op jit(solution)/shard_map/faces/ppermute | solution.py:345
  14.6 0.0 collective-permute-done.2.pair
  14.6 0.0 copy-start.6
  14.6 0.0 copy-start.3
  14.6 0.0 copy-start.4
  14.6 0.1 collective-permute-start.3
  14.7 0.6 %interior.3 = (f32[3,64,8,128]{3,2,1,0:T(8,128)S(1)}, f32[4,3,8,128]{3,2,1,0:T(8,128)S(1)}, f32[2,8,128]{2,1,0:T(8,128)S(1)}) custom-call(s32[8,128]{1,0:T(8,128)S(1)} %get-tuple-element.26.refs_0_.slots, f32[4,4,96,128]{3,2,1,0:T(8,128)S(1)} %copy-done, bf16[256,128]{1,0:T(8,128)(2,1)S(1)} %copy-done.5, ...), custom_call_target="tpu_custom_call" | custom-call | flops 10000000 | bytes 1500000 | tf_op jit(solution)/shard_map/interior/interior/pallas_call | solution.py:363
  15.3 0.7 %collective-permute-done.3.swap = f32[27,8,128]{2,1,0:T(8,128)S(1)} collective-permute-done((f32[27,8,128]{2,1,0:T(8,128)S(1)}, f32[27,8,128]{2,1,0:T(8,128)S(1)}, u32[]{:S(2)}, u32[]{:S(2)}) %collective-permute-start.3) | collective-permute-done | bytes 110624 | tf_op jit(solution)/shard_map/faces/ppermute | solution.py:345
  16.0 0.5 %ghosts.1 = (f32[9,8,128]{2,1,0:T(8,128)S(1)}, f32[2,3,8,128]{3,2,1,0:T(8,128)S(1)}, f32[2,3,8,128]{3,2,1,0:T(8,128)S(1)}, f32[2,3,8,128]{3,2,1,0:T(8,128)S(1)}) custom-call(s32[2,8,128]{2,1,0:T(8,128)S(1)} %joins.1, f32[4,4,3,128]{3,2,1,0:T(4,128)S(1)} %copy-done.6, f32[9,8,128]{2,1,0:T(8,128)S(1)} %collective-permute-done.chip, ...), custom_call_target="tpu_custom_call" | custom-call | flops 1000000 | bytes 500000 | tf_op jit(solution)/shard_map/ghosts/ghosts/pallas_call | solution.py:385
  16.5 2.8 %collective-permute-start.4 = (f32[2,3,8,128]{3,2,1,0:T(8,128)S(1)}, f32[2,3,8,128]{3,2,1,0:T(8,128)S(1)}, u32[]{:S(2)}, u32[]{:S(2)}) collective-permute-start(f32[2,3,8,128]{3,2,1,0:T(8,128)S(1)} %get-tuple-element.47), channel_id=1, source_target_pairs={{2,0},{3,1},{0,2},{1,3},{6,4},{7,5},{4,6},{5,7},{10,8},{11,9},{8,1... | collective-permute-start | bytes 73736 | tf_op jit(solution)/shard_map/line/ppermute | solution.py:391
  19.3 0.9 %collective-permute-start.5 = (f32[2,3,8,128]{3,2,1,0:T(8,128)S(1)}, f32[2,3,8,128]{3,2,1,0:T(8,128)S(1)}, u32[]{:S(2)}, u32[]{:S(2)}) collective-permute-start(f32[2,3,8,128]{3,2,1,0:T(8,128)S(1)} %get-tuple-element.48), channel_id=1, source_target_pairs={{3,0},{2,1},{1,2},{0,3},{7,4},{6,5},{5,6},{4,7},{11,8},{10,9},{9,1... | collective-permute-start | bytes 73736 | tf_op jit(solution)/shard_map/line/ppermute | solution.py:391
  20.2 0.0 copy-start.2
  20.2 2.1 %local.1 = (f32[3,96,8,128]{3,2,1,0:T(8,128)}, f32[3,96,8,128]{3,2,1,0:T(8,128)S(1)}) custom-call(s32[8,128]{1,0:T(8,128)S(1)} %get-tuple-element.26.refs_0_.slots, f32[4,5,104,128]{3,2,1,0:T(8,128)S(1)} %copy-done.3, f32[4,2,96,128]{3,2,1,0:T(8,128)S(1)} %copy-done.4, f32[3,96,8,128]{3,2,1,0:T(8,128)S(1)} %get-tuple-element.27.refs_3_.field, ...), custom_call_target="tpu_custom_call" | custom-call | flops 100000000 | bytes 6000000 | tf_op jit(solution)/shard_map/local/local/pallas_call | solution.py:396
  22.4 0.9 %collective-permute-done.5.three = f32[2,3,8,128]{3,2,1,0:T(8,128)S(1)} collective-permute-done((f32[2,3,8,128]{3,2,1,0:T(8,128)S(1)}, f32[2,3,8,128]{3,2,1,0:T(8,128)S(1)}, u32[]{:S(2)}, u32[]{:S(2)}) %collective-permute-start.5) | collective-permute-done | bytes 24608 | tf_op jit(solution)/shard_map/line/ppermute | solution.py:391
  23.2 1.3 %last.1 = f32[3,96,8,128]{3,2,1,0:T(8,128)} custom-call(bf16[4,768,144]{2,1,0:T(8,128)(2,1)S(1)} %copy-done.2, f32[3,96,8,128]{3,2,1,0:T(8,128)S(1)} %get-tuple-element.46.local, f32[2,3,8,128]{3,2,1,0:T(8,128)S(1)} %collective-permute-done.4.two, f32[2,3,8,128]{3,2,1,0:T(8,128)S(1)} %collective-permute-done.5.three, ...), custom_call_target="tpu_custom_call" | custom-call | flops 10000000 | bytes 2400000 | tf_op jit(solution)/shard_map/last/last/pallas_call | solution.py:406
  (15 shorter events, 0.1 us)
Async XLA Ops:
  0.6 5.0 %copy-start.5 = (bf16[256,128]{1,0:T(8,128)(2,1)S(1)}, bf16[256,128]{1,0:T(8,128)(2,1)}, u32[]{:S(2)}) copy-start(bf16[256,128]{1,0:T(8,128)(2,1)} %constant.37.clone.refs_2_) | copy-start | bytes 196612
  0.6 5.0 %copy-start = (f32[4,4,96,128]{3,2,1,0:T(8,128)S(1)}, f32[4,4,96,128]{3,2,1,0:T(8,128)}, u32[]{:S(2)}) copy-start(f32[4,4,96,128]{3,2,1,0:T(8,128)} %constant.32.clone.refs_1_) | copy-start | bytes 2359300
  0.7 5.0 %copy-start.1 = (f32[96,8,128]{2,1,0:T(8,128)S(1)}, f32[96,8,128]{2,1,0:T(8,128)}, u32[]{:S(2)}) copy-start(f32[96,8,128]{2,1,0:T(8,128)} %refs_4_.3) | copy-start | bytes 1179652
  2.3 4.2 %collective-permute-start = (f32[9,8,128]{2,1,0:T(8,128)S(1)}, f32[9,8,128]{2,1,0:T(8,128)S(1)}, u32[]{:S(2)}, u32[]{:S(2)}) collective-permute-start(f32[9,8,128]{2,1,0:T(8,128)S(1)} %get-tuple-element.28), channel_id=1, source_target_pairs={{4,0},{0,4},{12,8},{8,12},{20,16},{16,20},{28,24},{24,28},{36,32},... | collective-permute-start | bytes 110600 | tf_op jit(solution)/shard_map/faces/ppermute | solution.py:345
  6.5 8.0 %collective-permute-start.1 = (f32[18,8,128]{2,1,0:T(8,128)S(1)}, f32[18,8,128]{2,1,0:T(8,128)S(1)}, u32[]{:S(2)}, u32[]{:S(2)}) collective-permute-start(f32[18,8,128]{2,1,0:T(8,128)S(1)} %constant_dynamic-update-slice_fusion), channel_id=1, source_target_pairs={{136,0},{252,4},{144,8},{4,12},{152,16},{12,20},{160,24},{20,28},{... | collective-permute-start | bytes 221192 | tf_op jit(solution)/shard_map/faces/ppermute | solution.py:345
  6.5 8.0 %collective-permute-start.2 = (f32[18,8,128]{2,1,0:T(8,128)S(1)}, f32[18,8,128]{2,1,0:T(8,128)S(1)}, u32[]{:S(2)}, u32[]{:S(2)}) collective-permute-start(f32[18,8,128]{2,1,0:T(8,128)S(1)} %constant_dynamic-update-slice_fusion), channel_id=1, source_target_pairs={{0,0},{132,4},{8,8},{140,12},{16,16},{148,20},{24,24},{156,28},{32... | collective-permute-start | bytes 221192 | tf_op jit(solution)/shard_map/faces/ppermute | solution.py:345
  14.6 1.4 %copy-start.6 = (f32[4,4,3,128]{3,2,1,0:T(4,128)S(1)}, f32[4,4,3,128]{3,2,1,0:T(4,128)}, u32[]{:S(2)}) copy-start(f32[4,4,3,128]{3,2,1,0:T(4,128)} %constant.33.clone.packed) | copy-start | bytes 73732
  14.6 5.6 %copy-start.3 = (f32[4,5,104,128]{3,2,1,0:T(8,128)S(1)}, f32[4,5,104,128]{3,2,1,0:T(8,128)}, u32[]{:S(2)}) copy-start(f32[4,5,104,128]{3,2,1,0:T(8,128)} %constant.34.clone.forward) | copy-start | bytes 3194884
  14.6 5.6 %copy-start.4 = (f32[4,2,96,128]{3,2,1,0:T(8,128)S(1)}, f32[4,2,96,128]{3,2,1,0:T(8,128)}, u32[]{:S(2)}) copy-start(f32[4,2,96,128]{3,2,1,0:T(8,128)} %constant.35.clone.back) | copy-start | bytes 1179652
  14.6 1.4 %collective-permute-start.3 = (f32[27,8,128]{2,1,0:T(8,128)S(1)}, f32[27,8,128]{2,1,0:T(8,128)S(1)}, u32[]{:S(2)}, u32[]{:S(2)}) collective-permute-start(f32[27,8,128]{2,1,0:T(8,128)S(1)} %pad_maximum_fusion), channel_id=1, source_target_pairs={{4,0},{0,4},{12,8},{8,12},{20,16},{16,20},{28,24},{24,28},{36,32},... | collective-permute-start | bytes 331784 | tf_op jit(solution)/shard_map/faces/ppermute | solution.py:345
  16.5 5.8 %collective-permute-start.4 = (f32[2,3,8,128]{3,2,1,0:T(8,128)S(1)}, f32[2,3,8,128]{3,2,1,0:T(8,128)S(1)}, u32[]{:S(2)}, u32[]{:S(2)}) collective-permute-start(f32[2,3,8,128]{3,2,1,0:T(8,128)S(1)} %get-tuple-element.47), channel_id=1, source_target_pairs={{2,0},{3,1},{0,2},{1,3},{6,4},{7,5},{4,6},{5,7},{10,8},{11,9},{8,1... | collective-permute-start | bytes 73736 | tf_op jit(solution)/shard_map/line/ppermute | solution.py:391
  19.3 3.9 %collective-permute-start.5 = (f32[2,3,8,128]{3,2,1,0:T(8,128)S(1)}, f32[2,3,8,128]{3,2,1,0:T(8,128)S(1)}, u32[]{:S(2)}, u32[]{:S(2)}) collective-permute-start(f32[2,3,8,128]{3,2,1,0:T(8,128)S(1)} %get-tuple-element.48), channel_id=1, source_target_pairs={{3,0},{2,1},{1,2},{0,3},{7,4},{6,5},{5,6},{4,7},{11,8},{10,9},{9,1... | collective-permute-start | bytes 73736 | tf_op jit(solution)/shard_map/line/ppermute | solution.py:391
  20.2 3.0 %collective-permute-start.6 = (f32[2,3,8,128]{3,2,1,0:T(8,128)S(1)}, f32[2,3,8,128]{3,2,1,0:T(8,128)S(1)}, u32[]{:S(2)}, u32[]{:S(2)}) collective-permute-start(f32[2,3,8,128]{3,2,1,0:T(8,128)S(1)} %get-tuple-element.49), channel_id=1, source_target_pairs={{1,0},{0,1},{3,2},{2,3},{5,4},{4,5},{7,6},{6,7},{9,8},{8,9},{11,10... | collective-permute-start | bytes 73736 | tf_op jit(solution)/shard_map/line/ppermute | solution.py:391
  20.2 3.0 %copy-start.2 = (bf16[4,768,144]{2,1,0:T(8,128)(2,1)S(1)}, bf16[4,768,144]{2,1,0:T(8,128)(2,1)}, u32[]{:S(2)}) copy-start(bf16[4,768,144]{2,1,0:T(8,128)(2,1)} %constant.36.clone.outer) | copy-start | bytes 2654212

commit v6 on v5

--- a/solution.py
+++ b/solution.py
@@ -179,13 +179,13 @@
             coef[r, c] = sums[r][c] + before[r, c] if more else sums[r][c]
 
 
-def ghost_kernel(joins, packed, chip, far, pair, swap, edge_a, edge_b, coef, delta, near_out, far_out, far_too):
+def ghost_kernel(ring, joins, packed, other, swap, edge_a, edge_b, coef, delta, near_out, far_out, far_too):
     part = lax.axis_index("line")
     blk = lax.axis_index("blk")
     count = lax.axis_size("blk")
     even = blk % 2 == 0
     lane = iota(1)
-    tiles = chip.shape[0]
+    tiles = ring.shape[0]
     parts = tiles // 3
     shift = (joins[0] // SLOTS - blk) & (count - 1)
     src = joins[0] % SLOTS
@@ -193,10 +193,10 @@
     raw = []
     for k in range(tiles):
         pick = lambda v: jnp.take_along_axis(v, src, axis=0, mode="promise_in_bounds")
-        row = pick(jnp.where(even, swap[k], chip[k]))
-        row = jnp.where(is_one, pick(jnp.where(even, swap[2 * tiles + k], pair[k])), row)
-        row = jnp.where(is_two, pick(jnp.where(even, swap[tiles + k], swap[k])), row)
-        raw.append(jnp.where(is_three, pick(jnp.where(even, far[k], swap[tiles + k])), row))
+        row = pick(ring[k])
+        row = jnp.where(is_one, pick(jnp.where(even, other[k], swap[k])), row)
+        row = jnp.where(is_two, pick(other[tiles + k]), row)
+        raw.append(jnp.where(is_three, pick(jnp.where(even, swap[k], other[k])), row))
     turn = joins[1]
     cosine = jnp.where(turn == 0, 1.0, jnp.where(turn == 2, -1.0, 0.0))
     sine = jnp.where(turn == 1, 1.0, jnp.where(turn == 3, -1.0, 0.0))
@@ -345,8 +345,8 @@
         return lax.ppermute(x, "blk", pairs)
 
     core = [(d ^ 1, d) for d in range(count)]
-    pair = [(d if d % 2 == 0 else (d + half) % count, d) for d in range(count)]
-    far = [((d + half + 2) % count if d % 2 == 0 else (d - 2) % count, d) for d in range(count)]
+    ring = [((d - 1) % count, d) for d in range(count)]
+    other = [((d + half + 2 * (d % 2)) % count, d) for d in range(count)]
 
     lengths, connect, orient = (v[None] for v in (lengths, connect, orient))
     field, lengths, connect, orient = (
@@ -358,6 +358,7 @@
             scratch=[pltpu.VMEM((1, SLOTS), jnp.int32), dma((4,))], kinds={2: jnp.int32},
         )(lengths, field)
         chip = over_blk(faces, core)
+        before = over_blk(faces, ring)
 
     def inside(begin, length, metric, *before):
         return call(
@@ -367,25 +368,22 @@
 
     with jax.named_scope("interior"):
         rates_a, coef, edge_a = inside(0, PER_TILE, stretch)
-        chip, rates_a, coef, edge_a = lax.optimization_barrier((chip, rates_a, coef, edge_a))
     with jax.named_scope("faces"):
         both = jnp.concatenate([faces, chip], axis=0)
-        from_far = over_blk(both, far)
-        from_pair = over_blk(both, pair)
+        from_other = over_blk(both, other)
         (joins,) = call(
             joins_kernel, "joins", [HBM] * 2, [(2, SLOTS, LANES)], 4, 10**5, 10**5,
             scratch=[pltpu.VMEM((1, SLOTS), jnp.int32)] * 2 + [dma((2,))], kinds={0: jnp.int32},
         )(*lax.optimization_barrier((connect, orient, chip))[:2])
-        from_far, coef, joins = lax.optimization_barrier((from_far, coef, joins))
-        middle = jnp.where(lax.axis_index("blk") % 2 == 0, from_far[tiles:], from_pair[:tiles])
-        swapped = over_blk(jnp.concatenate([from_far[:tiles], middle, from_pair[tiles:]], axis=0), core)
+        from_other, coef, joins, rates_a, edge_a = lax.optimization_barrier((from_other, coef, joins, rates_a, edge_a))
+        swapped = over_blk(from_other[tiles:], core)
     with jax.named_scope("interior"):
         rates_b, coef, edge_b = inside(PER_TILE, size - PER_TILE, stretch, coef)
     with jax.named_scope("ghosts"):
         delta, near_sum, far_sum, far_again = call(
-            ghost_kernel, "ghosts", [VMEM] * 9,
+            ghost_kernel, "ghosts", [VMEM] * 8,
             [packed_tile] + [(2, 3, SLOTS, LANES)] * 3, 8, 10**6, 500000,
-        )(joins, packed, chip, from_far, from_pair, swapped, edge_a, edge_b, coef)
+        )(before, joins, packed, from_other, swapped, edge_a, edge_b, coef)
 
     def over_line(x, k):
         return lax.ppermute(x, "line", [(e ^ k, e) for e in range(parts)])

time: 24.6 us -> 24.1 us (0.980)
  the two profiles are of different devices: /device:TPU:1 before, /device:TPU:8 now
where the time goes in v6:
time: 24.1 us; the launch traced here: 24 us
  starting transfers between devices  11.3 us (47%)
  Pallas kernels  7.3 us (30%)
  waiting for transfers between devices  4.56 us (19%)
  between operations  0.78 us (3%)
    ppermute x4, starting transfers between devices, over_blk(): return lax.ppermute(x, 'blk', pairs)  7.09 us
    ppermute x3, starting transfers between devices, over_line(): return lax.ppermute(x, 'line', [(e ^ k, e) for e in range(parts)])  4.25 us
    ppermute x4, waiting for transfers between devices, over_blk(): return lax.ppermute(x, 'blk', pairs)  2.81 us
    pallas_call x1, Pallas kernels, shards(): call(local_kernel, 'local', [VMEM] * 7, [block, block], 12, 10 ** 8, 6000...  2.11 us
    ppermute x3, waiting for transfers between devices, over_line(): return lax.ppermute(x, 'line', [(e ^ k, e) for e in range(parts)])  1.75 us
    pallas_call x1, Pallas kernels, shards(): call(faces_kernel, 'faces', [HBM] * 2, [packed_tile, block, (SLOTS, LANES...  1.66 us
    pallas_call x1, Pallas kernels, shards(): call(last_kernel, 'last', [VMEM] * 5, [block], 8, 10 ** 7, 2400000, out_s...  1.25 us
    pallas_call x2, Pallas kernels, inside(): call(functools.partial(interior_kernel, begin, bool(before)), 'interior',...  0.98 us
  transfers between devices with their start and end apart: 7, of which 3 were waited for; matrix products, arithmetic and copies ran while one was open for 0% of the time, Pallas kernels for 16%

profile of v6, /device:TPU:8, one launch (start us, length us, event | category | flops | bytes accessed | tf_op | source)
XLA Modules:
  0.0 24.0 jit_solution(12895948747693660426)
XLA Ops:
  0.6 0.0 copy-start.5
  0.6 0.0 copy-start
  0.7 1.7 %faces.1 = (f32[9,8,128]{2,1,0:T(8,128)S(1)}, f32[3,96,8,128]{3,2,1,0:T(8,128)S(1)}, s32[8,128]{1,0:T(8,128)S(1)}) custom-call(s32[1,8]{1,0:T(1,128)} %bitcast.3, f32[3,96,8,128]{3,2,1,0:T(8,128)} %field.1), custom_call_target="tpu_custom_call" | custom-call | flops 1000000 | bytes 1200000 | tf_op jit(solution)/shard_map/faces/faces/pallas_call | solution.py:356
  2.3 0.1 collective-permute-start
  2.4 1.2 %collective-permute-done = f32[9,8,128]{2,1,0:T(8,128)S(1)} collective-permute-done((f32[9,8,128]{2,1,0:T(8,128)S(1)}, f32[9,8,128]{2,1,0:T(8,128)S(1)}, u32[]{:S(2)}, u32[]{:S(2)}) %collective-permute-start) | collective-permute-done | bytes 36896 | tf_op jit(solution)/shard_map/faces/ppermute | solution.py:345
  3.6 2.3 %collective-permute-start.1 = (f32[18,8,128]{2,1,0:T(8,128)S(1)}, f32[18,8,128]{2,1,0:T(8,128)S(1)}, u32[]{:S(2)}, u32[]{:S(2)}) collective-permute-start(f32[18,8,128]{2,1,0:T(8,128)S(1)} %pad_maximum_fusion), channel_id=1, source_target_pairs={{128,0},{140,4},{136,8},{148,12},{144,16},{156,20},{152,24},{164,2... | collective-permute-start | bytes 221192 | tf_op jit(solution)/shard_map/faces/ppermute | solution.py:345
  5.9 4.5 %collective-permute-start.2 = (f32[9,8,128]{2,1,0:T(8,128)S(1)}, f32[9,8,128]{2,1,0:T(8,128)S(1)}, u32[]{:S(2)}, u32[]{:S(2)}) collective-permute-start(f32[9,8,128]{2,1,0:T(8,128)S(1)} %get-tuple-element.26), channel_id=1, source_target_pairs={{252,0},{0,4},{4,8},{8,12},{12,16},{16,20},{20,24},{24,28},{28,32}... | collective-permute-start | bytes 110600 | tf_op jit(solution)/shard_map/faces/ppermute | solution.py:345
  10.4 0.3 %interior.2 = (f32[3,32,8,128]{3,2,1,0:T(8,128)S(1)}, f32[4,3,8,128]{3,2,1,0:T(8,128)S(1)}, f32[1,8,128]{2,1,0:T(8,128)S(1)}) custom-call(s32[8,128]{1,0:T(8,128)S(1)} %get-tuple-element.24.refs_0_.slots, f32[4,4,96,128]{3,2,1,0:T(8,128)S(1)} %copy-done, bf16[256,128]{1,0:T(8,128)(2,1)S(1)} %copy-done.5, ...), custom_call_target="tpu_custom_call" | custom-call | flops 10000000 | bytes 1500000 | tf_op jit(solution)/shard_map/interior/interior/pallas_call | solution.py:364
  10.8 0.8 %joins.1 = s32[2,8,128]{2,1,0:T(8,128)S(1)} custom-call(s32[1,8]{1,0:T(1,128)} %bitcast.4, s32[1,8]{1,0:T(1,128)} %bitcast.5), custom_call_target="tpu_custom_call" | custom-call | flops 100000 | bytes 100000 | tf_op jit(solution)/shard_map/faces/joins/pallas_call | solution.py:374
  11.6 0.0 collective-permute-done.1.other
  11.6 0.0 copy-start.6
  11.6 0.0 copy-start.3
  11.6 0.0 copy-start.4
  11.7 0.2 %collective-permute-start.3 = (f32[9,8,128]{2,1,0:T(8,128)S(1)}, f32[9,8,128]{2,1,0:T(8,128)S(1)}, u32[]{:S(2)}, u32[]{:S(2)}) collective-permute-start(f32[9,8,128]{2,1,0:T(8,128)S(1)} %slice.3), channel_id=1, source_target_pairs={{4,0},{0,4},{12,8},{8,12},{20,16},{16,20},{28,24},{24,28},{36,32},... | collective-permute-start | bytes 110600 | tf_op jit(solution)/shard_map/faces/ppermute | solution.py:345
  11.9 0.6 %interior.3 = (f32[3,64,8,128]{3,2,1,0:T(8,128)S(1)}, f32[4,3,8,128]{3,2,1,0:T(8,128)S(1)}, f32[2,8,128]{2,1,0:T(8,128)S(1)}) custom-call(s32[8,128]{1,0:T(8,128)S(1)} %get-tuple-element.24.refs_0_.slots, f32[4,4,96,128]{3,2,1,0:T(8,128)S(1)} %copy-done, bf16[256,128]{1,0:T(8,128)(2,1)S(1)} %copy-done.5, ...), custom_call_target="tpu_custom_call" | custom-call | flops 10000000 | bytes 1500000 | tf_op jit(solution)/shard_map/interior/interior/pallas_call | solution.py:364
  12.5 1.6 %collective-permute-done.2.ring = f32[9,8,128]{2,1,0:T(8,128)S(1)} collective-permute-done((f32[9,8,128]{2,1,0:T(8,128)S(1)}, f32[9,8,128]{2,1,0:T(8,128)S(1)}, u32[]{:S(2)}, u32[]{:S(2)}) %collective-permute-start.2) | collective-permute-done | bytes 36896 | tf_op jit(solution)/shard_map/faces/ppermute | solution.py:345
  14.2 0.5 %ghosts.1 = (f32[9,8,128]{2,1,0:T(8,128)S(1)}, f32[2,3,8,128]{3,2,1,0:T(8,128)S(1)}, f32[2,3,8,128]{3,2,1,0:T(8,128)S(1)}, f32[2,3,8,128]{3,2,1,0:T(8,128)S(1)}) custom-call(f32[9,8,128]{2,1,0:T(8,128)S(1)} %collective-permute-done.2.ring, s32[2,8,128]{2,1,0:T(8,128)S(1)} %joins.1, f32[4,4,3,128]{3,2,1,0:T(4,128)S(1)} %copy-done.6, ...), custom_call_target="tpu_custom_call" | custom-call | flops 1000000 | bytes 500000 | tf_op jit(solution)/shard_map/ghosts/ghosts/pallas_call | solution.py:383
  14.6 3.1 %collective-permute-start.4 = (f32[2,3,8,128]{3,2,1,0:T(8,128)S(1)}, f32[2,3,8,128]{3,2,1,0:T(8,128)S(1)}, u32[]{:S(2)}, u32[]{:S(2)}) collective-permute-start(f32[2,3,8,128]{3,2,1,0:T(8,128)S(1)} %get-tuple-element.43), channel_id=1, source_target_pairs={{2,0},{3,1},{0,2},{1,3},{6,4},{7,5},{4,6},{5,7},{10,8},{11,9},{8,1... | collective-permute-start | bytes 73736 | tf_op jit(solution)/shard_map/line/ppermute | solution.py:389
  17.7 1.1 %collective-permute-start.5 = (f32[2,3,8,128]{3,2,1,0:T(8,128)S(1)}, f32[2,3,8,128]{3,2,1,0:T(8,128)S(1)}, u32[]{:S(2)}, u32[]{:S(2)}) collective-permute-start(f32[2,3,8,128]{3,2,1,0:T(8,128)S(1)} %get-tuple-element.44), channel_id=1, source_target_pairs={{3,0},{2,1},{1,2},{0,3},{7,4},{6,5},{5,6},{4,7},{11,8},{10,9},{9,1... | collective-permute-start | bytes 73736 | tf_op jit(solution)/shard_map/line/ppermute | solution.py:389
  18.9 0.0 collective-permute-start.6
  18.9 0.0 copy-start.2
  18.9 2.1 %local.1 = (f32[3,96,8,128]{3,2,1,0:T(8,128)}, f32[3,96,8,128]{3,2,1,0:T(8,128)S(1)}) custom-call(s32[8,128]{1,0:T(8,128)S(1)} %get-tuple-element.24.refs_0_.slots, f32[4,5,104,128]{3,2,1,0:T(8,128)S(1)} %copy-done.3, f32[4,2,96,128]{3,2,1,0:T(8,128)S(1)} %copy-done.4, f32[3,96,8,128]{3,2,1,0:T(8,128)S(1)} %get-tuple-element.25.refs_3_.field, ...), custom_call_target="tpu_custom_call" | custom-call | flops 100000000 | bytes 6000000 | tf_op jit(solution)/shard_map/local/local/pallas_call | solution.py:394
  21.0 1.7 %collective-permute-done.5.three = f32[2,3,8,128]{3,2,1,0:T(8,128)S(1)} collective-permute-done((f32[2,3,8,128]{3,2,1,0:T(8,128)S(1)}, f32[2,3,8,128]{3,2,1,0:T(8,128)S(1)}, u32[]{:S(2)}, u32[]{:S(2)}) %collective-permute-start.5) | collective-permute-done | bytes 24608 | tf_op jit(solution)/shard_map/line/ppermute | solution.py:389
  22.8 1.3 %last.1 = f32[3,96,8,128]{3,2,1,0:T(8,128)} custom-call(bf16[4,768,144]{2,1,0:T(8,128)(2,1)S(1)} %copy-done.2, f32[3,96,8,128]{3,2,1,0:T(8,128)S(1)} %get-tuple-element.42.local, f32[2,3,8,128]{3,2,1,0:T(8,128)S(1)} %collective-permute-done.4.two, f32[2,3,8,128]{3,2,1,0:T(8,128)S(1)} %collective-permute-done.5.three, ...), custom_call_target="tpu_custom_call" | custom-call | flops 10000000 | bytes 2400000 | tf_op jit(solution)/shard_map/last/last/pallas_call | solution.py:404
  (13 shorter events, 0.0 us)
Async XLA Ops:
  0.6 9.8 %copy-start.5 = (bf16[256,128]{1,0:T(8,128)(2,1)S(1)}, bf16[256,128]{1,0:T(8,128)(2,1)}, u32[]{:S(2)}) copy-start(bf16[256,128]{1,0:T(8,128)(2,1)} %constant.17.clone.refs_2_) | copy-start | bytes 196612
  0.6 9.8 %copy-start = (f32[4,4,96,128]{3,2,1,0:T(8,128)S(1)}, f32[4,4,96,128]{3,2,1,0:T(8,128)}, u32[]{:S(2)}) copy-start(f32[4,4,96,128]{3,2,1,0:T(8,128)} %constant.12.clone.refs_1_) | copy-start | bytes 2359300
  0.7 9.7 %copy-start.1 = (f32[96,8,128]{2,1,0:T(8,128)S(1)}, f32[96,8,128]{2,1,0:T(8,128)}, u32[]{:S(2)}) copy-start(f32[96,8,128]{2,1,0:T(8,128)} %refs_4_.3) | copy-start | bytes 1179652
  2.3 1.3 %collective-permute-start = (f32[9,8,128]{2,1,0:T(8,128)S(1)}, f32[9,8,128]{2,1,0:T(8,128)S(1)}, u32[]{:S(2)}, u32[]{:S(2)}) collective-permute-start(f32[9,8,128]{2,1,0:T(8,128)S(1)} %get-tuple-element.26), channel_id=1, source_target_pairs={{4,0},{0,4},{12,8},{8,12},{20,16},{16,20},{28,24},{24,28},{36,32},... | collective-permute-start | bytes 110600 | tf_op jit(solution)/shard_map/faces/ppermute | solution.py:345
  3.6 8.0 %collective-permute-start.1 = (f32[18,8,128]{2,1,0:T(8,128)S(1)}, f32[18,8,128]{2,1,0:T(8,128)S(1)}, u32[]{:S(2)}, u32[]{:S(2)}) collective-permute-start(f32[18,8,128]{2,1,0:T(8,128)S(1)} %pad_maximum_fusion), channel_id=1, source_target_pairs={{128,0},{140,4},{136,8},{148,12},{144,16},{156,20},{152,24},{164,2... | collective-permute-start | bytes 221192 | tf_op jit(solution)/shard_map/faces/ppermute | solution.py:345
  5.9 8.2 %collective-permute-start.2 = (f32[9,8,128]{2,1,0:T(8,128)S(1)}, f32[9,8,128]{2,1,0:T(8,128)S(1)}, u32[]{:S(2)}, u32[]{:S(2)}) collective-permute-start(f32[9,8,128]{2,1,0:T(8,128)S(1)} %get-tuple-element.26), channel_id=1, source_target_pairs={{252,0},{0,4},{4,8},{8,12},{12,16},{16,20},{20,24},{24,28},{28,32}... | collective-permute-start | bytes 110600 | tf_op jit(solution)/shard_map/faces/ppermute | solution.py:345
  11.6 2.5 %copy-start.6 = (f32[4,4,3,128]{3,2,1,0:T(4,128)S(1)}, f32[4,4,3,128]{3,2,1,0:T(4,128)}, u32[]{:S(2)}) copy-start(f32[4,4,3,128]{3,2,1,0:T(4,128)} %constant.13.clone.packed) | copy-start | bytes 73732
  11.6 7.2 %copy-start.3 = (f32[4,5,104,128]{3,2,1,0:T(8,128)S(1)}, f32[4,5,104,128]{3,2,1,0:T(8,128)}, u32[]{:S(2)}) copy-start(f32[4,5,104,128]{3,2,1,0:T(8,128)} %constant.14.clone.forward) | copy-start | bytes 3194884
  11.6 7.2 %copy-start.4 = (f32[4,2,96,128]{3,2,1,0:T(8,128)S(1)}, f32[4,2,96,128]{3,2,1,0:T(8,128)}, u32[]{:S(2)}) copy-start(f32[4,2,96,128]{3,2,1,0:T(8,128)} %constant.15.clone.back) | copy-start | bytes 1179652
  11.7 2.5 %collective-permute-start.3 = (f32[9,8,128]{2,1,0:T(8,128)S(1)}, f32[9,8,128]{2,1,0:T(8,128)S(1)}, u32[]{:S(2)}, u32[]{:S(2)}) collective-permute-start(f32[9,8,128]{2,1,0:T(8,128)S(1)} %slice.3), channel_id=1, source_target_pairs={{4,0},{0,4},{12,8},{8,12},{20,16},{16,20},{28,24},{24,28},{36,32},... | collective-permute-start | bytes 110600 | tf_op jit(solution)/shard_map/faces/ppermute | solution.py:345
  14.6 6.4 %collective-permute-start.4 = (f32[2,3,8,128]{3,2,1,0:T(8,128)S(1)}, f32[2,3,8,128]{3,2,1,0:T(8,128)S(1)}, u32[]{:S(2)}, u32[]{:S(2)}) collective-permute-start(f32[2,3,8,128]{3,2,1,0:T(8,128)S(1)} %get-tuple-element.43), channel_id=1, source_target_pairs={{2,0},{3,1},{0,2},{1,3},{6,4},{7,5},{4,6},{5,7},{10,8},{11,9},{8,1... | collective-permute-start | bytes 73736 | tf_op jit(solution)/shard_map/line/ppermute | solution.py:389
  17.7 5.0 %collective-permute-start.5 = (f32[2,3,8,128]{3,2,1,0:T(8,128)S(1)}, f32[2,3,8,128]{3,2,1,0:T(8,128)S(1)}, u32[]{:S(2)}, u32[]{:S(2)}) collective-permute-start(f32[2,3,8,128]{3,2,1,0:T(8,128)S(1)} %get-tuple-element.44), channel_id=1, source_target_pairs={{3,0},{2,1},{1,2},{0,3},{7,4},{6,5},{5,6},{4,7},{11,8},{10,9},{9,1... | collective-permute-start | bytes 73736 | tf_op jit(solution)/shard_map/line/ppermute | solution.py:389
  18.9 3.9 %collective-permute-start.6 = (f32[2,3,8,128]{3,2,1,0:T(8,128)S(1)}, f32[2,3,8,128]{3,2,1,0:T(8,128)S(1)}, u32[]{:S(2)}, u32[]{:S(2)}) collective-permute-start(f32[2,3,8,128]{3,2,1,0:T(8,128)S(1)} %get-tuple-element.45), channel_id=1, source_target_pairs={{1,0},{0,1},{3,2},{2,3},{5,4},{4,5},{7,6},{6,7},{9,8},{8,9},{11,10... | collective-permute-start | bytes 73736 | tf_op jit(solution)/shard_map/line/ppermute | solution.py:389
  18.9 3.9 %copy-start.2 = (bf16[4,768,144]{2,1,0:T(8,128)(2,1)S(1)}, bf16[4,768,144]{2,1,0:T(8,128)(2,1)}, u32[]{:S(2)}) copy-start(bf16[4,768,144]{2,1,0:T(8,128)(2,1)} %constant.16.clone.outer) | copy-start | bytes 2654212

commit v7 on v6

--- a/solution.py
+++ b/solution.py
@@ -369,13 +369,14 @@
     with jax.named_scope("interior"):
         rates_a, coef, edge_a = inside(0, PER_TILE, stretch)
     with jax.named_scope("faces"):
-        both = jnp.concatenate([faces, chip], axis=0)
-        from_other = over_blk(both, other)
         (joins,) = call(
             joins_kernel, "joins", [HBM] * 2, [(2, SLOTS, LANES)], 4, 10**5, 10**5,
             scratch=[pltpu.VMEM((1, SLOTS), jnp.int32)] * 2 + [dma((2,))], kinds={0: jnp.int32},
-        )(*lax.optimization_barrier((connect, orient, chip))[:2])
-        from_other, coef, joins, rates_a, edge_a = lax.optimization_barrier((from_other, coef, joins, rates_a, edge_a))
+        )(connect, orient)
+        chip, joins = lax.optimization_barrier((chip, joins))
+        both = jnp.concatenate([faces, chip], axis=0)
+        from_other = over_blk(both, other)
+        from_other, coef, rates_a, edge_a = lax.optimization_barrier((from_other, coef, rates_a, edge_a))
         swapped = over_blk(from_other[tiles:], core)
     with jax.named_scope("interior"):
         rates_b, coef, edge_b = inside(PER_TILE, size - PER_TILE, stretch, coef)

time: 24.1 us -> 24.2 us (level)
  starting transfers between devices: 11.3 us -> 12.3 us
  waiting for transfers between devices: 4.56 us -> 3.71 us
    ppermute x4, starting transfers between devices: 7.09 us -> 8 us  [over_blk(): return lax.ppermute(x, 'blk', pairs)]
    ppermute x4, waiting for transfers between devices: 2.81 us -> 1.96 us  [over_blk(): return lax.ppermute(x, 'blk', pairs)]
where the time goes in v7:
time: 24.2 us; the launch traced here: 24.1 us
  starting transfers between devices  12.3 us (51%)
  Pallas kernels  7.3 us (30%)
  waiting for transfers between devices  3.71 us (15%)
  between operations  0.78 us (3%)
    ppermute x4, starting transfers between devices, over_blk(): return lax.ppermute(x, 'blk', pairs)  8 us
    ppermute x3, starting transfers between devices, over_line(): return lax.ppermute(x, 'line', [(e ^ k, e) for e in range(parts)])  4.25 us
    pallas_call x1, Pallas kernels, shards(): call(local_kernel, 'local', [VMEM] * 7, [block, block], 12, 10 ** 8, 6000...  2.11 us
    ppermute x4, waiting for transfers between devices, over_blk(): return lax.ppermute(x, 'blk', pairs)  1.96 us
    ppermute x3, waiting for transfers between devices, over_line(): return lax.ppermute(x, 'line', [(e ^ k, e) for e in range(parts)])  1.75 us
    pallas_call x1, Pallas kernels, shards(): call(faces_kernel, 'faces', [HBM] * 2, [packed_tile, block, (SLOTS, LANES...  1.66 us
    pallas_call x1, Pallas kernels, shards(): call(last_kernel, 'last', [VMEM] * 5, [block], 8, 10 ** 7, 2400000, out_s...  1.25 us
    pallas_call x2, Pallas kernels, inside(): call(functools.partial(interior_kernel, begin, bool(before)), 'interior',...  0.98 us
  transfers between devices with their start and end apart: 7, of which 3 were waited for; matrix products, arithmetic and copies ran while one was open for 0% of the time, Pallas kernels for 16%

profile of v7, /device:TPU:8, one launch (start us, length us, event | category | flops | bytes accessed | tf_op | source)
XLA Modules:
  0.0 24.1 jit_solution(2228018263750763391)
XLA Ops:
  0.6 0.0 copy-start.5
  0.6 0.0 copy-start
  0.7 1.7 %faces.1 = (f32[9,8,128]{2,1,0:T(8,128)S(1)}, f32[3,96,8,128]{3,2,1,0:T(8,128)S(1)}, s32[8,128]{1,0:T(8,128)S(1)}) custom-call(s32[1,8]{1,0:T(1,128)} %bitcast.3, f32[3,96,8,128]{3,2,1,0:T(8,128)} %field.1), custom_call_target="tpu_custom_call" | custom-call | flops 1000000 | bytes 1200000 | tf_op jit(solution)/shard_map/faces/faces/pallas_call | solution.py:356
  2.3 0.1 collective-permute-start
  2.4 0.8 %joins.1 = s32[2,8,128]{2,1,0:T(8,128)S(1)} custom-call(s32[1,8]{1,0:T(1,128)} %bitcast.4, s32[1,8]{1,0:T(1,128)} %bitcast.5), custom_call_target="tpu_custom_call" | custom-call | flops 100000 | bytes 100000 | tf_op jit(solution)/shard_map/faces/joins/pallas_call | solution.py:372
  3.3 0.4 %collective-permute-done = f32[9,8,128]{2,1,0:T(8,128)S(1)} collective-permute-done((f32[9,8,128]{2,1,0:T(8,128)S(1)}, f32[9,8,128]{2,1,0:T(8,128)S(1)}, u32[]{:S(2)}, u32[]{:S(2)}) %collective-permute-start) | collective-permute-done | bytes 36896 | tf_op jit(solution)/shard_map/faces/ppermute | solution.py:345
  3.6 2.3 %collective-permute-start.1 = (f32[18,8,128]{2,1,0:T(8,128)S(1)}, f32[18,8,128]{2,1,0:T(8,128)S(1)}, u32[]{:S(2)}, u32[]{:S(2)}) collective-permute-start(f32[18,8,128]{2,1,0:T(8,128)S(1)} %pad_maximum_fusion), channel_id=1, source_target_pairs={{128,0},{140,4},{136,8},{148,12},{144,16},{156,20},{152,24},{164,2... | collective-permute-start | bytes 221192 | tf_op jit(solution)/shard_map/faces/ppermute | solution.py:345
  5.9 4.5 %collective-permute-start.2 = (f32[9,8,128]{2,1,0:T(8,128)S(1)}, f32[9,8,128]{2,1,0:T(8,128)S(1)}, u32[]{:S(2)}, u32[]{:S(2)}) collective-permute-start(f32[9,8,128]{2,1,0:T(8,128)S(1)} %get-tuple-element.25), channel_id=1, source_target_pairs={{252,0},{0,4},{4,8},{8,12},{12,16},{16,20},{20,24},{24,28},{28,32}... | collective-permute-start | bytes 110600 | tf_op jit(solution)/shard_map/faces/ppermute | solution.py:345
  10.5 0.3 %interior.2 = (f32[3,32,8,128]{3,2,1,0:T(8,128)S(1)}, f32[4,3,8,128]{3,2,1,0:T(8,128)S(1)}, f32[1,8,128]{2,1,0:T(8,128)S(1)}) custom-call(s32[8,128]{1,0:T(8,128)S(1)} %get-tuple-element.23.refs_0_.slots, f32[4,4,96,128]{3,2,1,0:T(8,128)S(1)} %copy-done, bf16[256,128]{1,0:T(8,128)(2,1)S(1)} %copy-done.5, ...), custom_call_target="tpu_custom_call" | custom-call | flops 10000000 | bytes 1500000 | tf_op jit(solution)/shard_map/interior/interior/pallas_call | solution.py:364
  10.8 0.0 copy-start.6
  10.9 0.0 copy-start.3
  10.9 0.0 copy-start.4
  10.9 1.1 %collective-permute-start.3 = (f32[9,8,128]{2,1,0:T(8,128)S(1)}, f32[9,8,128]{2,1,0:T(8,128)S(1)}, u32[]{:S(2)}, u32[]{:S(2)}) collective-permute-start(f32[9,8,128]{2,1,0:T(8,128)S(1)} %slice.3), channel_id=1, source_target_pairs={{4,0},{0,4},{12,8},{8,12},{20,16},{16,20},{28,24},{24,28},{36,32},... | collective-permute-start | bytes 110600 | tf_op jit(solution)/shard_map/faces/ppermute | solution.py:345
  12.0 0.6 %interior.3 = (f32[3,64,8,128]{3,2,1,0:T(8,128)S(1)}, f32[4,3,8,128]{3,2,1,0:T(8,128)S(1)}, f32[2,8,128]{2,1,0:T(8,128)S(1)}) custom-call(s32[8,128]{1,0:T(8,128)S(1)} %get-tuple-element.23.refs_0_.slots, f32[4,4,96,128]{3,2,1,0:T(8,128)S(1)} %copy-done, bf16[256,128]{1,0:T(8,128)(2,1)S(1)} %copy-done.5, ...), custom_call_target="tpu_custom_call" | custom-call | flops 10000000 | bytes 1500000 | tf_op jit(solution)/shard_map/interior/interior/pallas_call | solution.py:364
  12.6 1.6 %collective-permute-done.2.ring = f32[9,8,128]{2,1,0:T(8,128)S(1)} collective-permute-done((f32[9,8,128]{2,1,0:T(8,128)S(1)}, f32[9,8,128]{2,1,0:T(8,128)S(1)}, u32[]{:S(2)}, u32[]{:S(2)}) %collective-permute-start.2) | collective-permute-done | bytes 36896 | tf_op jit(solution)/shard_map/faces/ppermute | solution.py:345
  14.2 0.0 collective-permute-done.3.swap
  14.2 0.5 %ghosts.1 = (f32[9,8,128]{2,1,0:T(8,128)S(1)}, f32[2,3,8,128]{3,2,1,0:T(8,128)S(1)}, f32[2,3,8,128]{3,2,1,0:T(8,128)S(1)}, f32[2,3,8,128]{3,2,1,0:T(8,128)S(1)}) custom-call(f32[9,8,128]{2,1,0:T(8,128)S(1)} %collective-permute-done.2.ring, s32[2,8,128]{2,1,0:T(8,128)S(1)} %joins.1, f32[4,4,3,128]{3,2,1,0:T(4,128)S(1)} %copy-done.6, ...), custom_call_target="tpu_custom_call" | custom-call | flops 1000000 | bytes 500000 | tf_op jit(solution)/shard_map/ghosts/ghosts/pallas_call | solution.py:384
  14.7 3.1 %collective-permute-start.4 = (f32[2,3,8,128]{3,2,1,0:T(8,128)S(1)}, f32[2,3,8,128]{3,2,1,0:T(8,128)S(1)}, u32[]{:S(2)}, u32[]{:S(2)}) collective-permute-start(f32[2,3,8,128]{3,2,1,0:T(8,128)S(1)} %get-tuple-element.41), channel_id=1, source_target_pairs={{2,0},{3,1},{0,2},{1,3},{6,4},{7,5},{4,6},{5,7},{10,8},{11,9},{8,1... | collective-permute-start | bytes 73736 | tf_op jit(solution)/shard_map/line/ppermute | solution.py:390
  17.8 1.1 %collective-permute-start.5 = (f32[2,3,8,128]{3,2,1,0:T(8,128)S(1)}, f32[2,3,8,128]{3,2,1,0:T(8,128)S(1)}, u32[]{:S(2)}, u32[]{:S(2)}) collective-permute-start(f32[2,3,8,128]{3,2,1,0:T(8,128)S(1)} %get-tuple-element.42), channel_id=1, source_target_pairs={{3,0},{2,1},{1,2},{0,3},{7,4},{6,5},{5,6},{4,7},{11,8},{10,9},{9,1... | collective-permute-start | bytes 73736 | tf_op jit(solution)/shard_map/line/ppermute | solution.py:390
  19.0 0.0 copy-start.2
  19.0 2.1 %local.1 = (f32[3,96,8,128]{3,2,1,0:T(8,128)}, f32[3,96,8,128]{3,2,1,0:T(8,128)S(1)}) custom-call(s32[8,128]{1,0:T(8,128)S(1)} %get-tuple-element.23.refs_0_.slots, f32[4,5,104,128]{3,2,1,0:T(8,128)S(1)} %copy-done.3, f32[4,2,96,128]{3,2,1,0:T(8,128)S(1)} %copy-done.4, f32[3,96,8,128]{3,2,1,0:T(8,128)S(1)} %get-tuple-element.24.refs_3_.field, ...), custom_call_target="tpu_custom_call" | custom-call | flops 100000000 | bytes 6000000 | tf_op jit(solution)/shard_map/local/local/pallas_call | solution.py:395
  21.1 1.7 %collective-permute-done.5.three = f32[2,3,8,128]{3,2,1,0:T(8,128)S(1)} collective-permute-done((f32[2,3,8,128]{3,2,1,0:T(8,128)S(1)}, f32[2,3,8,128]{3,2,1,0:T(8,128)S(1)}, u32[]{:S(2)}, u32[]{:S(2)}) %collective-permute-start.5) | collective-permute-done | bytes 24608 | tf_op jit(solution)/shard_map/line/ppermute | solution.py:390
  22.8 0.0 collective-permute-done.6.one
  22.8 1.3 %last.1 = f32[3,96,8,128]{3,2,1,0:T(8,128)} custom-call(bf16[4,768,144]{2,1,0:T(8,128)(2,1)S(1)} %copy-done.2, f32[3,96,8,128]{3,2,1,0:T(8,128)S(1)} %get-tuple-element.40.local, f32[2,3,8,128]{3,2,1,0:T(8,128)S(1)} %collective-permute-done.4.two, f32[2,3,8,128]{3,2,1,0:T(8,128)S(1)} %collective-permute-done.5.three, ...), custom_call_target="tpu_custom_call" | custom-call | flops 10000000 | bytes 2400000 | tf_op jit(solution)/shard_map/last/last/pallas_call | solution.py:405
  (13 shorter events, 0.0 us)
Async XLA Ops:
  0.6 9.8 %copy-start.5 = (bf16[256,128]{1,0:T(8,128)(2,1)S(1)}, bf16[256,128]{1,0:T(8,128)(2,1)}, u32[]{:S(2)}) copy-start(bf16[256,128]{1,0:T(8,128)(2,1)} %constant.17.clone.refs_2_) | copy-start | bytes 196612
  0.6 9.8 %copy-start = (f32[4,4,96,128]{3,2,1,0:T(8,128)S(1)}, f32[4,4,96,128]{3,2,1,0:T(8,128)}, u32[]{:S(2)}) copy-start(f32[4,4,96,128]{3,2,1,0:T(8,128)} %constant.12.clone.refs_1_) | copy-start | bytes 2359300
  0.7 9.8 %copy-start.1 = (f32[96,8,128]{2,1,0:T(8,128)S(1)}, f32[96,8,128]{2,1,0:T(8,128)}, u32[]{:S(2)}) copy-start(f32[96,8,128]{2,1,0:T(8,128)} %refs_4_.3) | copy-start | bytes 1179652
  2.3 1.3 %collective-permute-start = (f32[9,8,128]{2,1,0:T(8,128)S(1)}, f32[9,8,128]{2,1,0:T(8,128)S(1)}, u32[]{:S(2)}, u32[]{:S(2)}) collective-permute-start(f32[9,8,128]{2,1,0:T(8,128)S(1)} %get-tuple-element.25), channel_id=1, source_target_pairs={{4,0},{0,4},{12,8},{8,12},{20,16},{16,20},{28,24},{24,28},{36,32},... | collective-permute-start | bytes 110600 | tf_op jit(solution)/shard_map/faces/ppermute | solution.py:345
  3.6 7.2 %collective-permute-start.1 = (f32[18,8,128]{2,1,0:T(8,128)S(1)}, f32[18,8,128]{2,1,0:T(8,128)S(1)}, u32[]{:S(2)}, u32[]{:S(2)}) collective-permute-start(f32[18,8,128]{2,1,0:T(8,128)S(1)} %pad_maximum_fusion), channel_id=1, source_target_pairs={{128,0},{140,4},{136,8},{148,12},{144,16},{156,20},{152,24},{164,2... | collective-permute-start | bytes 221192 | tf_op jit(solution)/shard_map/faces/ppermute | solution.py:345
  5.9 8.3 %collective-permute-start.2 = (f32[9,8,128]{2,1,0:T(8,128)S(1)}, f32[9,8,128]{2,1,0:T(8,128)S(1)}, u32[]{:S(2)}, u32[]{:S(2)}) collective-permute-start(f32[9,8,128]{2,1,0:T(8,128)S(1)} %get-tuple-element.25), channel_id=1, source_target_pairs={{252,0},{0,4},{4,8},{8,12},{12,16},{16,20},{20,24},{24,28},{28,32}... | collective-permute-start | bytes 110600 | tf_op jit(solution)/shard_map/faces/ppermute | solution.py:345
  10.8 3.4 %copy-start.6 = (f32[4,4,3,128]{3,2,1,0:T(4,128)S(1)}, f32[4,4,3,128]{3,2,1,0:T(4,128)}, u32[]{:S(2)}) copy-start(f32[4,4,3,128]{3,2,1,0:T(4,128)} %constant.13.clone.packed) | copy-start | bytes 73732
  10.9 8.1 %copy-start.3 = (f32[4,5,104,128]{3,2,1,0:T(8,128)S(1)}, f32[4,5,104,128]{3,2,1,0:T(8,128)}, u32[]{:S(2)}) copy-start(f32[4,5,104,128]{3,2,1,0:T(8,128)} %constant.14.clone.forward) | copy-start | bytes 3194884
  10.9 8.1 %copy-start.4 = (f32[4,2,96,128]{3,2,1,0:T(8,128)S(1)}, f32[4,2,96,128]{3,2,1,0:T(8,128)}, u32[]{:S(2)}) copy-start(f32[4,2,96,128]{3,2,1,0:T(8,128)} %constant.15.clone.back) | copy-start | bytes 1179652
  10.9 3.3 %collective-permute-start.3 = (f32[9,8,128]{2,1,0:T(8,128)S(1)}, f32[9,8,128]{2,1,0:T(8,128)S(1)}, u32[]{:S(2)}, u32[]{:S(2)}) collective-permute-start(f32[9,8,128]{2,1,0:T(8,128)S(1)} %slice.3), channel_id=1, source_target_pairs={{4,0},{0,4},{12,8},{8,12},{20,16},{16,20},{28,24},{24,28},{36,32},... | collective-permute-start | bytes 110600 | tf_op jit(solution)/shard_map/faces/ppermute | solution.py:345
  14.7 6.4 %collective-permute-start.4 = (f32[2,3,8,128]{3,2,1,0:T(8,128)S(1)}, f32[2,3,8,128]{3,2,1,0:T(8,128)S(1)}, u32[]{:S(2)}, u32[]{:S(2)}) collective-permute-start(f32[2,3,8,128]{3,2,1,0:T(8,128)S(1)} %get-tuple-element.41), channel_id=1, source_target_pairs={{2,0},{3,1},{0,2},{1,3},{6,4},{7,5},{4,6},{5,7},{10,8},{11,9},{8,1... | collective-permute-start | bytes 73736 | tf_op jit(solution)/shard_map/line/ppermute | solution.py:390
  17.8 5.0 %collective-permute-start.5 = (f32[2,3,8,128]{3,2,1,0:T(8,128)S(1)}, f32[2,3,8,128]{3,2,1,0:T(8,128)S(1)}, u32[]{:S(2)}, u32[]{:S(2)}) collective-permute-start(f32[2,3,8,128]{3,2,1,0:T(8,128)S(1)} %get-tuple-element.42), channel_id=1, source_target_pairs={{3,0},{2,1},{1,2},{0,3},{7,4},{6,5},{5,6},{4,7},{11,8},{10,9},{9,1... | collective-permute-start | bytes 73736 | tf_op jit(solution)/shard_map/line/ppermute | solution.py:390
  18.9 3.9 %collective-permute-start.6 = (f32[2,3,8,128]{3,2,1,0:T(8,128)S(1)}, f32[2,3,8,128]{3,2,1,0:T(8,128)S(1)}, u32[]{:S(2)}, u32[]{:S(2)}) collective-permute-start(f32[2,3,8,128]{3,2,1,0:T(8,128)S(1)} %get-tuple-element.43), channel_id=1, source_target_pairs={{1,0},{0,1},{3,2},{2,3},{5,4},{4,5},{7,6},{6,7},{9,8},{8,9},{11,10... | collective-permute-start | bytes 73736 | tf_op jit(solution)/shard_map/line/ppermute | solution.py:390
  19.0 3.9 %copy-start.2 = (bf16[4,768,144]{2,1,0:T(8,128)(2,1)S(1)}, bf16[4,768,144]{2,1,0:T(8,128)(2,1)}, u32[]{:S(2)}) copy-start(bf16[4,768,144]{2,1,0:T(8,128)(2,1)} %constant.16.clone.outer) | copy-start | bytes 2654212
